TPU v7x, 32 devices: a whole 2x2x4 slice. The times are simulated.
32 devices in a mesh: fsdp: 32 (over z, y, x, core).
Axes of the slice: x: 2, y: 2, z: 4, core: 2. Of those that a mesh axis runs over, the one named last changes fastest.
Arguments:
- layer_in: bfloat16 [20480, 1280], P('fsdp'), may hold values from -6 to 6
- out_grad: bfloat16 [20480, 1280], P('fsdp'), may hold values from -6 to 6
- segment_ids: int32 [20480], P('fsdp'), may hold values from 0 to 51, as said below
- segment_parents: int32 [52], replicated, may hold values from 0 to 43, as said below
- norm_gain1: bfloat16 [1280], P('fsdp'), may hold values from 0.5 to 1.5
- w_query: bfloat16 [1280, 1280], P('fsdp'), may hold values from -0.15625 to 0.15625
- w_key: bfloat16 [1280, 320], P('fsdp'), may hold values from -0.15625 to 0.15625
- w_value: bfloat16 [1280, 320], P('fsdp'), may hold values from -0.15625 to 0.15625
- w_output: bfloat16 [1280, 1280], P(None, 'fsdp'), may hold values from -4 to 4
- norm_gain2: bfloat16 [1280], P('fsdp'), may hold values from 0.5 to 1.5
- w_gate: bfloat16 [1280, 3584], P('fsdp'), may hold values from -0.15625 to 0.15625
- w_up: bfloat16 [1280, 3584], P('fsdp'), may hold values from -0.15625 to 0.15625
- w_down: bfloat16 [3584, 1280], P(None, 'fsdp'), may hold values from -0.09375 to 0.09375
Outputs:
- layer_out: bfloat16 [20480, 1280], P('fsdp')
- input_grad: float32 [20480, 1280], P('fsdp')
- grad_norm_gain1: float32 [1280], P('fsdp')
- grad_w_query: float32 [1280, 1280], P('fsdp')
- grad_w_key: float32 [1280, 320], P('fsdp')
- grad_w_value: float32 [1280, 320], P('fsdp')
- grad_w_output: float32 [1280, 1280], P(None, 'fsdp')
- grad_norm_gain2: float32 [1280], P('fsdp')
- grad_w_gate: float32 [1280, 3584], P('fsdp')
- grad_w_up: float32 [1280, 3584], P('fsdp')
- grad_w_down: float32 [3584, 1280], P(None, 'fsdp')
Inputs may be any that keep to these rules, and one draw needn't show every extreme that they name: `segment_ids`: tree k holds rows k * 5120 to (k + 1) * 5120 - 1 and segments k * 13 to (k + 1) * 13 - 1 in rising order: first its trunk, then 4 branches, then 2 * 4 leaves; every segment has at least one token. `segment_parents`: A trunk's parent is itself, each branch's parent is its tree's trunk, each leaf's parent is one of its tree's branches, and every branch is the parent of exactly two leaves.
All inputs are finite; a program needn't handle non-finite values.
Results may differ from a plain program's by a relative error of at most 0.014.
Values may be sent and summed in bfloat16 or wider, within the bound.
No kernel may reach another device: no remote copies, remote signals or barrier semaphores. Data moves between devices by JAX's collectives and lax.ppermute only.
A program may use at most 320 MiB of HBM per device.

v0:
```python
import math

import jax
import jax.numpy as jnp
from jax import lax
from jax.sharding import PartitionSpec as P

HEADS = 20
KV_HEADS = 5
HEAD = 64
TREE = 5120


EPSILON = 1e-05
ROPE_BASE = 10000.0
MASKED_SCORE = -1e30


def from_behind(shard, axis, by):
    size = lax.axis_size(axis)
    pairs = [(i, i + by) for i in range(size) if 0 <= i + by < size]
    return lax.ppermute(shard, axis, pairs)


def rms_scale(inputs):
    return lax.rsqrt(jnp.mean(inputs * inputs, axis=-1, keepdims=True) + EPSILON)


def rotate(inputs, cosine, sine_table):
    middle = inputs.shape[-1] // 2
    turned = jnp.concatenate([-inputs[..., middle:], inputs[..., :middle]], axis=-1)
    return inputs * cosine + turned * sine_table


def rotate_back(grad_values, cosine, sine_table):
    middle = grad_values.shape[-1] // 2
    scaled = grad_values * sine_table
    turned = jnp.concatenate([scaled[..., middle:], -scaled[..., :middle]], axis=-1)
    return grad_values * cosine + turned


def table_lookup(onehot, values_table):
    return jnp.sum(onehot * values_table[None, :], axis=1)


def norm_backward(grad_normed, inputs, norm_scale, gain_vector):
    weighted = grad_normed * gain_vector
    grad_gain = jnp.sum(grad_normed * inputs * norm_scale, axis=0)
    grad_inputs = norm_scale * weighted - inputs * (
        norm_scale * norm_scale * norm_scale
    ) * jnp.mean(weighted * inputs, axis=-1, keepdims=True)
    return (grad_gain, grad_inputs)


def body(
    layer_in,
    out_grad,
    segment_ids,
    segment_parents,
    norm_gain1,
    w_query,
    w_key,
    w_value,
    w_output,
    norm_gain2,
    w_gate,
    w_up,
    w_down,
):
    tok_rows = layer_in.shape[0]
    kv_width = KV_HEADS * HEAD
    group_size = HEADS // KV_HEADS
    group_span = TREE // tok_rows
    my_index = lax.axis_index("fsdp")
    seg_total = segment_parents.shape[0]
    seg_range = jnp.arange(seg_total, dtype=jnp.int32)
    seg_float = seg_range.astype(jnp.float32)
    own_onehot = (segment_ids[:, None] == seg_range[None, :]).astype(jnp.float32)
    seg_lengths = lax.psum(jnp.sum(own_onehot, axis=0), "fsdp")
    parent_float = segment_parents.astype(jnp.float32)
    parent_onehot = (segment_parents[:, None] == seg_range[None, :]).astype(jnp.float32)
    grand_float = table_lookup(parent_onehot, parent_float)
    grand_onehot = (grand_float[:, None] == seg_float[None, :]).astype(jnp.float32)
    depth_start = jnp.where(
        parent_float != seg_float, table_lookup(parent_onehot, seg_lengths), 0.0
    ) + jnp.where(grand_float != parent_float, table_lookup(grand_onehot, seg_lengths), 0.0)
    layout_start = jnp.cumsum(seg_lengths) - seg_lengths
    own_rows = (my_index * tok_rows + jnp.arange(tok_rows, dtype=jnp.int32)).astype(jnp.float32)
    positions = (
        table_lookup(own_onehot, depth_start) + own_rows - table_lookup(own_onehot, layout_start)
    )
    ancestry = jnp.stack(
        [
            table_lookup(own_onehot, seg_float),
            table_lookup(own_onehot, parent_float),
            table_lookup(own_onehot, grand_float),
        ],
        axis=1,
    )
    middle = HEAD // 2
    inverse = jnp.exp(jnp.arange(middle, dtype=jnp.float32) * (-2.0 * math.log(ROPE_BASE) / HEAD))
    angles = positions[:, None] * inverse[None, :]
    cosine = jnp.concatenate([jnp.cos(angles), jnp.cos(angles)], axis=1)[:, None, :]
    sine_table = jnp.concatenate([jnp.sin(angles), jnp.sin(angles)], axis=1)[:, None, :]
    attention_set = (
        lax.all_gather(norm_gain1, "fsdp", axis=0, tiled=True),
        lax.all_gather(w_query, "fsdp", axis=0, tiled=True),
        lax.all_gather(w_key, "fsdp", axis=0, tiled=True),
        lax.all_gather(w_value, "fsdp", axis=0, tiled=True),
        lax.all_gather(w_output, "fsdp", axis=1, tiled=True),
    )
    gain1, query_w, key_w, value_w, output_w = attention_set
    inputs = layer_in.astype(jnp.float32)
    gain1_f = gain1.astype(jnp.float32)
    scale1 = rms_scale(inputs)
    normed1 = (inputs * scale1 * gain1_f).astype(jnp.bfloat16)
    query_proj = jnp.dot(normed1, query_w, preferred_element_type=jnp.float32)
    key_proj = jnp.dot(normed1, key_w, preferred_element_type=jnp.float32)
    values = jnp.dot(normed1, value_w, preferred_element_type=jnp.float32).astype(jnp.bfloat16)
    query_rot = rotate(query_proj.reshape(tok_rows, HEADS, HEAD), cosine, sine_table).astype(
        jnp.bfloat16
    )
    keys_rot = rotate(key_proj.reshape(tok_rows, KV_HEADS, HEAD), cosine, sine_table).astype(
        jnp.bfloat16
    )
    packed = jnp.concatenate([keys_rot.reshape(tok_rows, kv_width), values], axis=1)
    piece_list = [packed]
    for shift_step in range(1, group_span):
        piece_list.append(from_behind(packed, "fsdp", shift_step))
    piece_stack = jnp.stack(piece_list)
    piece_first = (my_index - jnp.arange(group_span, dtype=jnp.int32)) * tok_rows
    key_rows = (piece_first[:, None] + jnp.arange(tok_rows, dtype=jnp.int32)[None, :]).astype(
        jnp.float32
    )
    key_segs = (
        jnp.sum((layout_start[None, None, :] <= key_rows[:, :, None]).astype(jnp.float32), axis=2)
        - 1.0
    )
    query_groups = query_rot.reshape(tok_rows, KV_HEADS, group_size, HEAD)
    score_scale = HEAD ** (-0.5)

    def allowed_mask(key_seg, key_row):
        matched = (
            (key_seg[None, :] == ancestry[:, 0:1])
            | (key_seg[None, :] == ancestry[:, 1:2])
            | (key_seg[None, :] == ancestry[:, 2:3])
        )
        return matched & (key_row[None, :] <= own_rows[:, None])

    def piece_keys(packed_piece):
        return packed_piece[:, :kv_width].reshape(tok_rows, KV_HEADS, HEAD)

    def piece_values(packed_piece):
        return packed_piece[:, kv_width:].reshape(tok_rows, KV_HEADS, HEAD)

    def masked_scores(packed_piece, allowed):
        raw_scores = (
            jnp.einsum(
                "qhgd,khd->hgqk",
                query_groups,
                piece_keys(packed_piece),
                preferred_element_type=jnp.float32,
            )
            * score_scale
        )
        return jnp.where(allowed[None, None], raw_scores, MASKED_SCORE)

    def stats_step(carry_state, scan_entry):
        packed_piece, key_seg, key_row = scan_entry
        allowed = allowed_mask(key_seg, key_row)

        def stats_update(running):
            running_max, running_total = running
            scores = masked_scores(packed_piece, allowed)
            new_max = jnp.maximum(running_max, jnp.max(scores, axis=-1))
            new_total = running_total * jnp.exp(running_max - new_max) + jnp.sum(
                jnp.exp(scores - new_max[..., None]), axis=-1
            )
            return (new_max, new_total)

        def stats_unchanged(running):
            return running

        return (lax.cond(jnp.any(allowed), stats_update, stats_unchanged, carry_state), None)

    stat_shape = (KV_HEADS, group_size, tok_rows)
    stats_init = (
        jnp.full(stat_shape, MASKED_SCORE, jnp.float32),
        jnp.zeros(stat_shape, jnp.float32),
    )
    (row_max, row_total), unused_stats = lax.scan(
        stats_step, stats_init, (piece_stack, key_segs, key_rows)
    )
    log_total = row_max + jnp.log(row_total)

    def output_step(carry_sum, scan_entry):
        packed_piece, key_seg, key_row = scan_entry
        allowed = allowed_mask(key_seg, key_row)

        def output_update(running):
            prob_values = jnp.exp(
                masked_scores(packed_piece, allowed) - log_total[..., None]
            ).astype(jnp.bfloat16)
            return running + jnp.einsum(
                "hgqk,khd->qhgd",
                prob_values,
                piece_values(packed_piece),
                preferred_element_type=jnp.float32,
            )

        def output_unchanged(running):
            return running

        return (lax.cond(jnp.any(allowed), output_update, output_unchanged, carry_sum), None)

    attended_sum, unused_out = lax.scan(
        output_step,
        jnp.zeros((tok_rows, KV_HEADS, group_size, HEAD), jnp.float32),
        (piece_stack, key_segs, key_rows),
    )
    attended = attended_sum.reshape(tok_rows, HEADS * HEAD).astype(jnp.bfloat16)
    mid_stream = inputs + jnp.dot(attended, output_w, preferred_element_type=jnp.float32)
    mlp_set = (
        lax.all_gather(norm_gain2, "fsdp", axis=0, tiled=True),
        lax.all_gather(w_gate, "fsdp", axis=0, tiled=True),
        lax.all_gather(w_up, "fsdp", axis=0, tiled=True),
        lax.all_gather(w_down, "fsdp", axis=1, tiled=True),
    )
    gain2, gate_w, up_w, down_w = mlp_set
    gain2_f = gain2.astype(jnp.float32)
    scale2 = rms_scale(mid_stream)
    normed2 = (mid_stream * scale2 * gain2_f).astype(jnp.bfloat16)
    gate_act = jnp.dot(normed2, gate_w, preferred_element_type=jnp.float32)
    up_act = jnp.dot(normed2, up_w, preferred_element_type=jnp.float32)
    sigmoid_gate = jax.nn.sigmoid(gate_act)
    silu_gate = gate_act * sigmoid_gate
    hidden = (silu_gate * up_act).astype(jnp.bfloat16)
    result = mid_stream + jnp.dot(hidden, down_w, preferred_element_type=jnp.float32)
    layer_out = result.astype(jnp.bfloat16)
    gain2, gate_w, up_w, down_w = (
        lax.all_gather(norm_gain2, "fsdp", axis=0, tiled=True),
        lax.all_gather(w_gate, "fsdp", axis=0, tiled=True),
        lax.all_gather(w_up, "fsdp", axis=0, tiled=True),
        lax.all_gather(w_down, "fsdp", axis=1, tiled=True),
    )
    grad_hidden = jnp.einsum("td,fd->tf", out_grad, down_w, preferred_element_type=jnp.float32)
    grad_gate = (
        grad_hidden * up_act * sigmoid_gate * (1.0 + gate_act * (1.0 - sigmoid_gate))
    ).astype(jnp.bfloat16)
    grad_up = (grad_hidden * silu_gate).astype(jnp.bfloat16)
    grad_normed2 = jnp.einsum(
        "tf,df->td", grad_gate, gate_w, preferred_element_type=jnp.float32
    ) + jnp.einsum("tf,df->td", grad_up, up_w, preferred_element_type=jnp.float32)
    gain_term2 = jnp.sum(grad_normed2 * mid_stream * scale2, axis=0)
    weighted2 = grad_normed2 * gain2_f
    grad_mid_norm = scale2 * weighted2 - mid_stream * (scale2 * scale2 * scale2) * jnp.mean(
        weighted2 * mid_stream, axis=-1, keepdims=True
    )
    grad_mid = out_grad.astype(jnp.float32) + grad_mid_norm
    grad_down = jnp.einsum("tf,td->fd", hidden, out_grad, preferred_element_type=jnp.float32)
    grad_gate_w = jnp.einsum("td,tf->df", normed2, grad_gate, preferred_element_type=jnp.float32)
    grad_up_w = jnp.einsum("td,tf->df", normed2, grad_up, preferred_element_type=jnp.float32)
    mlp_grads = (
        lax.psum_scatter(gain_term2, "fsdp", scatter_dimension=0, tiled=True),
        lax.psum_scatter(grad_gate_w, "fsdp", scatter_dimension=0, tiled=True),
        lax.psum_scatter(grad_up_w, "fsdp", scatter_dimension=0, tiled=True),
        lax.psum_scatter(grad_down, "fsdp", scatter_dimension=1, tiled=True),
    )
    gain1, query_w, key_w, value_w, output_w = (
        lax.all_gather(norm_gain1, "fsdp", axis=0, tiled=True),
        lax.all_gather(w_query, "fsdp", axis=0, tiled=True),
        lax.all_gather(w_key, "fsdp", axis=0, tiled=True),
        lax.all_gather(w_value, "fsdp", axis=0, tiled=True),
        lax.all_gather(w_output, "fsdp", axis=1, tiled=True),
    )
    gain1_f = gain1.astype(jnp.float32)
    grad_mid_b = grad_mid.astype(jnp.bfloat16)
    grad_attended = jnp.einsum(
        "td,ed->te", grad_mid_b, output_w, preferred_element_type=jnp.float32
    ).astype(jnp.bfloat16)
    grad_output_w = jnp.einsum(
        "te,td->ed", attended, grad_mid_b, preferred_element_type=jnp.float32
    )
    grad_att_groups = grad_attended.reshape(tok_rows, KV_HEADS, group_size, HEAD)

    def delta_step(carry_sum, scan_entry):
        packed_piece, key_seg, key_row = scan_entry
        allowed = allowed_mask(key_seg, key_row)

        def delta_update(running):
            prob_values = jnp.exp(masked_scores(packed_piece, allowed) - log_total[..., None])
            grad_probs = jnp.einsum(
                "qhgd,khd->hgqk",
                grad_att_groups,
                piece_values(packed_piece),
                preferred_element_type=jnp.float32,
            )
            return running + jnp.sum(prob_values * grad_probs, axis=-1)

        def delta_unchanged(running):
            return running

        return (lax.cond(jnp.any(allowed), delta_update, delta_unchanged, carry_sum), None)

    row_delta, unused_delta = lax.scan(
        delta_step, jnp.zeros(stat_shape, jnp.float32), (piece_stack, key_segs, key_rows)
    )

    def grad_step(carry_sum, scan_entry):
        packed_piece, key_seg, key_row = scan_entry
        allowed = allowed_mask(key_seg, key_row)

        def grad_update(running):
            prob_values = jnp.exp(masked_scores(packed_piece, allowed) - log_total[..., None])
            grad_probs = jnp.einsum(
                "qhgd,khd->hgqk",
                grad_att_groups,
                piece_values(packed_piece),
                preferred_element_type=jnp.float32,
            )
            grad_scores = (prob_values * (grad_probs - row_delta[..., None])).astype(jnp.bfloat16)
            new_query = (
                running
                + jnp.einsum(
                    "hgqk,khd->qhgd",
                    grad_scores,
                    piece_keys(packed_piece),
                    preferred_element_type=jnp.float32,
                )
                * score_scale
            )
            grad_piece_keys = (
                jnp.einsum(
                    "hgqk,qhgd->khd", grad_scores, query_groups, preferred_element_type=jnp.float32
                )
                * score_scale
            )
            grad_piece_values = jnp.einsum(
                "hgqk,qhgd->khd",
                prob_values.astype(jnp.bfloat16),
                grad_att_groups,
                preferred_element_type=jnp.float32,
            )
            return (
                new_query,
                jnp.concatenate(
                    [
                        grad_piece_keys.reshape(tok_rows, kv_width),
                        grad_piece_values.reshape(tok_rows, kv_width),
                    ],
                    axis=1,
                ),
            )

        def grad_unchanged(running):
            return (running, jnp.zeros((tok_rows, 2 * kv_width), jnp.float32))

        return lax.cond(jnp.any(allowed), grad_update, grad_unchanged, carry_sum)

    grad_query_rot, piece_grads = lax.scan(
        grad_step,
        jnp.zeros((tok_rows, KV_HEADS, group_size, HEAD), jnp.float32),
        (piece_stack, key_segs, key_rows),
    )
    grad_packed = piece_grads[0]
    for shift_step in range(1, group_span):
        grad_packed = grad_packed + from_behind(
            piece_grads[shift_step].astype(jnp.bfloat16), "fsdp", -shift_step
        ).astype(jnp.float32)
    grad_keys = (
        rotate_back(grad_packed[:, :kv_width].reshape(tok_rows, KV_HEADS, HEAD), cosine, sine_table)
        .reshape(tok_rows, kv_width)
        .astype(jnp.bfloat16)
    )
    grad_values = grad_packed[:, kv_width:].astype(jnp.bfloat16)
    grad_query = (
        rotate_back(grad_query_rot.reshape(tok_rows, HEADS, HEAD), cosine, sine_table)
        .reshape(tok_rows, HEADS * HEAD)
        .astype(jnp.bfloat16)
    )
    grad_normed1 = jnp.einsum("te,de->td", grad_query, query_w, preferred_element_type=jnp.float32)
    grad_normed1 = grad_normed1 + jnp.einsum(
        "te,de->td", grad_keys, key_w, preferred_element_type=jnp.float32
    )
    grad_normed1 = grad_normed1 + jnp.einsum(
        "te,de->td", grad_values, value_w, preferred_element_type=jnp.float32
    )
    grad_query_w = jnp.einsum("td,te->de", normed1, grad_query, preferred_element_type=jnp.float32)
    grad_key_w = jnp.einsum("td,te->de", normed1, grad_keys, preferred_element_type=jnp.float32)
    grad_value_w = jnp.einsum("td,te->de", normed1, grad_values, preferred_element_type=jnp.float32)
    grad_gain1, grad_in_norm = norm_backward(grad_normed1, inputs, scale1, gain1_f)
    input_grad = grad_mid + grad_in_norm
    attention_grads = (
        lax.psum_scatter(grad_gain1, "fsdp", scatter_dimension=0, tiled=True),
        lax.psum_scatter(grad_query_w, "fsdp", scatter_dimension=0, tiled=True),
        lax.psum_scatter(grad_key_w, "fsdp", scatter_dimension=0, tiled=True),
        lax.psum_scatter(grad_value_w, "fsdp", scatter_dimension=0, tiled=True),
        lax.psum_scatter(grad_output_w, "fsdp", scatter_dimension=1, tiled=True),
    )
    return (
        layer_out,
        input_grad,
        attention_grads[0],
        attention_grads[1],
        attention_grads[2],
        attention_grads[3],
        attention_grads[4],
        mlp_grads[0],
        mlp_grads[1],
        mlp_grads[2],
        mlp_grads[3],
    )


def solution(mesh):
    return jax.shard_map(
        body,
        mesh=mesh,
        in_specs=(
            P("fsdp", None),
            P("fsdp", None),
            P("fsdp"),
            P(),
            P("fsdp"),
            P("fsdp", None),
            P("fsdp", None),
            P("fsdp", None),
            P(None, "fsdp"),
            P("fsdp"),
            P("fsdp", None),
            P("fsdp", None),
            P(None, "fsdp"),
        ),
        out_specs=(
            P("fsdp", None),
            P("fsdp", None),
            P("fsdp"),
            P("fsdp", None),
            P("fsdp", None),
            P("fsdp", None),
            P(None, "fsdp"),
            P("fsdp"),
            P("fsdp", None),
            P("fsdp", None),
            P(None, "fsdp"),
        ),
        check_vma=False,
    )
```

profile of v0, /device:TPU:0, one launch (start us, length us, event | category | flops | bytes accessed | tf_op | source)
XLA Modules:
  0.0 2926.1 jit_solution(7603601784172223906)
XLA Ops:
  13.0 42.2 %psum.7 = f32[52]{0:T(128)S(1)} all-reduce(f32[52]{0:T(128)S(1)} %convert_reduce_fusion.1), channel_id=1, replica_groups=mesh['fsdp'=32] {'fsdp'}, use_global_device_ids=true, to_apply=%region_2.0 | all-reduce | flops 52 | bytes 416 | tf_op jit(solution)/shard_map/psum | solution.py:79
  59.6 40.3 %all-reduce.7 = (bf16[1280]{0:T(1024)(128)(2,1)S(1)}, bf16[1280]{0:T(1024)(128)(2,1)S(1)}) all-reduce(bf16[1280]{0:T(1024)(128)(2,1)S(1)} %dynamic-update-slice, bf16[1280]{0:T(1024)(128)(2,1)S(1)} %dynamic-update-slice.1), channel_id=1, replica_groups=mesh['fsdp'=32] {'fsdp'}, use_global_device_ids=true, to_apply=%add | all-reduce | flops 2560 | bytes 10240
  102.8 44.9 %all_gather.36 = bf16[1280,320]{1,0:T(8,128)(2,1)S(1)} all-gather(bf16[40,320]{1,0:T(8,128)(2,1)S(1)} %copy-done.42), channel_id=1, replica_groups=mesh['fsdp'=32] {'fsdp'}, dimensions={0}, use_global_device_ids=true | all-gather | bytes 844800 | tf_op jit(solution)/shard_map/all_gather | solution.py:108
  149.5 41.4 %all_gather.37 = bf16[1280,320]{1,0:T(8,128)(2,1)S(1)} all-gather(bf16[40,320]{1,0:T(8,128)(2,1)S(1)} %copy-done.43), channel_id=1, replica_groups=mesh['fsdp'=32] {'fsdp'}, dimensions={0}, use_global_device_ids=true | all-gather | bytes 844800 | tf_op jit(solution)/shard_map/all_gather | solution.py:109
  208.2 36.9 %collective-permute-start.4 = (bf16[640,640]{0,1:T(8,128)(2,1)S(1)}, bf16[640,640]{0,1:T(8,128)(2,1)S(1)}, u32[]{:S(2)}, u32[]{:S(2)}) collective-permute-start(bf16[640,640]{0,1:T(8,128)(2,1)S(1)} %pad_maximum_fusion.1), channel_id=1, source_target_pairs={{0,5},{1,6},{2,7},{3,8},{4,9},{5,10},{6,11},{7,12},{8,13},{9,14},{... | collective-permute-start | bytes 2457608 | tf_op jit(solution)/shard_map/ppermute | solution.py:22
  259.3 65.2 %collective-permute-start.6 = (bf16[640,640]{0,1:T(8,128)(2,1)S(1)}, bf16[640,640]{0,1:T(8,128)(2,1)S(1)}, u32[]{:S(2)}, u32[]{:S(2)}) collective-permute-start(bf16[640,640]{0,1:T(8,128)(2,1)S(1)} %pad_maximum_fusion.1), channel_id=1, source_target_pairs={{0,7},{1,8},{2,9},{3,10},{4,11},{5,12},{6,13},{7,14},{8,15},{9,16}... | collective-permute-start | bytes 2457608 | tf_op jit(solution)/shard_map/ppermute | solution.py:22
  342.4 46.5 %while.57 = (s32[]{:T(128)}, f32[5,4,640]{2,1,0:T(4,128)S(1)}, f32[5,4,640]{2,1,0:T(4,128)S(1)}, f32[8,640]{1,0:T(8,128)S(1)}, f32[640,1]{0,1:T(1,128)S(1)}, /*i...) while((s32[]{:T(128)}, f32[5,4,640]{2,1,0:T(4,128)S(1)}, ...), condition=%wide.region_19.20_spmd.clone, body=%wide.region_13.19_spmd.clone.sunk | while | flops 1109223680 | bytes 71979768 | solution.py:191
  344.6 30.4 %conditional.12 = ((f32[5,4,640]{2,1,0:T(4,128)S(1)}, f32[5,4,640]{2,1,0:T(4,128)S(1)})) conditional(s32[]{:T(128)} %convert_element_type.317, (f32[5,4,640]{2,1,0:T(4,128)S(1)}, f32[5,4,640]{2,1,0:T(4,128)S(1)}) %tuple.168, (pred[640,640]{0,1:T(8,128)(4,1)S(1)}, bf16[8,640,640]{1,2,0:T(8,128)(2,1)}, s32[]{:T(128)}, ...), branch_computations={%region_15.15_spmd, %region_16.18_spmd} | conditional | flops 1105945600 | bytes 71526424 | solution.py:184
  391.6 30.9 %while.58 = (s32[]{:T(128)}, f32[640,5,4,64]{0,3,2,1:T(8,128)}, f32[8,640]{1,0:T(8,128)S(1)}, f32[640,1]{0,1:T(1,128)S(1)}, f32[640,1]{0,1:T(1,128)S(1)}, /*inde...) while((s32[]{:T(128)}, f32[640,5,4,64]{0,3,2,1:T(8,128)}, ...), condition=%wide.region_24.25_spmd.clone, body=%wide.region_20.24_spmd.clone.sunk | while | flops 2134017280 | bytes 13202139 | solution.py:216
  461.4 16.7 multiply_convert_fusion
  512.1 48.5 %while.59 = (s32[]{:T(128)}, f32[5,4,640]{2,1,0:T(4,128)S(1)}, f32[8,640]{1,0:T(8,128)S(1)}, f32[640,1]{0,1:T(1,128)S(1)}, f32[640,1]{0,1:T(1,128)S(1)}, /*index...) while((s32[]{:T(128)}, f32[5,4,640]{2,1,0:T(4,128)S(1)}, ...), condition=%wide.region_32.33_spmd.clone, body=%wide.region_27.32_spmd.clone.sunk | while | flops 2141390080 | bytes 74027752 | solution.py:305
  514.1 32.6 %conditional.14 = (f32[5,4,640]{2,1,0:T(4,128)S(1)}) conditional(s32[]{:T(128)} %convert_element_type.321, f32[5,4,640]{2,1,0:T(4,128)S(1)} %get-tuple-element.1188, (pred[640,640]{0,1:T(8,128)(4,1)S(1)}, bf16[8,640,640]{1,2,0:T(8,128)(2,1)}, s32[]{:T(128)}, bf16[640,5,4,64]{0,3,2,1:T(8,128)(2,1)}, f32[5,4,640]{2,1,0:T(4,128)}, ...), branch_computations={%region_29.29_spmd, %region_30.31_spmd} | conditional | flops 2138112000 | bytes 73574408 | solution.py:303
  515.4 16.7 fusion.83
  562.1 118.6 %while.60 = (s32[]{:T(128)}, f32[640,5,4,64]{0,3,2,1:T(8,128)S(1)}, f32[8,640,640]{1,2,0:T(8,128)}, f32[8,640]{1,0:T(8,128)S(1)}, f32[640,1]{0,1:T(1,128)S(1)}, ...) while((s32[]{:T(128)}, f32[640,5,4,64]{0,3,2,1:T(8,128)S(1)}, ...), condition=%wide.region_37.38_spmd.clone, body=%wide.region_33.37_spmd.clone.sunk | while | flops 5330331136 | bytes 207455664 | solution.py:360
  565.2 65.6 %conditional.15 = (f32[640,5,4,64]{0,3,2,1:T(8,128)S(1)}, f32[1,640,640]{1,2,0:T(8,128)}) conditional(s32[]{:T(128)} %convert_element_type.323, f32[640,5,4,64]{0,3,2,1:T(8,128)S(1)} %get-tuple-element.1232, (pred[640,640]{0,1:T(8,128)(4,1)}, bf16[8,640,640]{1,2,0:T(8,128)(2,1)}, s32[]{:T(128)}, bf16[640,5,4,64]{0,3,2,1:T(8,128)(2,1)}, ...), branch_computations={%region_35.35_spmd, %region_36.36_spmd} | conditional | flops 5327052800 | bytes 203724976 | solution.py:358
  698.4 137.6 %collective-permute-done.7 = bf16[640,640]{0,1:T(8,128)(2,1)S(1)} collective-permute-done((bf16[640,640]{0,1:T(8,128)(2,1)S(1)}, bf16[640,640]{0,1:T(8,128)(2,1)S(1)}, u32[]{:S(2)}, u32[]{:S(2)}) %collective-permute-start.7) | collective-permute-done | bytes 819232 | tf_op jit(solution)/shard_map/ppermute | solution.py:22
  837.3 758.0 %collective-permute-done.13 = bf16[640,640]{0,1:T(8,128)(2,1)S(1)} collective-permute-done((bf16[640,640]{0,1:T(8,128)(2,1)S(1)}, bf16[640,640]{0,1:T(8,128)(2,1)S(1)}, u32[]{:S(2)}, u32[]{:S(2)}) %collective-permute-start.13) | collective-permute-done | bytes 819232 | tf_op jit(solution)/shard_map/ppermute | solution.py:22
  1704.0 245.7 %all-reduce.6 = (f32[1280]{0:T(1024)S(1)}, f32[1280]{0:T(1024)S(1)}) all-reduce(f32[1280]{0:T(1024)S(1)} %get-tuple-element.594, f32[1280]{0:T(1024)S(1)} %copy-done.45), channel_id=2, replica_groups=mesh['fsdp'=32] {'fsdp'}, use_global_device_ids=true, to_apply=%region_40.41.clone | all-reduce | flops 2560 | bytes 20480
  1956.5 65.2 %reduce-scatter.22.cloned.1.call-done = f32[40,320]{1,0:T(8,128)} async-done(((f32[1280,320]{1,0:T(8,128)}), f32[40,320]{1,0:T(8,128)}) %reduce-scatter.22.cloned.1.call-update) | async-done | bytes 51216
  2021.6 147.4 %reduce-scatter.14.cloned.1.call-done = f32[1280,40]{0,1:T(8,128)} async-done(((f32[1280,1280]{0,1:T(8,128)}), f32[1280,40]{0,1:T(8,128)}) %reduce-scatter.14.cloned.1.call-update) | async-done | bytes 204816 | tf_op jit(solution)/shard_map/reduce_scatter | solution.py:398
  2169.0 144.3 %reduce-scatter.12.cloned.1.call-done = f32[40,1280]{1,0:T(8,128)} async-done(((f32[1280,1280]{1,0:T(8,128)}), f32[40,1280]{1,0:T(8,128)}) %reduce-scatter.12.cloned.1.call-update) | async-done | bytes 204816 | tf_op jit(solution)/shard_map/reduce_scatter | solution.py:395
  2313.3 198.3 %reduce-scatter.20.cloned.1.call-done = f32[3584,40]{0,1:T(8,128)} async-done(((f32[3584,1280]{0,1:T(8,128)}), f32[3584,40]{0,1:T(8,128)}) %reduce-scatter.20.cloned.1.call-update) | async-done | bytes 573456 | tf_op jit(solution)/shard_map/reduce_scatter | solution.py:267
  2511.6 203.8 %reduce-scatter.18.cloned.1.call-done = f32[40,3584]{1,0:T(8,128)} async-done(((f32[1280,3584]{1,0:T(8,128)}), f32[40,3584]{1,0:T(8,128)}) %reduce-scatter.18.cloned.1.call-update) | async-done | bytes 573456 | tf_op jit(solution)/shard_map/reduce_scatter | solution.py:266
  2715.4 203.5 %reduce-scatter.16.cloned.1.call-done = f32[40,3584]{1,0:T(8,128)} async-done(((f32[1280,3584]{1,0:T(8,128)}), f32[40,3584]{1,0:T(8,128)}) %reduce-scatter.16.cloned.1.call-update) | async-done | bytes 573456 | tf_op jit(solution)/shard_map/reduce_scatter | solution.py:265
  (502 shorter events, 502.6 us)
Async XLA Ops:
  7.2 328.1 %all-gather.6.cloned.1.call-start = ((), (), s32[]{:S(2)}) async-start(), calls=%async_computation.7 | async-start | bytes 3379200 | tf_op jit(solution)/shard_map/all_gather | solution.py:107
  7.9 416.9 %all-gather.8.cloned.1.call-start = ((), (), s32[]{:S(2)}) async-start(), calls=%async_computation.8 | async-start | bytes 3379200 | tf_op jit(solution)/shard_map/all_gather | solution.py:110
  8.7 423.2 %all-gather.12.cloned.1.call-start = ((), (), s32[]{:S(2)}) async-start(), calls=%async_computation.10 | async-start | bytes 9461760 | tf_op jit(solution)/shard_map/all_gather | solution.py:226
  9.4 435.1 %all-gather.10.cloned.1.call-start = ((), (), s32[]{:S(2)}) async-start(), calls=%async_computation.9 | async-start | bytes 9461760 | tf_op jit(solution)/shard_map/all_gather | solution.py:225
  10.0 451.4 %all-gather.14.cloned.1.call-start = ((), (), s32[]{:S(2)}) async-start(), calls=%async_computation.11 | async-start | bytes 9461760 | tf_op jit(solution)/shard_map/all_gather | solution.py:227
  10.6 1945.9 %reduce-scatter.24.cloned.1.call-start = ((), (), s32[]{:S(2)}) async-start(), calls=%async_computation.18 | async-start | bytes 2027520
  193.0 138.8 %collective-permute-start.5 = (bf16[640,640]{0,1:T(8,128)(2,1)S(1)}, bf16[640,640]{0,1:T(8,128)(2,1)}, u32[]{:S(2)}, u32[]{:S(2)}) collective-permute-start(bf16[640,640]{0,1:T(8,128)(2,1)S(1)} %pad_maximum_fusion.1), channel_id=1, source_target_pairs={{0,6},{1,7},{2,8},{3,9},{4,10},{5,11},{6,12},{7,13},{8,14},{9,15},... | collective-permute-start | bytes 2457608 | tf_op jit(solution)/shard_map/ppermute | solution.py:22
  195.2 133.5 %collective-permute-start.3 = (bf16[640,640]{0,1:T(8,128)(2,1)S(1)}, bf16[640,640]{0,1:T(8,128)(2,1)}, u32[]{:S(2)}, u32[]{:S(2)}) collective-permute-start(bf16[640,640]{0,1:T(8,128)(2,1)S(1)} %pad_maximum_fusion.1), channel_id=1, source_target_pairs={{0,4},{1,5},{2,6},{3,7},{4,8},{5,9},{6,10},{7,11},{8,12},{9,13},{1... | collective-permute-start | bytes 2457608 | tf_op jit(solution)/shard_map/ppermute | solution.py:22
  197.5 129.2 %collective-permute-start.2 = (bf16[640,640]{0,1:T(8,128)(2,1)S(1)}, bf16[640,640]{0,1:T(8,128)(2,1)}, u32[]{:S(2)}, u32[]{:S(2)}) collective-permute-start(bf16[640,640]{0,1:T(8,128)(2,1)S(1)} %pad_maximum_fusion.1), channel_id=1, source_target_pairs={{0,3},{1,4},{2,5},{3,6},{4,7},{5,8},{6,9},{7,10},{8,11},{9,12},{10... | collective-permute-start | bytes 2457608 | tf_op jit(solution)/shard_map/ppermute | solution.py:22
  201.5 57.8 %collective-permute-start.1 = (bf16[640,640]{0,1:T(8,128)(2,1)S(1)}, bf16[640,640]{0,1:T(8,128)(2,1)}, u32[]{:S(2)}, u32[]{:S(2)}) collective-permute-start(bf16[640,640]{0,1:T(8,128)(2,1)S(1)} %pad_maximum_fusion.1), channel_id=1, source_target_pairs={{0,2},{1,3},{2,4},{3,5},{4,6},{5,7},{6,8},{7,9},{8,10},{9,11},{10,... | collective-permute-start | bytes 2457608 | tf_op jit(solution)/shard_map/ppermute | solution.py:22
  208.2 122.6 %collective-permute-start.4 = (bf16[640,640]{0,1:T(8,128)(2,1)S(1)}, bf16[640,640]{0,1:T(8,128)(2,1)S(1)}, u32[]{:S(2)}, u32[]{:S(2)}) collective-permute-start(bf16[640,640]{0,1:T(8,128)(2,1)S(1)} %pad_maximum_fusion.1), channel_id=1, source_target_pairs={{0,5},{1,6},{2,7},{3,8},{4,9},{5,10},{6,11},{7,12},{8,13},{9,14},{... | collective-permute-start | bytes 2457608 | tf_op jit(solution)/shard_map/ppermute | solution.py:22
  259.3 75.0 %collective-permute-start.6 = (bf16[640,640]{0,1:T(8,128)(2,1)S(1)}, bf16[640,640]{0,1:T(8,128)(2,1)S(1)}, u32[]{:S(2)}, u32[]{:S(2)}) collective-permute-start(bf16[640,640]{0,1:T(8,128)(2,1)S(1)} %pad_maximum_fusion.1), channel_id=1, source_target_pairs={{0,7},{1,8},{2,9},{3,10},{4,11},{5,12},{6,13},{7,14},{8,15},{9,16}... | collective-permute-start | bytes 2457608 | tf_op jit(solution)/shard_map/ppermute | solution.py:22
  691.9 144.1 %collective-permute-start.7 = (bf16[640,640]{0,1:T(8,128)(2,1)S(1)}, bf16[640,640]{0,1:T(8,128)(2,1)S(1)}, u32[]{:S(2)}, u32[]{:S(2)}) collective-permute-start(bf16[640,640]{0,1:T(8,128)(2,1)S(1)} %get-tuple-element.730), channel_id=1, source_target_pairs={{1,0},{2,1},{3,2},{4,3},{5,4},{6,5},{7,6},{8,7},{9,8},{10,9},{11,1... | collective-permute-start | bytes 2457608 | tf_op jit(solution)/shard_map/ppermute | solution.py:22
  693.2 902.0 %collective-permute-start.13 = (bf16[640,640]{0,1:T(8,128)(2,1)S(1)}, bf16[640,640]{0,1:T(8,128)(2,1)S(1)}, u32[]{:S(2)}, u32[]{:S(2)}) collective-permute-start(bf16[640,640]{0,1:T(8,128)(2,1)S(1)} %get-tuple-element.731), channel_id=1, source_target_pairs={{7,0},{8,1},{9,2},{10,3},{11,4},{12,5},{13,6},{14,7},{15,8},{16,9}... | collective-permute-start | bytes 2457608 | tf_op jit(solution)/shard_map/ppermute | solution.py:22
  694.5 902.1 %collective-permute-start.12 = (bf16[640,640]{0,1:T(8,128)(2,1)S(1)}, bf16[640,640]{0,1:T(8,128)(2,1)S(1)}, u32[]{:S(2)}, u32[]{:S(2)}) collective-permute-start(bf16[640,640]{0,1:T(8,128)(2,1)S(1)} %get-tuple-element.732), channel_id=1, source_target_pairs={{6,0},{7,1},{8,2},{9,3},{10,4},{11,5},{12,6},{13,7},{14,8},{15,9},... | collective-permute-start | bytes 2457608 | tf_op jit(solution)/shard_map/ppermute | solution.py:22
  695.8 900.8 %collective-permute-start.11 = (bf16[640,640]{0,1:T(8,128)(2,1)S(1)}, bf16[640,640]{0,1:T(8,128)(2,1)S(1)}, u32[]{:S(2)}, u32[]{:S(2)}) collective-permute-start(bf16[640,640]{0,1:T(8,128)(2,1)S(1)} %get-tuple-element.733), channel_id=1, source_target_pairs={{5,0},{6,1},{7,2},{8,3},{9,4},{10,5},{11,6},{12,7},{13,8},{14,9},{... | collective-permute-start | bytes 2457608 | tf_op jit(solution)/shard_map/ppermute | solution.py:22
  697.1 899.6 %collective-permute-start.10 = (bf16[640,640]{0,1:T(8,128)(2,1)S(1)}, bf16[640,640]{0,1:T(8,128)(2,1)S(1)}, u32[]{:S(2)}, u32[]{:S(2)}) collective-permute-start(bf16[640,640]{0,1:T(8,128)(2,1)S(1)} %get-tuple-element.734), channel_id=1, source_target_pairs={{4,0},{5,1},{6,2},{7,3},{8,4},{9,5},{10,6},{11,7},{12,8},{13,9},{1... | collective-permute-start | bytes 2457608 | tf_op jit(solution)/shard_map/ppermute | solution.py:22
  836.0 760.7 %collective-permute-start.9 = (bf16[640,640]{0,1:T(8,128)(2,1)S(1)}, bf16[640,640]{0,1:T(8,128)(2,1)S(1)}, u32[]{:S(2)}, u32[]{:S(2)}) collective-permute-start(bf16[640,640]{0,1:T(8,128)(2,1)S(1)} %get-tuple-element.735), channel_id=1, source_target_pairs={{3,0},{4,1},{5,2},{6,3},{7,4},{8,5},{9,6},{10,7},{11,8},{12,9},{13... | collective-permute-start | bytes 2457608 | tf_op jit(solution)/shard_map/ppermute | solution.py:22
  1615.5 406.1 %reduce-scatter.22.cloned.1.call-start = ((), (), s32[]{:S(2)}) async-start(), calls=%async_computation.17 | async-start | bytes 2027520
  1621.1 547.9 %reduce-scatter.14.cloned.1.call-start = ((), (), s32[]{:S(2)}) async-start(), calls=%async_computation.13 | async-start | bytes 6758400 | tf_op jit(solution)/shard_map/reduce_scatter | solution.py:398
  1629.1 684.2 %reduce-scatter.12.cloned.1.call-start = ((), (), s32[]{:S(2)}) async-start(), calls=%async_computation.12 | async-start | bytes 6758400 | tf_op jit(solution)/shard_map/reduce_scatter | solution.py:395
  1637.7 873.9 %reduce-scatter.20.cloned.1.call-start = ((), (), s32[]{:S(2)}) async-start(), calls=%async_computation.16 | async-start | bytes 18923520 | tf_op jit(solution)/shard_map/reduce_scatter | solution.py:267
  1652.5 1062.8 %reduce-scatter.18.cloned.1.call-start = ((), (), s32[]{:S(2)}) async-start(), calls=%async_computation.15 | async-start | bytes 18923520 | tf_op jit(solution)/shard_map/reduce_scatter | solution.py:266
  1667.4 1251.5 %reduce-scatter.16.cloned.1.call-start = ((), (), s32[]{:S(2)}) async-start(), calls=%async_computation.14 | async-start | bytes 18923520 | tf_op jit(solution)/shard_map/reduce_scatter | solution.py:265
  (50 other events, 1675.8 us)
Sparse Core Ops, SparseCore 0:
  10.9 61.9 all-gather.5
  75.8 59.7 all-gather.7
  138.5 112.8 all-gather.11
  254.0 118.2 all-gather.9
  375.0 86.3 all-gather.13
  1615.7 303.0 reduce-scatter.23
  1924.6 96.9 reduce-scatter.21
  2024.5 144.4 reduce-scatter.13
  2171.9 141.3 reduce-scatter.11
  2316.1 195.4 reduce-scatter.19
  2514.6 200.7 reduce-scatter.17
  2718.1 200.7 reduce-scatter.15
where the time goes:
time: 2940 us; the launch traced here: 2930 us
  waiting for transfers between devices  1890 us (64%)
  blocking collectives  414 us (14%)
  matrix products  280 us (10%)
  starting transfers between devices  125 us (4%)
  other arithmetic  94.8 us (3%)
  local copies, waits for them, and re-layouts  81.2 us (3%)
    ppermute x14, waiting for transfers between devices, from_behind(): return lax.ppermute(shard, axis, pairs)  921 us
    unnamed x2, blocking collectives  286 us
    reduce_scatter x1, waiting for transfers between devices, body(): lax.psum_scatter(grad_up_w, 'fsdp', scatter_dimension=0, tiled=True)  204 us
    reduce_scatter x1, waiting for transfers between devices, body(): lax.psum_scatter(grad_gate_w, 'fsdp', scatter_dimension=0, tiled=True)  204 us
    reduce_scatter x1, waiting for transfers between devices, body(): lax.psum_scatter(grad_down, 'fsdp', scatter_dimension=1, tiled=True)  198 us
    reduce_scatter x1, waiting for transfers between devices, body(): lax.psum_scatter(grad_output_w, 'fsdp', scatter_dimension=1, tiled=True)  147 us
    reduce_scatter x1, waiting for transfers between devices, body(): lax.psum_scatter(grad_query_w, 'fsdp', scatter_dimension=0, tiled=True)  144 us
    ppermute x14, starting transfers between devices, from_behind(): return lax.ppermute(shard, axis, pairs)  125 us
  transfers between devices with their start and end apart: 26, of which 12 were waited for; matrix products, arithmetic and copies ran while one was open for 8% of the time, Pallas kernels for 0%

commit v1 on v0

v1 whole, which is shorter than its diff:
```python
import functools
import math

import jax
import jax.numpy as jnp
from jax import lax
from jax.experimental import pallas as pl
from jax.experimental.pallas import tpu as pltpu
from jax.sharding import PartitionSpec as P

HEADS = 20
KV_HEADS = 5
GROUP = HEADS // KV_HEADS
HEAD = 64
TREE = 5120
D = 1280
FF = 3584
HALF = FF // 2
LANES = 128
GROUP_COLS = GROUP * HEAD + 2 * HEAD
QKV = KV_HEADS * GROUP_COLS
QKV_PAD = QKV + LANES
BQ = 128
BK = 256
STACK = GROUP * BQ

EPSILON = 1e-05
ROPE_BASE = 10000.0
MASKED = -1e30
SCALE = HEAD**-0.5
SCALE2 = SCALE * math.log2(math.e)
SAFE_EXPONENT = 60.0
FAR = 1 << 20

F32 = jnp.float32
BF16 = jnp.bfloat16
ROWS_BY_ROWS = (((1,), (1,)), ((), ()))
COLS_BY_COLS = (((0,), (0,)), ((), ()))
VMEM_SPACE = pl.BlockSpec(memory_space=pltpu.VMEM)
SMEM_SPACE = pl.BlockSpec(memory_space=pltpu.SMEM)
ANY_SPACE = pl.BlockSpec(memory_space=pl.ANY)


def params(mib):
    return pltpu.CompilerParams(vmem_limit_bytes=mib * 2**20)


def lane_iota(shape):
    return lax.broadcasted_iota(jnp.int32, shape, len(shape) - 1)


def dot(a, b):
    return jnp.dot(a, b, preferred_element_type=F32)


def dot_tr(a, b):
    return lax.dot_general(a, b, ROWS_BY_ROWS, preferred_element_type=F32)


def dot_cc(a, b):
    return lax.dot_general(a, b, COLS_BY_COLS, preferred_element_type=F32)


def half_turn(z, low):
    return jnp.where(low, pltpu.roll(z, LANES - 32, 1), pltpu.roll(z, 32, 1))


def project_kernel(x_ref, w_ref, cos_ref, sin_ref, n_ref, q_ref, kv_ref, gain_ref):
    gains = w_ref[:, QKV:].astype(F32).T
    gain_ref[...] = gains[:8, :]
    gain1 = gains[0:1, :]
    rows = x_ref.shape[0]

    def norm(i, _):
        at = pl.ds(i * BQ, BQ)
        x = x_ref[at, :].astype(F32)
        scale = lax.rsqrt(jnp.mean(x * x, axis=1, keepdims=True) + EPSILON)
        n_ref[at, :] = (x * scale * gain1).astype(BF16)
        return 0

    lax.fori_loop(0, rows // BQ, norm, 0)
    lane = lane_iota((rows, LANES))
    low = (lane % HEAD) < HEAD // 2
    left = lane < HEAD
    cos = cos_ref[...]
    sin = sin_ref[...]
    for g in range(KV_HEADS):
        z = dot(n_ref[...], w_ref[:, g * GROUP_COLS : (g + 1) * GROUP_COLS])
        for pair in range(GROUP // 2):
            zp = z[:, pair * LANES : (pair + 1) * LANES]
            rot = (zp * cos + half_turn(zp, low) * sin).astype(BF16).astype(F32)
            head = g * GROUP + 2 * pair
            q_ref[head] = jnp.where(left, rot, 0.0).astype(BF16)
            q_ref[head + 1] = jnp.where(left, pltpu.roll(rot, HEAD, 1), 0.0).astype(BF16)
        zk = z[:, GROUP * HEAD :]
        rot = zk * cos + half_turn(zk, low) * sin
        kv_ref[g] = jnp.where(left, rot, zk).astype(BF16)


def project(x, w, cos, sin):
    rows = x.shape[0]
    return pl.pallas_call(
        project_kernel,
        out_shape=[
            jax.ShapeDtypeStruct((rows, D), BF16),
            jax.ShapeDtypeStruct((HEADS, rows, LANES), BF16),
            jax.ShapeDtypeStruct((KV_HEADS, rows, LANES), BF16),
            jax.ShapeDtypeStruct((8, D), F32),
        ],
        compiler_params=params(48),
        name="project",
    )(x, w, cos, sin)


def gather_keys(block, kv_refs, kv, sems):
    rows = kv_refs[0].shape[1]
    copies = []
    for e, ref in enumerate(kv_refs):
        at = pl.multiple_of((block ^ e) * rows, LANES)
        copies.append(pltpu.make_async_copy(ref, kv.at[:, pl.ds(at, rows), :], sems.at[e]))
    for copy in copies:
        copy.start()
    for copy in copies:
        copy.wait()


def tile_pair(meta_ref, tiles, i, t):
    spots = []
    count = meta_ref[1 + i]
    for k in (2 * t, 2 * t + 1):
        first = pl.multiple_of(meta_ref[1 + BQ + i * tiles + jnp.minimum(k, count - 1)] * BK, BK)
        spots.append((first, jnp.where(k < count, first, FAR)))
    return spots


def mask_bias(info_ref, seg_ref, i, spots):
    info = info_ref[pl.ds(i * BQ, BQ), :]
    own, parent, grand, row = (info[:, c : c + 1] for c in range(4))
    parts = []
    for first, name in spots:
        seg = seg_ref[:, pl.ds(first, BK)]
        key_row = lane_iota((1, BK)) + name
        ok = ((seg == own) | (seg == parent) | (seg == grand)) & (key_row <= row)
        parts.append(jnp.where(ok, 0.0, MASKED))
    return jnp.concatenate(parts, axis=1)


def key_pair(kv, g, spots):
    return jnp.concatenate([kv[g, pl.ds(first, BK), :] for first, _ in spots], axis=0)


def masked(s, bias):
    return (s.reshape(GROUP, BQ, 2 * BK) * SCALE2 + bias[None]).reshape(STACK, 2 * BK)


def largest_square(ref, rows):
    ones = jnp.where(lax.broadcasted_iota(jnp.int32, (LANES, LANES), 0) < HEAD, 1.0, 0.0)
    ones = ones.astype(BF16)

    def step(n, top):
        for g in range(ref.shape[0]):
            v = ref[g, pl.ds(n * BK, BK), :].astype(F32)
            sums = dot((v * v).astype(BF16), ones)
            top = jnp.maximum(top, jnp.max(sums.reshape(BK // 8, 8, LANES), axis=0))
        return top

    top = lax.fori_loop(0, rows // BK, step, jnp.zeros((8, LANES), F32))
    return jnp.max(top)


def forward_kernel(
    meta_ref, q_ref, *refs, tiles, span
):
    kv_refs = refs[:span]
    info_ref, seg_ref, att_ref, lse_ref, kv, acc, total, top, sems = refs[span:]
    rows = q_ref.shape[1]
    gather_keys(meta_ref[0], kv_refs, kv, sems)

    def q_rows(i, g):
        at = pl.ds(pl.multiple_of(i * BQ, BQ), BQ)
        return q_ref[pl.ds(g * GROUP, GROUP), at, :].reshape(STACK, LANES)

    def fold(i, g, spots, bias, ceiling):
        pair = key_pair(kv, g, spots)
        s = masked(dot_tr(q_rows(i, g), pair), bias)
        if ceiling:
            s = s - top[g, :, 0:1]
        p = jnp.exp2(s)
        total[g] += sum(p[:, k * LANES : (k + 1) * LANES] for k in range(2 * BK // LANES))
        acc[g] += dot(p.astype(BF16), pair)

    def finish(i, ceiling):
        at = pl.ds(pl.multiple_of(i * BQ, BQ), BQ)
        lane = lane_iota((BQ, LANES))
        logs = jnp.zeros((BQ, LANES), F32)
        for g in range(KV_HEADS):
            sums = jnp.sum(total[g], axis=1, keepdims=True)
            out = acc[g] * (1.0 / sums)
            lse = jnp.log2(sums)
            if ceiling:
                lse = lse + top[g, :, 0:1]
            for h in range(GROUP):
                logs = jnp.where(lane == g * GROUP + h, lse[h * BQ : (h + 1) * BQ], logs)
            for pair in range(GROUP // 2):
                first = out[2 * pair * BQ : (2 * pair + 1) * BQ]
                second = out[(2 * pair + 1) * BQ : (2 * pair + 2) * BQ]
                both = jnp.where(lane < HEAD, pltpu.roll(first, HEAD, 1), second)
                column = (g * GROUP // 2 + pair) * LANES
                att_ref[at, column : column + LANES] = both.astype(BF16)
        lse_ref[at, :] = logs

    def run(ceiling):
        def q_loop(i, _):
            acc[...] = jnp.zeros_like(acc)
            total[...] = jnp.zeros_like(total)
            pairs = (meta_ref[1 + i] + 1) // 2
            if ceiling:
                top[...] = jnp.full_like(top, 2 * MASKED)

                def top_loop(t, _):
                    spots = tile_pair(meta_ref, tiles, i, t)
                    bias = mask_bias(info_ref, seg_ref, i, spots)

                    def top_group(g, _):
                        s = masked(dot_tr(q_rows(i, g), key_pair(kv, g, spots)), bias)
                        top[g] = jnp.maximum(top[g], jnp.max(s, axis=1, keepdims=True))
                        return 0

                    lax.fori_loop(0, KV_HEADS, top_group, 0)
                    return 0

                lax.fori_loop(0, pairs, top_loop, 0)

            def k_loop(t, _):
                spots = tile_pair(meta_ref, tiles, i, t)
                bias = mask_bias(info_ref, seg_ref, i, spots)
                if ceiling:

                    def group(g, _):
                        fold(i, g, spots, bias, True)
                        return 0

                    lax.fori_loop(0, KV_HEADS, group, 0)
                else:
                    for g in range(KV_HEADS):
                        fold(i, g, spots, bias, False)
                return 0

            lax.fori_loop(0, pairs, k_loop, 0)
            finish(i, ceiling)
            return 0

        lax.fori_loop(0, rows // BQ, q_loop, 0)

    bound = largest_square(q_ref, rows // BK * BK)
    if rows % BK:
        bound = jnp.maximum(bound, largest_square(q_ref.at[:, rows - BK :, :], BK))
    bound = bound * largest_square(kv, kv.shape[1])
    limit = (SAFE_EXPONENT / SCALE2) ** 2
    safe = bound < limit

    @pl.when(safe)
    def _():
        run(False)

    @pl.when(jnp.logical_not(safe))
    def _():
        run(True)


def attention_forward(meta, q, kvs, info, seg):
    rows = q.shape[1]
    span = len(kvs)
    keys = span * rows
    tiles = keys // BK
    return pl.pallas_call(
        functools.partial(forward_kernel, tiles=tiles, span=span),
        out_shape=[
            jax.ShapeDtypeStruct((rows, D), BF16),
            jax.ShapeDtypeStruct((rows, LANES), F32),
        ],
        in_specs=[SMEM_SPACE, VMEM_SPACE] + [ANY_SPACE] * span + [VMEM_SPACE] * 2,
        out_specs=[VMEM_SPACE] * 2,
        scratch_shapes=[
            pltpu.VMEM((KV_HEADS, keys, LANES), BF16),
            pltpu.VMEM((KV_HEADS, STACK, LANES), F32),
            pltpu.VMEM((KV_HEADS, STACK, LANES), F32),
            pltpu.VMEM((KV_HEADS, STACK, LANES), F32),
            pltpu.SemaphoreType.DMA((span,)),
        ],
        compiler_params=params(52),
        cost_estimate=pl.CostEstimate(
            flops=20 * 10**9, bytes_accessed=15 * 10**6, transcendentals=3 * 10**7
        ),
        name="attention_forward",
    )(meta, q, *kvs, info, seg)


def backward_kernel(meta_ref, q_ref, da_ref, att_ref, lse_ref, cos_ref, sin_ref, *refs, tiles, span):
    kv_refs = refs[:span]
    info_ref, seg_ref, dq_ref, near_ref, far_ref, kv, dkv, dq, qd, stats, sems = refs[span:]
    rows = q_ref.shape[1]
    block = meta_ref[0]
    gather_keys(block, kv_refs, kv, sems)

    def clear(n, _):
        dkv[:, pl.ds(n * BK, BK), :] = jnp.zeros((KV_HEADS, BK, LANES), F32)
        return 0

    lax.fori_loop(0, kv.shape[1] // BK, clear, 0)
    lane = lane_iota((BQ, LANES))
    left = lane < HEAD

    def q_loop(i, _):
        at = pl.ds(pl.multiple_of(i * BQ, BQ), BQ)
        dq[...] = jnp.zeros_like(dq)
        logs = lse_ref[at, :]
        for h in range(HEADS):
            g, r = h // GROUP, h % GROUP
            column = h // 2 * LANES
            da = da_ref[at, column : column + LANES].astype(F32)
            delta = da * att_ref[at, column : column + LANES].astype(F32)
            mine = left if h % 2 == 0 else jnp.logical_not(left)
            delta = jnp.sum(jnp.where(mine, delta, 0.0), axis=1, keepdims=True)
            if h % 2 == 0:
                da = pltpu.roll(da, HEAD, 1)
            da = jnp.where(left, 0.0, da).astype(BF16)
            qd[g, r * BQ : (r + 1) * BQ, :] = q_ref[h, at, :]
            qd[g, STACK + r * BQ : STACK + (r + 1) * BQ, :] = da
            stats[g, r * BQ : (r + 1) * BQ, :] = jnp.where(left, logs[:, h : h + 1], delta)

        def k_loop(t, _):
            spots = tile_pair(meta_ref, tiles, i, t)
            bias = mask_bias(info_ref, seg_ref, i, spots)
            for g in range(KV_HEADS):
                pair = key_pair(kv, g, spots)
                both = qd[g]
                sd = dot_tr(both, pair)
                p = jnp.exp2(masked(sd[:STACK], bias) - stats[g, :, 0:1])
                ds = (p * (sd[STACK:] - stats[g, :, HEAD : HEAD + 1])).astype(BF16)
                p = p.astype(BF16)
                dq[g] += dot(ds, pair)
                moved = dot_cc(jnp.concatenate([ds, p], axis=0), both)
                for n, (first, _) in enumerate(spots):
                    dkv[g, pl.ds(first, BK), :] += moved[n * BK : (n + 1) * BK]
            return 0

        lax.fori_loop(0, (meta_ref[1 + i] + 1) // 2, k_loop, 0)
        cos = cos_ref[at, :]
        sin = sin_ref[at, :]
        low = (lane % HEAD) < HEAD // 2
        for g in range(KV_HEADS):
            for pair in range(GROUP // 2):
                first = dq[g, 2 * pair * BQ : (2 * pair + 1) * BQ]
                second = dq[g, (2 * pair + 1) * BQ : (2 * pair + 2) * BQ]
                z = jnp.where(left, first, pltpu.roll(second, HEAD, 1)) * SCALE
                z = z * cos - half_turn(z, low) * sin
                column = (g * GROUP // 2 + pair) * LANES
                dq_ref[at, column : column + LANES] = z.astype(BF16)
        return 0

    lax.fori_loop(0, rows // BQ, q_loop, 0)
    factor = jnp.where(lane < HEAD, SCALE, 1.0)
    for e in range(span):
        target = near_ref if e % 2 == 0 else far_ref
        first = (block ^ e) * rows

        def leave(n, _):
            at = pl.ds(pl.multiple_of(n * BQ, BQ), BQ)
            source = pl.ds(pl.multiple_of(first + n * BQ, BQ), BQ)
            for g in range(KV_HEADS):
                target[e // 2, g, at, :] = (dkv[g, source, :] * factor).astype(BF16)
            return 0

        lax.fori_loop(0, rows // BQ, leave, 0)


def attention_backward(meta, q, da, att, lse, cos, sin, kvs, info, seg):
    rows = q.shape[1]
    span = len(kvs)
    keys = span * rows
    tiles = keys // BK
    return pl.pallas_call(
        functools.partial(backward_kernel, tiles=tiles, span=span),
        out_shape=[
            jax.ShapeDtypeStruct((rows, D), BF16),
            jax.ShapeDtypeStruct((span // 2, KV_HEADS, rows, LANES), BF16),
            jax.ShapeDtypeStruct((span // 2, KV_HEADS, rows, LANES), BF16),
        ],
        in_specs=[SMEM_SPACE] + [VMEM_SPACE] * 6 + [ANY_SPACE] * span + [VMEM_SPACE] * 2,
        out_specs=[VMEM_SPACE] * 3,
        scratch_shapes=[
            pltpu.VMEM((KV_HEADS, keys, LANES), BF16),
            pltpu.VMEM((KV_HEADS, keys, LANES), F32),
            pltpu.VMEM((KV_HEADS, STACK, LANES), F32),
            pltpu.VMEM((KV_HEADS, 2 * STACK, LANES), BF16),
            pltpu.VMEM((KV_HEADS, STACK, LANES), F32),
            pltpu.SemaphoreType.DMA((span,)),
        ],
        compiler_params=params(60),
        cost_estimate=pl.CostEstimate(
            flops=60 * 10**9, bytes_accessed=30 * 10**6, transcendentals=3 * 10**7
        ),
        name="attention_backward",
    )(meta, q, da, att, lse, cos, sin, *kvs, info, seg)


def middle_kernel(x_ref, att_ref, w_ref, gain_ref, mid_ref, n_ref):
    mid_ref[...] = dot_tr(att_ref[...], w_ref[...])
    gain2 = gain_ref[1:2, :]

    def norm(i, _):
        at = pl.ds(pl.multiple_of(i * BQ, BQ), BQ)
        mid = x_ref[at, :].astype(F32) + mid_ref[at, :]
        scale = lax.rsqrt(jnp.mean(mid * mid, axis=1, keepdims=True) + EPSILON)
        mid_ref[at, :] = mid
        n_ref[at, :] = (mid * scale * gain2).astype(BF16)
        return 0

    lax.fori_loop(0, mid_ref.shape[0] // BQ, norm, 0)


def middle(x, att, w, gains):
    rows = x.shape[0]
    return pl.pallas_call(
        middle_kernel,
        out_shape=[
            jax.ShapeDtypeStruct((rows, D), F32),
            jax.ShapeDtypeStruct((rows, D), BF16),
        ],
        compiler_params=params(32),
        name="middle",
    )(x, att, w, gains)


def feed_forward_kernel(
    n1_ref, n2_ref, og1_ref, og2_ref, wg_ref, wu_ref, wd_ref,
    own_ref, far_ref, dw_ref,
    n, og, nt, ogt, oacc, nacc, hid, dgate, dup,
):
    f = pl.program_id(0)
    part = pl.program_id(1)
    rows = n1_ref.shape[0]

    @pl.when((f == 0) & (part == 0))
    def _():
        n[:rows] = n1_ref[...]
        n[rows:] = n2_ref[...]
        og[:rows] = og1_ref[...]
        og[rows:] = og2_ref[...]
        nt[...] = n[...].T
        ogt[...] = og[...].T
        oacc[...] = jnp.zeros_like(oacc)
        nacc[...] = jnp.zeros_like(nacc)

    @pl.when(part == 0)
    def _():
        for k in range(2):
            at = slice(k * rows, (k + 1) * rows)
            gate = dot(n[at], wg_ref[...])
            up = dot(n[at], wu_ref[...])
            grad = dot(og[at], wd_ref[...])
            sig = jax.nn.sigmoid(gate)
            silu = gate * sig
            hid[at] = (silu * up).astype(BF16)
            dgate[at] = (grad * up * sig * (1.0 + gate * (1.0 - sig))).astype(BF16)
            dup[at] = (grad * silu).astype(BF16)
        dw_ref[...] = dot(nt[...], dgate[...]).astype(BF16)

    @pl.when(part == 1)
    def _():
        nacc[...] += dot_tr(dgate[...], wg_ref[...]) + dot_tr(dup[...], wu_ref[...])
        dw_ref[...] = dot(nt[...], dup[...]).astype(BF16)

    @pl.when(part == 2)
    def _():
        oacc[...] += dot_tr(hid[...], wd_ref[...])
        dw_ref[...] = dot(ogt[...], hid[...]).astype(BF16)

    @pl.when((f == pl.num_programs(0) - 1) & (part == 2))
    def _():
        own_ref[0] = oacc[:rows].astype(BF16)
        own_ref[1] = nacc[:rows].astype(BF16)
        far_ref[0] = oacc[rows:].astype(BF16)
        far_ref[1] = nacc[rows:].astype(BF16)


def feed_forward(n_own, n_far, og_own, og_far, w):
    rows = n_own.shape[0]
    block = 256
    steps = HALF // block
    whole = pl.BlockSpec((rows, D), lambda f, k: (0, 0), pipeline_mode=pl.Buffered(1))
    sides = pl.BlockSpec((2, rows, D), lambda f, k: (0, 0, 0))
    slab = [pl.BlockSpec((D, block), lambda f, k, m=m: (0, m * steps + f)) for m in range(3)]
    return pl.pallas_call(
        feed_forward_kernel,
        grid=(steps, 3),
        in_specs=[whole] * 4 + slab,
        out_specs=[sides, sides, pl.BlockSpec((D, block), lambda f, k: (0, k * steps + f))],
        out_shape=[
            jax.ShapeDtypeStruct((2, rows, D), BF16),
            jax.ShapeDtypeStruct((2, rows, D), BF16),
            jax.ShapeDtypeStruct((D, 3 * HALF), BF16),
        ],
        scratch_shapes=[
            pltpu.VMEM((2 * rows, D), BF16),
            pltpu.VMEM((2 * rows, D), BF16),
            pltpu.VMEM((D, 2 * rows), BF16),
            pltpu.VMEM((D, 2 * rows), BF16),
            pltpu.VMEM((2 * rows, D), F32),
            pltpu.VMEM((2 * rows, D), F32),
            pltpu.VMEM((2 * rows, block), BF16),
            pltpu.VMEM((2 * rows, block), BF16),
            pltpu.VMEM((2 * rows, block), BF16),
        ],
        compiler_params=params(62),
        cost_estimate=pl.CostEstimate(
            flops=52 * 10**9, bytes_accessed=40 * 10**6, transcendentals=3 * 10**6
        ),
        name="feed_forward",
    )(n_own, n_far, og_own, og_far, w, w, w)


def turn_kernel(
    mid_ref, own_ref, got_ref, og_ref, gain_ref, w_ref, att_ref,
    out_ref, gm_ref, da_ref, dw_ref, dgain_ref, gmb,
):
    gain2 = gain_ref[1:2, :]

    def step(i, dgain):
        at = pl.ds(pl.multiple_of(i * BQ, BQ), BQ)
        mid = mid_ref[at, :]
        out = mid + (own_ref[0, at, :].astype(F32) + got_ref[0, at, :].astype(F32))
        out_ref[at, :] = out.astype(BF16)
        dn = own_ref[1, at, :].astype(F32) + got_ref[1, at, :].astype(F32)
        scale = lax.rsqrt(jnp.mean(mid * mid, axis=1, keepdims=True) + EPSILON)
        dgain = dgain + jnp.sum((dn * mid * scale).reshape(BQ // 8, 8, D), axis=0)
        q2 = dn * gain2
        mean = jnp.mean(q2 * mid, axis=1, keepdims=True)
        gm = og_ref[at, :].astype(F32) + scale * q2 - mid * (scale * scale * scale * mean)
        gm_ref[at, :] = gm
        gmb[at, :] = gm.astype(BF16)
        return dgain

    dgain = lax.fori_loop(0, mid_ref.shape[0] // BQ, step, jnp.zeros((8, D), F32))
    dgain_ref[...] = dgain
    da_ref[...] = dot(gmb[...], w_ref[...]).astype(BF16)
    dw_ref[...] = dot_cc(gmb[...], att_ref[...]).astype(BF16)


def turn(mid, own, got, og, gains, w, att):
    rows = mid.shape[0]
    return pl.pallas_call(
        turn_kernel,
        out_shape=[
            jax.ShapeDtypeStruct((rows, D), BF16),
            jax.ShapeDtypeStruct((rows, D), F32),
            jax.ShapeDtypeStruct((rows, D), BF16),
            jax.ShapeDtypeStruct((D, D), BF16),
            jax.ShapeDtypeStruct((8, D), F32),
        ],
        scratch_shapes=[pltpu.VMEM((rows, D), BF16)],
        compiler_params=params(56),
        name="turn",
    )(mid, own, got, og, gains, w, att)


def finish_kernel(
    x_ref, n_ref, gm_ref, dq_ref, k0_ref, k1_ref, k2_ref, k3_ref, k4_ref, w_ref, gain_ref,
    dgain_ref, cos_ref, sin_ref, in_ref, dw_ref, dz, dn,
):
    rows = x_ref.shape[0]
    lane = lane_iota((BQ, LANES))
    low = (lane % HEAD) < HEAD // 2
    left = lane < HEAD

    def turn_back(i, _):
        at = pl.ds(pl.multiple_of(i * BQ, BQ), BQ)
        cos = cos_ref[at, :]
        sin = sin_ref[at, :]
        for g in range(KV_HEADS):
            z = sum(
                ref[g, at, :].astype(F32) for ref in (k0_ref, k1_ref, k2_ref, k3_ref, k4_ref)
            )
            rot = z * cos - half_turn(z, low) * sin
            base = g * GROUP_COLS
            span = GROUP * HEAD
            dz[at, base : base + span] = dq_ref[at, g * span : (g + 1) * span]
            dz[at, base + span : base + span + LANES] = jnp.where(left, rot, z).astype(BF16)
        return 0

    lax.fori_loop(0, rows // BQ, turn_back, 0)
    dw_ref[:, :QKV] = dot_cc(n_ref[...], dz[...]).astype(BF16)
    dn[...] = dot_tr(dz[...], w_ref[:, :QKV])
    gain1 = gain_ref[0:1, :]

    def step(i, dgain):
        at = pl.ds(pl.multiple_of(i * BQ, BQ), BQ)
        x = x_ref[at, :].astype(F32)
        grad = dn[at, :]
        scale = lax.rsqrt(jnp.mean(x * x, axis=1, keepdims=True) + EPSILON)
        dgain = dgain + jnp.sum((grad * x * scale).reshape(BQ // 8, 8, D), axis=0)
        q1 = grad * gain1
        mean = jnp.mean(q1 * x, axis=1, keepdims=True)
        in_ref[at, :] = gm_ref[at, :] + scale * q1 - x * (scale * scale * scale * mean)
        return dgain

    dgain1 = lax.fori_loop(0, rows // BQ, step, jnp.zeros((8, D), F32))
    dgain1 = jnp.sum(dgain1, axis=0, keepdims=True)
    dgain2 = jnp.sum(dgain_ref[...], axis=0, keepdims=True)
    row = lax.broadcasted_iota(jnp.int32, (LANES, D), 0)
    both = jnp.where(row == 0, dgain1, jnp.where(row == 1, dgain2, 0.0))
    dw_ref[:, QKV:] = both.T.astype(BF16)


def finish(x, n, gm, dq, pieces, w, gains, dgain, cos, sin):
    rows = x.shape[0]
    return pl.pallas_call(
        finish_kernel,
        out_shape=[
            jax.ShapeDtypeStruct((rows, D), F32),
            jax.ShapeDtypeStruct((D, QKV_PAD), BF16),
        ],
        scratch_shapes=[pltpu.VMEM((rows, QKV), BF16), pltpu.VMEM((rows, D), F32)],
        compiler_params=params(60),
        name="finish",
    )(x, n, gm, dq, *pieces, w, gains, dgain, cos, sin)


def body(
    layer_in, out_grad, segment_ids, segment_parents, norm_gain1, w_query, w_key, w_value, w_output,
    norm_gain2, w_gate, w_up, w_down,
):
    size = lax.axis_size("fsdp")
    rows = layer_in.shape[0]
    span = TREE // rows
    shard = D // size
    me = lax.axis_index("fsdp")
    block = me % span
    tree = me // span
    core = me % 2

    def swap(v, bit):
        return lax.ppermute(v, "fsdp", [(i, i ^ bit) for i in range(size)])

    same_core = [list(range(c, size, 2)) for c in range(2)]

    grouped = [w_query.reshape(shard, KV_HEADS, GROUP * HEAD)]
    grouped += [w.reshape(shard, KV_HEADS, HEAD) for w in (w_key, w_value)]
    grouped = jnp.concatenate(grouped, axis=2).reshape(shard, QKV)
    gain_pair = jnp.stack([norm_gain1, norm_gain2], axis=1)
    gain_pair = jnp.pad(gain_pair, ((0, 0), (0, LANES - 2)))
    qkv_w = lax.all_gather(
        jnp.concatenate([grouped, gain_pair], axis=1), "fsdp", axis=0, tiled=True
    )
    out_w = lax.all_gather(w_output.T, "fsdp", axis=0, tiled=True)
    sides = [
        jnp.concatenate([w[:, c * HALF : (c + 1) * HALF] for w in (w_gate, w_up, w_down.T)], axis=1)
        for c in range(2)
    ]
    keep = jnp.where(core == 0, sides[0], sides[1])
    got = swap(jnp.where(core == 0, sides[1], sides[0]), 1)
    ordered = jnp.where(
        core == 0, jnp.concatenate([keep, got], axis=0), jnp.concatenate([got, keep], axis=0)
    )
    ff_w = lax.all_gather(ordered, "fsdp", axis=0, tiled=True, axis_index_groups=same_core)

    tree_seg = segment_ids
    bit = 1
    while bit < span:
        other = swap(tree_seg, bit)
        first = (me & bit) == 0
        tree_seg = jnp.concatenate(
            [jnp.where(first, tree_seg, other), jnp.where(first, other, tree_seg)], axis=0
        )
        bit *= 2
    seg_count = segment_parents.shape[0] * span // size
    seg_base = tree * seg_count
    tree_seg = tree_seg - seg_base
    own_seg = segment_ids - seg_base
    ids = jnp.arange(seg_count, dtype=jnp.int32)
    parent = lax.dynamic_slice_in_dim(segment_parents, seg_base, seg_count) - seg_base

    def look(index, table):
        return jnp.sum(jnp.where(index[:, None] == ids[None, :], table[None, :], 0), axis=1)

    grand = look(parent, parent)
    lengths = jnp.sum((tree_seg[None, :] == ids[:, None]).astype(jnp.int32), axis=1)
    starts = jnp.sum(jnp.where(ids[None, :] < ids[:, None], lengths[None, :], 0), axis=1)
    depth = jnp.where(parent != ids, look(parent, lengths), 0)
    depth = depth + jnp.where(grand != parent, look(grand, lengths), 0)
    own_row = block * rows + jnp.arange(rows, dtype=jnp.int32)
    positions = (look(own_seg, depth - starts) + own_row).astype(F32)
    lane = jnp.arange(LANES, dtype=jnp.int32)
    inverse = jnp.exp((lane % 32).astype(F32) * (-2.0 * math.log(ROPE_BASE) / HEAD))
    angles = positions[:, None] * inverse[None, :]
    cos = jnp.cos(angles)
    sin = jnp.sin(angles) * jnp.where(lane % HEAD < HEAD // 2, -1.0, 1.0)[None, :]
    info = [own_seg, look(own_seg, parent), look(own_seg, grand), own_row]
    info = sum(jnp.where(lane[None, :] == c, v[:, None], 0) for c, v in enumerate(info))
    tiles = TREE // BK
    steps = rows // BQ
    tile_seg = tree_seg.reshape(tiles, BK)
    tile_first, tile_last = tile_seg[:, 0], tile_seg[:, -1]
    step_seg = own_seg.reshape(steps, BQ)

    def inside(s):
        return (tile_first[None, :] <= s[:, None]) & (s[:, None] <= tile_last[None, :])

    hit = inside(ids) | inside(parent) | inside(grand)
    here = (step_seg[:, :1] <= ids[None, :]) & (ids[None, :] <= step_seg[:, -1:])
    active = jnp.any(here[:, :, None] & hit[None, :, :], axis=1)
    tile_range = jnp.arange(tiles, dtype=jnp.int32)
    last_row = block * rows + (jnp.arange(steps, dtype=jnp.int32) + 1) * BQ - 1
    active = active & (tile_range[None, :] * BK <= last_row[:, None])
    before = tile_range[:, None] < tile_range[None, :]
    place = jnp.sum((active[:, :, None] & before[None]).astype(jnp.int32), axis=1)
    chosen = active[:, :, None] & (place[:, :, None] == tile_range[None, None, :])
    listed = jnp.sum(jnp.where(chosen, tile_range[None, :, None], 0), axis=1)
    counts = jnp.sum(active.astype(jnp.int32), axis=1)
    meta = jnp.concatenate(
        [block[None], jnp.pad(counts, (0, BQ - steps)), listed.reshape(steps * tiles)]
    )
    seg_row = tree_seg[None, :]

    og_far = swap(out_grad, 1)
    normed1, q, kv, gains = project(layer_in, qkv_w, cos, sin)
    kvs = [kv, swap(kv, 1)]
    for chip in range(1, span // 2):
        piece = swap(kv, 2 * chip)
        kvs += [piece, swap(piece, 1)]
    att, lse = attention_forward(meta, q, kvs, info, seg_row)
    mid, normed2 = middle(layer_in, att, out_w, gains)
    own, far, ff_dw = feed_forward(normed2, swap(normed2, 1), out_grad, og_far, ff_w)
    layer_out, grad_mid, da, out_dw, dgain2 = turn(
        mid, own, swap(far, 1), out_grad, gains, out_w, att
    )
    ff_dw = lax.psum_scatter(
        ff_dw, "fsdp", scatter_dimension=0, tiled=True, axis_index_groups=same_core
    )
    out_dw = lax.psum_scatter(out_dw, "fsdp", scatter_dimension=0, tiled=True)
    dq, near, far = attention_backward(meta, q, da, att, lse, cos, sin, kvs, info, seg_row)
    got = swap(far, 1)
    pieces = [near[0], got[0]]
    for chip in range(1, span // 2):
        both = (near[chip].astype(F32) + got[chip].astype(F32)).astype(BF16)
        pieces.append(swap(both, 2 * chip))
    input_grad, qkv_dw = finish(
        layer_in, normed1, grad_mid, dq, pieces, qkv_w, gains, dgain2, cos, sin
    )
    qkv_dw = lax.psum_scatter(qkv_dw, "fsdp", scatter_dimension=0, tiled=True).astype(F32)

    groups = qkv_dw[:, :QKV].reshape(shard, KV_HEADS, GROUP_COLS)
    grad_query = groups[:, :, : GROUP * HEAD].reshape(shard, HEADS * HEAD)
    grad_key = groups[:, :, GROUP * HEAD : GROUP * HEAD + HEAD].reshape(shard, KV_HEADS * HEAD)
    grad_value = groups[:, :, GROUP * HEAD + HEAD :].reshape(shard, KV_HEADS * HEAD)
    mine = jnp.where(core == 0, ff_dw[:shard], ff_dw[shard:])
    got = swap(jnp.where(core == 0, ff_dw[shard:], ff_dw[:shard]), 1)
    low = jnp.where(core == 0, mine, got).astype(F32).reshape(shard, 3, HALF)
    high = jnp.where(core == 0, got, mine).astype(F32).reshape(shard, 3, HALF)
    ff_grads = jnp.concatenate([low, high], axis=2)
    return (
        layer_out,
        input_grad,
        qkv_dw[:, QKV],
        grad_query,
        grad_key,
        grad_value,
        out_dw.astype(F32).T,
        qkv_dw[:, QKV + 1],
        ff_grads[:, 0],
        ff_grads[:, 1],
        ff_grads[:, 2].T,
    )


def solution(mesh):
    rows, cols, flat = P("fsdp", None), P(None, "fsdp"), P("fsdp")
    return jax.shard_map(
        body,
        mesh=mesh,
        in_specs=(rows, rows, flat, P(), flat, rows, rows, rows, cols, flat, rows, rows, cols),
        out_specs=(rows, rows, flat, rows, rows, rows, cols, flat, rows, rows, cols),
        check_vma=False,
    )
```

time: 2940 us -> 943 us (0.32)
  waiting for transfers between devices: 1890 us -> 544 us
  blocking collectives: 414 us -> 0 us
  matrix products: 280 us -> 0 us
  Pallas kernels: 0 us -> 209 us
  other arithmetic: 94.8 us -> 12.6 us
  local copies, waits for them, and re-layouts: 81.2 us -> 24.6 us
    ppermute x14 -> x19, waiting for transfers between devices: 921 us -> 97.7 us  [swap(): return lax.ppermute(v, 'fsdp', [(i, i ^ bit) for i in range(size)])]
    reduce_scatter x5 -> x3, waiting for transfers between devices: 897 us -> 267 us  [the longest x1 139 us: body(): lax.psum_scatter(qkv_dw, 'fsdp', scatter_dimension=0, tiled=True)]
    unnamed x2 -> x0, blocking collectives: 286 us -> none
    dot_general x30 -> x0, matrix products: 280 us -> none  [the longest x3 48 us: masked_scores(): jnp.einsum('qhgd,khd->hgqk', query_groups, piece_keys(packed_piece), pref...]
    pallas_call x0 -> x7, Pallas kernels: none -> 209 us  [the longest x1 72.2 us: feed_forward(): pl.pallas_call(feed_forward_kernel, grid=(steps, 3), in_specs=[whole] * 4...]
    all_gather x5 -> x3, waiting for transfers between devices: 4.82 us -> 179 us  [the longest x1 126 us: body(): lax.all_gather(ordered, 'fsdp', axis=0, tiled=True, axis_index_groups=sam...]
    all_gather x2 -> x0, blocking collectives: 86.3 us -> none  [the longest x1 44.9 us: body(): lax.all_gather(w_key, 'fsdp', axis=0, tiled=True)]
    unnamed x14 -> x6, waiting for transfers between devices: 68.4 us -> 0.78 us
  transfers between devices with their start and end apart: 26 -> 25, of which waited for: 12 -> 18; matrix products, arithmetic and copies ran while one was open for 8% -> 2% of each run, Pallas kernels for 0% -> 15%
where the time goes in v1:
time: 943 us; the launch traced here: 934 us
  waiting for transfers between devices  544 us (58%)
  Pallas kernels  209 us (22%)
  starting transfers between devices  129 us (14%)
  local copies, waits for them, and re-layouts  24.6 us (3%)
  between operations  14.9 us (2%)
  other arithmetic  12.6 us (1%)
    reduce_scatter x1, waiting for transfers between devices, body(): lax.psum_scatter(qkv_dw, 'fsdp', scatter_dimension=0, tiled=True)  139 us
    ppermute x19, starting transfers between devices, swap(): return lax.ppermute(v, 'fsdp', [(i, i ^ bit) for i in range(size)])  129 us
    reduce_scatter x1, waiting for transfers between devices, body(): out_dw = lax.psum_scatter(out_dw, 'fsdp', scatter_dimension=0, tiled=True)  127 us
    all_gather x1, waiting for transfers between devices, body(): lax.all_gather(ordered, 'fsdp', axis=0, tiled=True, axis_index_groups=sam...  126 us
    ppermute x19, waiting for transfers between devices, swap(): return lax.ppermute(v, 'fsdp', [(i, i ^ bit) for i in range(size)])  97.7 us
    pallas_call x1, Pallas kernels, feed_forward(): pl.pallas_call(feed_forward_kernel, grid=(steps, 3), in_specs=[whole] * 4...  72.2 us
    all_gather x1, waiting for transfers between devices, body(): lax.all_gather(jnp.concatenate([grouped, gain_pair], axis=1), 'fsdp', axi...  52.4 us
    pallas_call x1, Pallas kernels, attention_backward(): pl.pallas_call(functools.partial(backward_kernel, tiles=tiles, span=span)...  47.3 us
  transfers between devices with their start and end apart: 25, of which 18 were waited for; matrix products, arithmetic and copies ran while one was open for 2% of the time, Pallas kernels for 15%

profile of v1, /device:TPU:0, one launch (start us, length us, event | category | flops | bytes accessed | tf_op | source)
XLA Modules:
  0.0 934.0 jit_solution(6683644662861047431)
XLA Ops:
  17.2 2.9 collective-permute-start.1
  21.7 2.1 collective-permute-start.2
  27.4 52.4 %all-gather.4.cloned.1.call-done.w_ref = bf16[1280,2048]{1,0:T(8,128)(2,1)} async-done(((bf16[40,2048]{1,0:T(8,128)(2,1)}), bf16[1280,2048]{1,0:T(8,128)(2,1)}) %all-gather.4.cloned.1.call-update) | async-done | bytes 5242896 | tf_op jit(solution)/shard_map/all_gather | solution.py:653
  79.9 10.1 %project.1 = (bf16[640,1280]{1,0:T(8,128)(2,1)S(1)}, bf16[20,640,128]{2,1,0:T(8,128)(2,1)}, bf16[5,640,128]{2,1,0:T(8,128)(2,1)S(1)}, f32[8,1280]{1,0:T(8,128)S(1)}) custom-call(bf16[640,1280]{1,0:T(8,128)(2,1)S(1)} %copy-done, bf16[1280,2048]{1,0:T(8,128)(2,1)} %all-gather.4.cloned.1.call-done.w_ref, f32[640,128]{1,0:T(8,128)S(1)} %get-tuple-element.92.cos_ref, ...), custom_call_target="tpu_custom_call" | custom-call | tf_op jit(solution)/shard_map/project/pallas_call | solution.py:102
  95.6 17.8 %collective-permute-done.8.refs_6_ = bf16[5,640,128]{2,1,0:T(8,128)(2,1)} collective-permute-done((bf16[5,640,128]{2,1,0:T(8,128)(2,1)S(1)}, bf16[5,640,128]{2,1,0:T(8,128)(2,1)}, u32[]{:S(2)}, u32[]{:S(2)}) %collective-permute-start.8) | collective-permute-done | bytes 819232 | tf_op jit(solution)/shard_map/ppermute | solution.py:644
  113.3 18.3 %collective-permute-done.6.refs_4_ = bf16[5,640,128]{2,1,0:T(8,128)(2,1)} collective-permute-done((bf16[5,640,128]{2,1,0:T(8,128)(2,1)S(1)}, bf16[5,640,128]{2,1,0:T(8,128)(2,1)}, u32[]{:S(2)}, u32[]{:S(2)}) %collective-permute-start.6) | collective-permute-done | bytes 819232 | tf_op jit(solution)/shard_map/ppermute | solution.py:644
  136.6 39.1 %attention_forward.1 = (bf16[640,1280]{1,0:T(8,128)(2,1)}, f32[640,128]{1,0:T(8,128)S(1)}) custom-call(s32[229]{0:T(256)S(1)} %fusion.12.meta_ref, bf16[20,640,128]{2,1,0:T(8,128)(2,1)} %get-tuple-element.32.q_ref, bf16[5,640,128]{2,1,0:T(8,128)(2,1)S(1)} %get-tuple-element.33.refs_0_, bf16[5,640,128]{2,1,0:T(8,128)(2,1)} %copy-done.26, ...), custom_call_target="tpu_custom_call" | custom-call | flops 20000000000 | bytes 15000000 | tf_op jit(solution)/shard_map/attention_forward/pallas_call | solution.py:276
  179.2 3.2 middle.1
  185.3 10.1 %collective-permute-start.10 = (bf16[640,1280]{1,0:T(8,128)(2,1)S(1)}, bf16[640,1280]{1,0:T(8,128)(2,1)S(1)}, u32[]{:S(2)}, u32[]{:S(2)}) collective-permute-start(bf16[640,1280]{1,0:T(8,128)(2,1)S(1)} %get-tuple-element.37.n1_ref), channel_id=1, source_target_pairs={{0,1},{1,0},{2,3},{3,2},{4,5},{5,4},{6,7},{7,6},{8,9},{9,8},{10,11... | collective-permute-start | bytes 4915208 | tf_op jit(solution)/shard_map/ppermute | solution.py:644
  195.4 3.1 collective-permute-done.10.n2_ref
  198.5 126.5 %all-gather.8.cloned.1.call-done.wg_ref.wu_ref.wd_ref = bf16[1280,5376]{1,0:T(8,128)(2,1)} async-done(((bf16[80,5376]{1,0:T(8,128)(2,1)}), bf16[1280,5376]{1,0:T(8,128)(2,1)}) %all-gather.8.cloned.1.call-update) | async-done | bytes 13762576 | tf_op jit(solution)/shard_map/all_gather | solution.py:666
  325.0 72.2 %feed_forward.1 = (bf16[2,640,1280]{2,1,0:T(8,128)(2,1)}, bf16[2,640,1280]{2,1,0:T(8,128)(2,1)}, bf16[1280,5376]{1,0:T(8,128)(2,1)}) custom-call(bf16[640,1280]{1,0:T(8,128)(2,1)} %copy-done.11, bf16[640,1280]{1,0:T(8,128)(2,1)} %copy-done.25, bf16[640,1280]{1,0:T(8,128)(2,1)} %og_ref.1, bf16[640,1280]{1,0:T(8,128)(2,1)} %collective-permute-done.11.og2_ref, ...), custom_call_target="tpu_custom_call" | custom-call | flops 51999997952 | bytes 40000000 | tf_op jit(solution)/shard_map/feed_forward/pallas_call | solution.py:495
  397.3 6.0 collective-permute-done.13.got_ref
  405.0 16.6 %turn.1 = (bf16[640,1280]{1,0:T(8,128)(2,1)}, f32[640,1280]{1,0:T(8,128)}, bf16[640,1280]{1,0:T(8,128)(2,1)}, bf16[1280,1280]{1,0:T(8,128)(2,1)}, f32[8,1280]{1,0:T(8,128)}) custom-call(f32[640,1280]{1,0:T(8,128)} %copy-done.3, bf16[2,640,1280]{2,1,0:T(8,128)(2,1)} %get-tuple-element.38.own_ref, bf16[2,640,1280]{2,1,0:T(8,128)(2,1)} %copy-done.15, ...), custom_call_target="tpu_custom_call" | custom-call | tf_op jit(solution)/shard_map/turn/pallas_call | solution.py:553
  421.7 47.3 %attention_backward.1 = (bf16[640,1280]{1,0:T(8,128)(2,1)}, bf16[4,5,640,128]{3,2,1,0:T(8,128)(2,1)}, bf16[4,5,640,128]{3,2,1,0:T(8,128)(2,1)}) custom-call(s32[229]{0:T(256)} %copy-done.10, bf16[20,640,128]{2,1,0:T(8,128)(2,1)} %get-tuple-element.32.q_ref, bf16[640,1280]{1,0:T(8,128)(2,1)} %get-tuple-element.43.da_ref, ...), custom_call_target="tpu_custom_call" | custom-call | flops 60000002048 | bytes 30000000 | tf_op jit(solution)/shard_map/attention_backward/pallas_call | solution.py:383
  469.0 22.8 %collective-permute-start.14 = (bf16[4,5,640,128]{3,2,1,0:T(8,128)(2,1)}, bf16[4,5,640,128]{3,2,1,0:T(8,128)(2,1)S(1)}, u32[]{:S(2)}, u32[]{:S(2)}) collective-permute-start(bf16[4,5,640,128]{3,2,1,0:T(8,128)(2,1)} %get-tuple-element.47), channel_id=1, source_target_pairs={{0,1},{1,0},{2,3},{3,2},{4,5},{5,4},{6,7},{7,6},{8,9},{9,8},{10,11... | collective-permute-start | bytes 9830408 | tf_op jit(solution)/shard_map/ppermute | solution.py:644
  491.8 5.7 collective-permute-done.14
  497.5 2.3 fusion.2
  499.8 85.5 %collective-permute-start.17 = (bf16[5,640,128]{2,1,0:T(8,128)(2,1)S(1)}, bf16[5,640,128]{2,1,0:T(8,128)(2,1)S(1)}, u32[]{:S(2)}, u32[]{:S(2)}) collective-permute-start(bf16[5,640,128]{2,1,0:T(8,128)(2,1)S(1)} %get-tuple-element.67), channel_id=1, source_target_pairs={{0,6},{1,7},{2,4},{3,5},{4,2},{5,3},{6,0},{7,1},{8,14},{9,15},{10,... | collective-permute-start | bytes 2457608 | tf_op jit(solution)/shard_map/ppermute | solution.py:644
  589.0 15.4 %collective-permute-done.17.k4_ref = bf16[5,640,128]{2,1,0:T(8,128)(2,1)S(1)} collective-permute-done((bf16[5,640,128]{2,1,0:T(8,128)(2,1)S(1)}, bf16[5,640,128]{2,1,0:T(8,128)(2,1)S(1)}, u32[]{:S(2)}, u32[]{:S(2)}) %collective-permute-start.17) | collective-permute-done | bytes 819232 | tf_op jit(solution)/shard_map/ppermute | solution.py:644
  604.3 23.2 %collective-permute-done.16.k3_ref = bf16[5,640,128]{2,1,0:T(8,128)(2,1)S(1)} collective-permute-done((bf16[5,640,128]{2,1,0:T(8,128)(2,1)S(1)}, bf16[5,640,128]{2,1,0:T(8,128)(2,1)S(1)}, u32[]{:S(2)}, u32[]{:S(2)}) %collective-permute-start.16) | collective-permute-done | bytes 819232 | tf_op jit(solution)/shard_map/ppermute | solution.py:644
  628.7 20.3 %finish.1 = (f32[640,1280]{1,0:T(8,128)}, bf16[1280,2048]{1,0:T(8,128)(2,1)}) custom-call(bf16[640,1280]{1,0:T(8,128)(2,1)} %x_ref.5, bf16[640,1280]{1,0:T(8,128)(2,1)} %copy-done.6, f32[640,1280]{1,0:T(8,128)} %get-tuple-element.42.gm_ref, bf16[640,1280]{1,0:T(8,128)(2,1)} %get-tuple-element.45.dq_ref, bf16[5,640,128]{2,1,0:T(8,128)(2,1)} %slice_bitcast_fusion.1.k0_ref, ...), custom_call_target="tpu_custom_call" | custom-call | tf_op jit(solution)/shard_map/finish/pallas_call | solution.py:618
  650.4 127.1 %reduce-scatter.6.cloned.1.call-done = bf16[40,1280]{1,0:T(8,128)(2,1)} async-done(((bf16[1280,1280]{1,0:T(8,128)(2,1)}), bf16[40,1280]{1,0:T(8,128)(2,1)}) %reduce-scatter.6.cloned.1.call-update) | async-done | bytes 102416 | tf_op jit(solution)/shard_map/reduce_scatter | solution.py:741
  779.1 139.4 %reduce-scatter.4.cloned.1.call-done = bf16[40,2048]{1,0:T(8,128)(2,1)} async-done(((bf16[1280,2048]{1,0:T(8,128)(2,1)}), bf16[40,2048]{1,0:T(8,128)(2,1)}) %reduce-scatter.4.cloned.1.call-update) | async-done | bytes 163856 | tf_op jit(solution)/shard_map/reduce_scatter | solution.py:751
  (170 shorter events, 49.6 us)
Async XLA Ops:
  7.2 72.6 %all-gather.4.cloned.1.call-start = ((), (), s32[]{:S(2)}) async-start(), calls=%async_computation.3 | async-start | bytes 5406720 | tf_op jit(solution)/shard_map/all_gather | solution.py:653
  11.7 164.1 %all-gather.6.cloned.1.call-start = ((), (), s32[]{:S(2)}) async-start(), calls=%async_computation.4 | async-start | bytes 3379200 | tf_op jit(solution)/shard_map/all_gather | solution.py:656
  12.4 312.5 %all-gather.8.cloned.1.call-start = ((), (), s32[]{:S(2)}) async-start(), calls=%async_computation.5 | async-start | bytes 14622720 | tf_op jit(solution)/shard_map/all_gather | solution.py:666
  12.8 1.9 collective-permute-start.12
  15.8 633.2 %reduce-scatter.8.cloned.1.call-start = ((), (), s32[]{:S(2)}) async-start(), calls=%async_computation.8 | async-start | bytes 14622720 | tf_op jit(solution)/shard_map/reduce_scatter | solution.py:738
  16.3 179.0 %collective-permute-start.11 = (bf16[640,1280]{1,0:T(8,128)(2,1)}, bf16[640,1280]{1,0:T(8,128)(2,1)}, u32[]{:S(2)}, u32[]{:S(2)}) collective-permute-start(bf16[640,1280]{1,0:T(8,128)(2,1)} %og_ref.1), channel_id=1, source_target_pairs={{0,1},{1,0},{2,3},{3,2},{4,5},{5,4},{6,7},{7,6},{8,9},{9,8},{10,11... | collective-permute-start | bytes 4915208 | tf_op jit(solution)/shard_map/ppermute | solution.py:644
  17.2 4.5 collective-permute-start.1
  21.7 3.8 collective-permute-start.2
  91.2 22.1 %collective-permute-start.8 = (bf16[5,640,128]{2,1,0:T(8,128)(2,1)S(1)}, bf16[5,640,128]{2,1,0:T(8,128)(2,1)}, u32[]{:S(2)}, u32[]{:S(2)}) collective-permute-start(bf16[5,640,128]{2,1,0:T(8,128)(2,1)S(1)} %get-tuple-element.33.refs_0_), channel_id=1, source_target_pairs={{0,6},{1,7},{2,4},{3,5},{4,2},{5,3},{6,0},{7,1},{8,14},{9,15},{10,... | collective-permute-start | bytes 2457608 | tf_op jit(solution)/shard_map/ppermute | solution.py:644
  92.7 39.0 %collective-permute-start.6 = (bf16[5,640,128]{2,1,0:T(8,128)(2,1)S(1)}, bf16[5,640,128]{2,1,0:T(8,128)(2,1)}, u32[]{:S(2)}, u32[]{:S(2)}) collective-permute-start(bf16[5,640,128]{2,1,0:T(8,128)(2,1)S(1)} %get-tuple-element.33.refs_0_), channel_id=1, source_target_pairs={{0,4},{1,5},{2,6},{3,7},{4,0},{5,1},{6,2},{7,3},{8,12},{9,13},{10,... | collective-permute-start | bytes 2457608 | tf_op jit(solution)/shard_map/ppermute | solution.py:644
  94.1 39.0 %collective-permute-start.4 = (bf16[5,640,128]{2,1,0:T(8,128)(2,1)S(1)}, bf16[5,640,128]{2,1,0:T(8,128)(2,1)}, u32[]{:S(2)}, u32[]{:S(2)}) collective-permute-start(bf16[5,640,128]{2,1,0:T(8,128)(2,1)S(1)} %get-tuple-element.33.refs_0_), channel_id=1, source_target_pairs={{0,2},{1,3},{2,0},{3,1},{4,6},{5,7},{6,4},{7,5},{8,10},{9,11},{10,... | collective-permute-start | bytes 2457608 | tf_op jit(solution)/shard_map/ppermute | solution.py:644
  95.5 38.2 %collective-permute-start.3 = (bf16[5,640,128]{2,1,0:T(8,128)(2,1)S(1)}, bf16[5,640,128]{2,1,0:T(8,128)(2,1)S(1)}, u32[]{:S(2)}, u32[]{:S(2)}) collective-permute-start(bf16[5,640,128]{2,1,0:T(8,128)(2,1)S(1)} %get-tuple-element.33.refs_0_), channel_id=1, source_target_pairs={{0,1},{1,0},{2,3},{3,2},{4,5},{5,4},{6,7},{7,6},{8,9},{9,8},{10,11... | collective-permute-start | bytes 2457608 | tf_op jit(solution)/shard_map/ppermute | solution.py:644
  113.3 20.4 %collective-permute-start.9 = (bf16[5,640,128]{2,1,0:T(8,128)(2,1)}, bf16[5,640,128]{2,1,0:T(8,128)(2,1)S(1)}, u32[]{:S(2)}, u32[]{:S(2)}) collective-permute-start(bf16[5,640,128]{2,1,0:T(8,128)(2,1)} %collective-permute-done.8.refs_6_), channel_id=1, source_target_pairs={{0,1},{1,0},{2,3},{3,2},{4,5},{5,4},{6,7},{7,6},{8,9},{9,8},{10,11... | collective-permute-start | bytes 2457608 | tf_op jit(solution)/shard_map/ppermute | solution.py:644
  131.7 2.5 collective-permute-start.7
  133.1 2.5 collective-permute-start.5
  185.3 13.2 %collective-permute-start.10 = (bf16[640,1280]{1,0:T(8,128)(2,1)S(1)}, bf16[640,1280]{1,0:T(8,128)(2,1)S(1)}, u32[]{:S(2)}, u32[]{:S(2)}) collective-permute-start(bf16[640,1280]{1,0:T(8,128)(2,1)S(1)} %get-tuple-element.37.n1_ref), channel_id=1, source_target_pairs={{0,1},{1,0},{2,3},{3,2},{4,5},{5,4},{6,7},{7,6},{8,9},{9,8},{10,11... | collective-permute-start | bytes 4915208 | tf_op jit(solution)/shard_map/ppermute | solution.py:644
  397.2 380.3 %reduce-scatter.6.cloned.1.call-start = ((), (), s32[]{:S(2)}) async-start(), calls=%async_computation.7 | async-start | bytes 3379200 | tf_op jit(solution)/shard_map/reduce_scatter | solution.py:741
  397.3 6.1 collective-permute-start.13
  421.6 496.9 %reduce-scatter.4.cloned.1.call-start = ((), (), s32[]{:S(2)}) async-start(), calls=%async_computation.6 | async-start | bytes 5406720 | tf_op jit(solution)/shard_map/reduce_scatter | solution.py:751
  469.0 28.5 %collective-permute-start.14 = (bf16[4,5,640,128]{3,2,1,0:T(8,128)(2,1)}, bf16[4,5,640,128]{3,2,1,0:T(8,128)(2,1)S(1)}, u32[]{:S(2)}, u32[]{:S(2)}) collective-permute-start(bf16[4,5,640,128]{3,2,1,0:T(8,128)(2,1)} %get-tuple-element.47), channel_id=1, source_target_pairs={{0,1},{1,0},{2,3},{3,2},{4,5},{5,4},{6,7},{7,6},{8,9},{9,8},{10,11... | collective-permute-start | bytes 9830408 | tf_op jit(solution)/shard_map/ppermute | solution.py:644
  499.8 104.6 %collective-permute-start.17 = (bf16[5,640,128]{2,1,0:T(8,128)(2,1)S(1)}, bf16[5,640,128]{2,1,0:T(8,128)(2,1)S(1)}, u32[]{:S(2)}, u32[]{:S(2)}) collective-permute-start(bf16[5,640,128]{2,1,0:T(8,128)(2,1)S(1)} %get-tuple-element.67), channel_id=1, source_target_pairs={{0,6},{1,7},{2,4},{3,5},{4,2},{5,3},{6,0},{7,1},{8,14},{9,15},{10,... | collective-permute-start | bytes 2457608 | tf_op jit(solution)/shard_map/ppermute | solution.py:644
  585.3 42.2 %collective-permute-start.16 = (bf16[5,640,128]{2,1,0:T(8,128)(2,1)S(1)}, bf16[5,640,128]{2,1,0:T(8,128)(2,1)S(1)}, u32[]{:S(2)}, u32[]{:S(2)}) collective-permute-start(bf16[5,640,128]{2,1,0:T(8,128)(2,1)S(1)} %get-tuple-element.68), channel_id=1, source_target_pairs={{0,4},{1,5},{2,6},{3,7},{4,0},{5,1},{6,2},{7,3},{8,12},{9,13},{10,... | collective-permute-start | bytes 2457608 | tf_op jit(solution)/shard_map/ppermute | solution.py:644
  585.3 42.2 %collective-permute-start.15 = (bf16[5,640,128]{2,1,0:T(8,128)(2,1)S(1)}, bf16[5,640,128]{2,1,0:T(8,128)(2,1)S(1)}, u32[]{:S(2)}, u32[]{:S(2)}) collective-permute-start(bf16[5,640,128]{2,1,0:T(8,128)(2,1)S(1)} %get-tuple-element.69), channel_id=1, source_target_pairs={{0,2},{1,3},{2,0},{3,1},{4,6},{5,7},{6,4},{7,5},{8,10},{9,11},{10,... | collective-permute-start | bytes 2457608 | tf_op jit(solution)/shard_map/ppermute | solution.py:644
  650.3 272.3 %collective-permute-start.18 = (bf16[40,5376]{1,0:T(8,128)(2,1)S(1)}, bf16[40,5376]{1,0:T(8,128)(2,1)S(1)}, u32[]{:S(2)}, u32[]{:S(2)}) collective-permute-start(bf16[40,5376]{1,0:T(8,128)(2,1)S(1)} %broadcast_select_fusion.2), channel_id=1, source_target_pairs={{0,1},{1,0},{2,3},{3,2},{4,5},{5,4},{6,7},{7,6},{8,9},{9,8},{10,11... | collective-permute-start | bytes 1290248 | tf_op jit(solution)/shard_map/ppermute | solution.py:644
  (31 other events, 690.4 us)
Sparse Core Ops, SparseCore 0:
  11.8 68.0 all-gather.3
  82.7 77.3 all-gather.5
  162.9 161.9 all-gather.7
  397.3 240.2 reduce-scatter.7
  639.8 137.6 reduce-scatter.5
  779.7 138.7 reduce-scatter.3

commit v2 on v1

--- a/solution.py
+++ b/solution.py
@@ -23,6 +23,7 @@
 BQ = 128
 BK = 256
 STACK = GROUP * BQ
+HEAD_PARTS = ((0, 3), (3, 2))
 
 EPSILON = 1e-05
 ROPE_BASE = 10000.0
@@ -65,7 +66,25 @@
     return jnp.where(low, pltpu.roll(z, LANES - 32, 1), pltpu.roll(z, 32, 1))
 
 
-def project_kernel(x_ref, w_ref, cos_ref, sin_ref, n_ref, q_ref, kv_ref, gain_ref):
+def assembly(place_ref, piece_refs, w, sems):
+    copies = []
+    for e, ref in enumerate(piece_refs):
+        parts, rows, cols = ref.shape
+        col = pl.multiple_of(place_ref[e] * cols, LANES)
+        for part in range(parts):
+            k = len(copies)
+            row = pl.multiple_of(place_ref[len(piece_refs) + k] * rows, 16)
+            to = w.at[pl.ds(row, rows), pl.ds(col, cols)]
+            copies.append(pltpu.make_async_copy(ref.at[part], to, sems.at[k]))
+    for copy in copies:
+        copy.start()
+    return copies
+
+
+def project_kernel(place_ref, x_ref, cos_ref, sin_ref, *refs):
+    piece_refs, (n_ref, q_ref, kv_ref, gain_ref, w_ref, top_ref, sems) = refs[:-7], refs[-7:]
+    for copy in assembly(place_ref, piece_refs, w_ref, sems):
+        copy.wait()
     gains = w_ref[:, QKV:].astype(F32).T
     gain_ref[...] = gains[:8, :]
     gain1 = gains[0:1, :]
@@ -84,53 +103,75 @@
     left = lane < HEAD
     cos = cos_ref[...]
     sin = sin_ref[...]
+    same = (lax.broadcasted_iota(jnp.int32, (LANES, LANES), 0) < HEAD) == left[:LANES]
+    same = jnp.where(same, 1.0, 0.0).astype(BF16)
+
+    def squares(z):
+        sums = dot((z * z).astype(BF16), same)
+        return jnp.max(sums.reshape(rows // 8, 8, LANES), axis=0)
+
+    q_top = jnp.zeros((8, LANES), F32)
+    k_top = jnp.zeros((8, LANES), F32)
     for g in range(KV_HEADS):
         z = dot(n_ref[...], w_ref[:, g * GROUP_COLS : (g + 1) * GROUP_COLS])
         for pair in range(GROUP // 2):
             zp = z[:, pair * LANES : (pair + 1) * LANES]
             rot = (zp * cos + half_turn(zp, low) * sin).astype(BF16).astype(F32)
+            q_top = jnp.maximum(q_top, squares(rot))
             head = g * GROUP + 2 * pair
             q_ref[head] = jnp.where(left, rot, 0.0).astype(BF16)
             q_ref[head + 1] = jnp.where(left, pltpu.roll(rot, HEAD, 1), 0.0).astype(BF16)
         zk = z[:, GROUP * HEAD :]
         rot = zk * cos + half_turn(zk, low) * sin
-        kv_ref[g] = jnp.where(left, rot, zk).astype(BF16)
-
-
-def project(x, w, cos, sin):
+        k_top = jnp.maximum(k_top, squares(rot))
+        kv_ref[g, :rows] = jnp.where(left, rot, zk).astype(BF16)
+    top_ref[...] = q_top
+    k_top = jnp.max(jnp.where(left[:8], k_top, 0.0)) * 1.02
+    kv_ref[:, rows:] = jnp.full((KV_HEADS, 16, LANES), k_top, F32).astype(BF16)
+
+
+def project(place, x, cos, sin, pieces):
     rows = x.shape[0]
+    count = sum(p.shape[0] for p in pieces)
     return pl.pallas_call(
         project_kernel,
         out_shape=[
             jax.ShapeDtypeStruct((rows, D), BF16),
             jax.ShapeDtypeStruct((HEADS, rows, LANES), BF16),
-            jax.ShapeDtypeStruct((KV_HEADS, rows, LANES), BF16),
+            jax.ShapeDtypeStruct((KV_HEADS, rows + 16, LANES), BF16),
             jax.ShapeDtypeStruct((8, D), F32),
+            jax.ShapeDtypeStruct((D, QKV_PAD), BF16),
+            jax.ShapeDtypeStruct((8, LANES), F32),
         ],
+        in_specs=[SMEM_SPACE] + [VMEM_SPACE] * 3 + [ANY_SPACE] * len(pieces),
+        out_specs=[VMEM_SPACE] * 6,
+        scratch_shapes=[pltpu.SemaphoreType.DMA((count,))],
         compiler_params=params(48),
         name="project",
-    )(x, w, cos, sin)
-
-
-def gather_keys(block, kv_refs, kv, sems):
-    rows = kv_refs[0].shape[1]
+    )(place, x, cos, sin, *pieces)
+
+
+def gather_keys(block, kv_refs, kv, sems, heads):
+    rows = kv_refs[0].shape[1] - 16
     copies = []
     for e, ref in enumerate(kv_refs):
         at = pl.multiple_of((block ^ e) * rows, LANES)
-        copies.append(pltpu.make_async_copy(ref, kv.at[:, pl.ds(at, rows), :], sems.at[e]))
-    for copy in copies:
-        copy.start()
-    for copy in copies:
-        copy.wait()
-
-
-def tile_pair(meta_ref, tiles, i, t):
+        to = kv.at[:, pl.ds(at, rows), :]
+        copies.append(pltpu.make_async_copy(ref.at[heads, pl.ds(0, rows), :], to, sems.at[e]))
+    return copies
+
+
+def tile_pair(meta_ref, tiles, i, k):
     spots = []
     count = meta_ref[1 + i]
-    for k in (2 * t, 2 * t + 1):
+    for k in (k, k + 1):
         first = pl.multiple_of(meta_ref[1 + BQ + i * tiles + jnp.minimum(k, count - 1)] * BK, BK)
         spots.append((first, jnp.where(k < count, first, FAR)))
     return spots
+
+
+def open_tiles(meta_ref, i):
+    return meta_ref[1 + BQ // 2 + i] // 2 * 2
 
 
 def mask_bias(info_ref, seg_ref, i, spots):
@@ -153,54 +194,59 @@
     return (s.reshape(GROUP, BQ, 2 * BK) * SCALE2 + bias[None]).reshape(STACK, 2 * BK)
 
 
-def largest_square(ref, rows):
-    ones = jnp.where(lax.broadcasted_iota(jnp.int32, (LANES, LANES), 0) < HEAD, 1.0, 0.0)
-    ones = ones.astype(BF16)
-
-    def step(n, top):
-        for g in range(ref.shape[0]):
-            v = ref[g, pl.ds(n * BK, BK), :].astype(F32)
-            sums = dot((v * v).astype(BF16), ones)
-            top = jnp.maximum(top, jnp.max(sums.reshape(BK // 8, 8, LANES), axis=0))
-        return top
-
-    top = lax.fori_loop(0, rows // BK, step, jnp.zeros((8, LANES), F32))
-    return jnp.max(top)
-
-
-def forward_kernel(
-    meta_ref, q_ref, *refs, tiles, span
-):
+def split_keys(kv, first, second):
+    left = lane_iota((BK, LANES)) < HEAD
+    one = jnp.ones((BK, LANES), BF16)
+
+    def step(n, _):
+        at = pl.ds(pl.multiple_of(n * BK, BK), BK)
+        for g in range(kv.shape[0]):
+            v = kv[g, at, :]
+            second[g, at, :] = jnp.where(left, one, v)
+            if first is not None:
+                first[g, at, :] = jnp.where(left, v, one)
+        return 0
+
+    lax.fori_loop(0, kv.shape[1] // BK, step, 0)
+
+
+def forward_kernel(meta_ref, q_ref, top_ref, *refs, tiles, span):
     kv_refs = refs[:span]
-    info_ref, seg_ref, att_ref, lse_ref, kv, acc, total, top, sems = refs[span:]
+    info_ref, seg_ref, att_ref, lse_ref, kv, val, acc, top, k_tops, sems = refs[span:]
     rows = q_ref.shape[1]
-    gather_keys(meta_ref[0], kv_refs, kv, sems)
+    copies = gather_keys(meta_ref[0], kv_refs, kv, sems, pl.ds(0, KV_HEADS))
+    for e, ref in enumerate(kv_refs):
+        source = ref.at[0, pl.ds(rows, 16), :]
+        copies.append(pltpu.make_async_copy(source, k_tops.at[e], sems.at[span + e]))
+    for copy in copies:
+        copy.start()
+    for copy in copies:
+        copy.wait()
+    split_keys(kv, None, val)
 
     def q_rows(i, g):
         at = pl.ds(pl.multiple_of(i * BQ, BQ), BQ)
         return q_ref[pl.ds(g * GROUP, GROUP), at, :].reshape(STACK, LANES)
 
     def fold(i, g, spots, bias, ceiling):
-        pair = key_pair(kv, g, spots)
-        s = masked(dot_tr(q_rows(i, g), pair), bias)
+        s = dot_tr(q_rows(i, g), key_pair(kv, g, spots))
+        s = s * SCALE2 if bias is None else masked(s, bias)
         if ceiling:
             s = s - top[g, :, 0:1]
-        p = jnp.exp2(s)
-        total[g] += sum(p[:, k * LANES : (k + 1) * LANES] for k in range(2 * BK // LANES))
-        acc[g] += dot(p.astype(BF16), pair)
+        acc[g] += dot(jnp.exp2(s).astype(BF16), key_pair(val, g, spots))
 
     def finish(i, ceiling):
         at = pl.ds(pl.multiple_of(i * BQ, BQ), BQ)
         lane = lane_iota((BQ, LANES))
         logs = jnp.zeros((BQ, LANES), F32)
         for g in range(KV_HEADS):
-            sums = jnp.sum(total[g], axis=1, keepdims=True)
-            out = acc[g] * (1.0 / sums)
+            sums = acc[g]
             lse = jnp.log2(sums)
             if ceiling:
                 lse = lse + top[g, :, 0:1]
+            out = sums * pltpu.roll(1.0 / sums, HEAD, 1)
             for h in range(GROUP):
-                logs = jnp.where(lane == g * GROUP + h, lse[h * BQ : (h + 1) * BQ], logs)
+                logs = jnp.where(lane == g * GROUP + h, lse[h * BQ : (h + 1) * BQ, 0:1], logs)
             for pair in range(GROUP // 2):
                 first = out[2 * pair * BQ : (2 * pair + 1) * BQ]
                 second = out[(2 * pair + 1) * BQ : (2 * pair + 2) * BQ]
@@ -212,13 +258,14 @@
     def run(ceiling):
         def q_loop(i, _):
             acc[...] = jnp.zeros_like(acc)
-            total[...] = jnp.zeros_like(total)
-            pairs = (meta_ref[1 + i] + 1) // 2
+            count = meta_ref[1 + i]
+            free = open_tiles(meta_ref, i)
             if ceiling:
+                free = free * 0
                 top[...] = jnp.full_like(top, 2 * MASKED)
 
                 def top_loop(t, _):
-                    spots = tile_pair(meta_ref, tiles, i, t)
+                    spots = tile_pair(meta_ref, tiles, i, 2 * t)
                     bias = mask_bias(info_ref, seg_ref, i, spots)
 
                     def top_group(g, _):
@@ -229,10 +276,19 @@
                     lax.fori_loop(0, KV_HEADS, top_group, 0)
                     return 0
 
-                lax.fori_loop(0, pairs, top_loop, 0)
+                lax.fori_loop(0, (count + 1) // 2, top_loop, 0)
+            else:
+
+                def open_loop(t, _):
+                    spots = tile_pair(meta_ref, tiles, i, 2 * t)
+                    for g in range(KV_HEADS):
+                        fold(i, g, spots, None, False)
+                    return 0
+
+                lax.fori_loop(0, free // 2, open_loop, 0)
 
             def k_loop(t, _):
-                spots = tile_pair(meta_ref, tiles, i, t)
+                spots = tile_pair(meta_ref, tiles, i, free + 2 * t)
                 bias = mask_bias(info_ref, seg_ref, i, spots)
                 if ceiling:
 
@@ -246,18 +302,14 @@
                         fold(i, g, spots, bias, False)
                 return 0
 
-            lax.fori_loop(0, pairs, k_loop, 0)
+            lax.fori_loop(0, (count - free + 1) // 2, k_loop, 0)
             finish(i, ceiling)
             return 0
 
         lax.fori_loop(0, rows // BQ, q_loop, 0)
 
-    bound = largest_square(q_ref, rows // BK * BK)
-    if rows % BK:
-        bound = jnp.maximum(bound, largest_square(q_ref.at[:, rows - BK :, :], BK))
-    bound = bound * largest_square(kv, kv.shape[1])
-    limit = (SAFE_EXPONENT / SCALE2) ** 2
-    safe = bound < limit
+    bound = jnp.max(top_ref[...]) * jnp.max(k_tops[...].astype(F32))
+    safe = bound < (SAFE_EXPONENT / SCALE2) ** 2
 
     @pl.when(safe)
     def _():
@@ -268,7 +320,7 @@
         run(True)
 
 
-def attention_forward(meta, q, kvs, info, seg):
+def attention_forward(meta, q, top, kvs, info, seg):
     rows = q.shape[1]
     span = len(kvs)
     keys = span * rows
@@ -279,44 +331,61 @@
             jax.ShapeDtypeStruct((rows, D), BF16),
             jax.ShapeDtypeStruct((rows, LANES), F32),
         ],
-        in_specs=[SMEM_SPACE, VMEM_SPACE] + [ANY_SPACE] * span + [VMEM_SPACE] * 2,
+        in_specs=[SMEM_SPACE] + [VMEM_SPACE] * 2 + [ANY_SPACE] * span + [VMEM_SPACE] * 2,
         out_specs=[VMEM_SPACE] * 2,
         scratch_shapes=[
             pltpu.VMEM((KV_HEADS, keys, LANES), BF16),
+            pltpu.VMEM((KV_HEADS, keys, LANES), BF16),
             pltpu.VMEM((KV_HEADS, STACK, LANES), F32),
             pltpu.VMEM((KV_HEADS, STACK, LANES), F32),
-            pltpu.VMEM((KV_HEADS, STACK, LANES), F32),
-            pltpu.SemaphoreType.DMA((span,)),
+            pltpu.VMEM((span, 16, LANES), BF16),
+            pltpu.SemaphoreType.DMA((2 * span,)),
         ],
         compiler_params=params(52),
         cost_estimate=pl.CostEstimate(
-            flops=20 * 10**9, bytes_accessed=15 * 10**6, transcendentals=3 * 10**7
+            flops=80 * 10**9, bytes_accessed=15 * 10**6, transcendentals=3 * 10**7
         ),
         name="attention_forward",
-    )(meta, q, *kvs, info, seg)
-
-
-def backward_kernel(meta_ref, q_ref, da_ref, att_ref, lse_ref, cos_ref, sin_ref, *refs, tiles, span):
+    )(meta, q, top, *kvs, info, seg)
+
+
+def backward_kernel(
+    meta_ref, q_ref, da_ref, att_ref, lse_ref, cos_ref, sin_ref, *refs, tiles, span, heads
+):
+    first_head, groups = heads
     kv_refs = refs[:span]
-    info_ref, seg_ref, dq_ref, near_ref, far_ref, kv, dkv, dq, qd, stats, sems = refs[span:]
+    info_ref, seg_ref, dq_ref, near_ref, far_ref, key, val, dkv, dq, qd, lifted, sems = refs[span:]
     rows = q_ref.shape[1]
     block = meta_ref[0]
-    gather_keys(block, kv_refs, kv, sems)
+    copies = gather_keys(block, kv_refs, key, sems, pl.ds(first_head, groups))
+    for copy in copies:
+        copy.start()
 
     def clear(n, _):
-        dkv[:, pl.ds(n * BK, BK), :] = jnp.zeros((KV_HEADS, BK, LANES), F32)
+        dkv[:, pl.ds(n * BK, BK), :] = jnp.zeros((groups, BK, LANES), F32)
         return 0
 
-    lax.fori_loop(0, kv.shape[1] // BK, clear, 0)
+    lax.fori_loop(0, key.shape[1] // BK, clear, 0)
+    for copy in copies:
+        copy.wait()
+    split_keys(key, key, val)
     lane = lane_iota((BQ, LANES))
     left = lane < HEAD
+
+    def lanes_of(column, first):
+        out = jnp.zeros((BQ, LANES), F32)
+        for k in range(3):
+            top = column.astype(BF16).astype(F32)
+            out = jnp.where(lane == first + k, top, out)
+            column = column - top
+        return out
 
     def q_loop(i, _):
         at = pl.ds(pl.multiple_of(i * BQ, BQ), BQ)
         dq[...] = jnp.zeros_like(dq)
-        logs = lse_ref[at, :]
-        for h in range(HEADS):
-            g, r = h // GROUP, h % GROUP
+        logs = lse_ref[at, :] * (-1.0 / SCALE2)
+        for h in range(first_head * GROUP, (first_head + groups) * GROUP):
+            g, r = h // GROUP - first_head, h % GROUP
             column = h // 2 * LANES
             da = da_ref[at, column : column + LANES].astype(F32)
             delta = da * att_ref[at, column : column + LANES].astype(F32)
@@ -324,32 +393,49 @@
             delta = jnp.sum(jnp.where(mine, delta, 0.0), axis=1, keepdims=True)
             if h % 2 == 0:
                 da = pltpu.roll(da, HEAD, 1)
-            da = jnp.where(left, 0.0, da).astype(BF16)
-            qd[g, r * BQ : (r + 1) * BQ, :] = q_ref[h, at, :]
-            qd[g, STACK + r * BQ : STACK + (r + 1) * BQ, :] = da
-            stats[g, r * BQ : (r + 1) * BQ, :] = jnp.where(left, logs[:, h : h + 1], delta)
+            q = q_ref[h, at, :]
+            own = slice(r * BQ, (r + 1) * BQ)
+            other = slice(STACK + r * BQ, STACK + (r + 1) * BQ)
+            qd[g, own, :] = q
+            qd[g, other, :] = jnp.where(left, 0.0, da).astype(BF16)
+            lse = lanes_of(logs[:, h : h + 1], HEAD)
+            lifted[g, own, :] = jnp.where(left, q.astype(F32), lse).astype(BF16)
+            lifted[g, other, :] = jnp.where(left, lanes_of(-delta, 0), da).astype(BF16)
+
+        def fold(g, spots, bias):
+            keys = key_pair(key, g, spots)
+            s = dot_tr(lifted[g, :STACK, :], keys)
+            p = jnp.exp2(s * SCALE2 if bias is None else masked(s, bias))
+            ds = (p * dot_tr(lifted[g, STACK:, :], key_pair(val, g, spots))).astype(BF16)
+            p = p.astype(BF16)
+            dq[g] += dot(ds, keys)
+            moved = dot_cc(jnp.concatenate([ds, p], axis=0), qd[g])
+            for n, (first, _) in enumerate(spots):
+                dkv[g, pl.ds(first, BK), :] += moved[n * BK : (n + 1) * BK]
+
+        count = meta_ref[1 + i]
+        free = open_tiles(meta_ref, i)
+
+        def open_loop(t, _):
+            spots = tile_pair(meta_ref, tiles, i, 2 * t)
+            for g in range(groups):
+                fold(g, spots, None)
+            return 0
+
+        lax.fori_loop(0, free // 2, open_loop, 0)
 
         def k_loop(t, _):
-            spots = tile_pair(meta_ref, tiles, i, t)
+            spots = tile_pair(meta_ref, tiles, i, free + 2 * t)
             bias = mask_bias(info_ref, seg_ref, i, spots)
-            for g in range(KV_HEADS):
-                pair = key_pair(kv, g, spots)
-                both = qd[g]
-                sd = dot_tr(both, pair)
-                p = jnp.exp2(masked(sd[:STACK], bias) - stats[g, :, 0:1])
-                ds = (p * (sd[STACK:] - stats[g, :, HEAD : HEAD + 1])).astype(BF16)
-                p = p.astype(BF16)
-                dq[g] += dot(ds, pair)
-                moved = dot_cc(jnp.concatenate([ds, p], axis=0), both)
-                for n, (first, _) in enumerate(spots):
-                    dkv[g, pl.ds(first, BK), :] += moved[n * BK : (n + 1) * BK]
+            for g in range(groups):
+                fold(g, spots, bias)
             return 0
 
-        lax.fori_loop(0, (meta_ref[1 + i] + 1) // 2, k_loop, 0)
+        lax.fori_loop(0, (count - free + 1) // 2, k_loop, 0)
         cos = cos_ref[at, :]
         sin = sin_ref[at, :]
         low = (lane % HEAD) < HEAD // 2
-        for g in range(KV_HEADS):
+        for g in range(groups):
             for pair in range(GROUP // 2):
                 first = dq[g, 2 * pair * BQ : (2 * pair + 1) * BQ]
                 second = dq[g, (2 * pair + 1) * BQ : (2 * pair + 2) * BQ]
@@ -368,44 +454,50 @@
         def leave(n, _):
             at = pl.ds(pl.multiple_of(n * BQ, BQ), BQ)
             source = pl.ds(pl.multiple_of(first + n * BQ, BQ), BQ)
-            for g in range(KV_HEADS):
+            for g in range(groups):
                 target[e // 2, g, at, :] = (dkv[g, source, :] * factor).astype(BF16)
             return 0
 
         lax.fori_loop(0, rows // BQ, leave, 0)
 
 
-def attention_backward(meta, q, da, att, lse, cos, sin, kvs, info, seg):
+def attention_backward(heads, meta, q, da, att, lse, cos, sin, kvs, info, seg):
     rows = q.shape[1]
     span = len(kvs)
     keys = span * rows
     tiles = keys // BK
+    groups = heads[1]
+    work = 36 * 10**9 * groups
     return pl.pallas_call(
-        functools.partial(backward_kernel, tiles=tiles, span=span),
+        functools.partial(backward_kernel, tiles=tiles, span=span, heads=heads),
         out_shape=[
-            jax.ShapeDtypeStruct((rows, D), BF16),
-            jax.ShapeDtypeStruct((span // 2, KV_HEADS, rows, LANES), BF16),
-            jax.ShapeDtypeStruct((span // 2, KV_HEADS, rows, LANES), BF16),
+            jax.ShapeDtypeStruct((rows, groups * GROUP * HEAD), BF16),
+            jax.ShapeDtypeStruct((span // 2, groups, rows, LANES), BF16),
+            jax.ShapeDtypeStruct((span // 2, groups, rows, LANES), BF16),
         ],
         in_specs=[SMEM_SPACE] + [VMEM_SPACE] * 6 + [ANY_SPACE] * span + [VMEM_SPACE] * 2,
         out_specs=[VMEM_SPACE] * 3,
         scratch_shapes=[
-            pltpu.VMEM((KV_HEADS, keys, LANES), BF16),
-            pltpu.VMEM((KV_HEADS, keys, LANES), F32),
-            pltpu.VMEM((KV_HEADS, STACK, LANES), F32),
-            pltpu.VMEM((KV_HEADS, 2 * STACK, LANES), BF16),
-            pltpu.VMEM((KV_HEADS, STACK, LANES), F32),
+            pltpu.VMEM((groups, keys, LANES), BF16),
+            pltpu.VMEM((groups, keys, LANES), BF16),
+            pltpu.VMEM((groups, keys, LANES), F32),
+            pltpu.VMEM((groups, STACK, LANES), F32),
+            pltpu.VMEM((groups, 2 * STACK, LANES), BF16),
+            pltpu.VMEM((groups, 2 * STACK, LANES), BF16),
             pltpu.SemaphoreType.DMA((span,)),
         ],
-        compiler_params=params(60),
+        compiler_params=params(56),
         cost_estimate=pl.CostEstimate(
-            flops=60 * 10**9, bytes_accessed=30 * 10**6, transcendentals=3 * 10**7
+            flops=work, bytes_accessed=30 * 10**6, transcendentals=3 * 10**7
         ),
         name="attention_backward",
     )(meta, q, da, att, lse, cos, sin, *kvs, info, seg)
 
 
-def middle_kernel(x_ref, att_ref, w_ref, gain_ref, mid_ref, n_ref):
+def middle_kernel(place_ref, x_ref, att_ref, gain_ref, *refs):
+    piece_refs, (mid_ref, n_ref, w_ref, sems) = refs[:-4], refs[-4:]
+    for copy in assembly(place_ref, piece_refs, w_ref, sems):
+        copy.wait()
     mid_ref[...] = dot_tr(att_ref[...], w_ref[...])
     gain2 = gain_ref[1:2, :]
 
@@ -420,17 +512,22 @@
     lax.fori_loop(0, mid_ref.shape[0] // BQ, norm, 0)
 
 
-def middle(x, att, w, gains):
+def middle(x, att, gains, pieces, place):
     rows = x.shape[0]
+    count = sum(p.shape[0] for p in pieces)
     return pl.pallas_call(
         middle_kernel,
         out_shape=[
             jax.ShapeDtypeStruct((rows, D), F32),
             jax.ShapeDtypeStruct((rows, D), BF16),
+            jax.ShapeDtypeStruct((D, D), BF16),
         ],
+        in_specs=[SMEM_SPACE] + [VMEM_SPACE] * 3 + [ANY_SPACE] * len(pieces),
+        out_specs=[VMEM_SPACE] * 3,
+        scratch_shapes=[pltpu.SemaphoreType.DMA((count,))],
         compiler_params=params(32),
         name="middle",
-    )(x, att, w, gains)
+    )(place, x, att, gains, *pieces)
 
 
 def feed_forward_kernel(
@@ -565,66 +662,110 @@
     )(mid, own, got, og, gains, w, att)
 
 
-def finish_kernel(
-    x_ref, n_ref, gm_ref, dq_ref, k0_ref, k1_ref, k2_ref, k3_ref, k4_ref, w_ref, gain_ref,
-    dgain_ref, cos_ref, sin_ref, in_ref, dw_ref, dz, dn,
+def query_grad_kernel(n_ref, dq_ref, dw_ref):
+    dw_ref[...] = dot_cc(n_ref[...], dq_ref[...]).astype(BF16)
+
+
+def query_grad(n, dq):
+    return pl.pallas_call(
+        query_grad_kernel,
+        out_shape=jax.ShapeDtypeStruct((D, dq.shape[1]), BF16),
+        compiler_params=params(32),
+        cost_estimate=pl.CostEstimate(
+            flops=4 * 10**9, bytes_accessed=10**7, transcendentals=0
+        ),
+        name="query_grad",
+    )(n, dq)
+
+
+def project_back_kernel(
+    x_ref, n_ref, dqa_ref, dqb_ref, ka_refs, kb_refs, w_ref, dgain_ref,
+    cos_ref, sin_ref, dn_ref, dw_ref, dz,
 ):
     rows = x_ref.shape[0]
     lane = lane_iota((BQ, LANES))
     low = (lane % HEAD) < HEAD // 2
     left = lane < HEAD
+    first = dqa_ref.shape[1] // (GROUP * HEAD)
 
     def turn_back(i, _):
         at = pl.ds(pl.multiple_of(i * BQ, BQ), BQ)
         cos = cos_ref[at, :]
         sin = sin_ref[at, :]
         for g in range(KV_HEADS):
-            z = sum(
-                ref[g, at, :].astype(F32) for ref in (k0_ref, k1_ref, k2_ref, k3_ref, k4_ref)
-            )
+            refs, k, dq_ref = (ka_refs, g, dqa_ref) if g < first else (kb_refs, g - first, dqb_ref)
+            z = sum(ref[k, at, :].astype(F32) for ref in refs)
             rot = z * cos - half_turn(z, low) * sin
             base = g * GROUP_COLS
             span = GROUP * HEAD
-            dz[at, base : base + span] = dq_ref[at, g * span : (g + 1) * span]
+            dz[at, base : base + span] = dq_ref[at, k * span : (k + 1) * span]
             dz[at, base + span : base + span + LANES] = jnp.where(left, rot, z).astype(BF16)
         return 0
 
     lax.fori_loop(0, rows // BQ, turn_back, 0)
-    dw_ref[:, :QKV] = dot_cc(n_ref[...], dz[...]).astype(BF16)
-    dn[...] = dot_tr(dz[...], w_ref[:, :QKV])
-    gain1 = gain_ref[0:1, :]
+    kv_cols = [dz[:, g * GROUP_COLS + GROUP * HEAD : (g + 1) * GROUP_COLS] for g in range(KV_HEADS)]
+    dw_ref[:, : KV_HEADS * LANES] = dot_cc(
+        n_ref[...], jnp.concatenate(kv_cols, axis=1)
+    ).astype(BF16)
+    dn_ref[...] = dot_tr(dz[...], w_ref[:, :QKV])
 
     def step(i, dgain):
         at = pl.ds(pl.multiple_of(i * BQ, BQ), BQ)
         x = x_ref[at, :].astype(F32)
-        grad = dn[at, :]
         scale = lax.rsqrt(jnp.mean(x * x, axis=1, keepdims=True) + EPSILON)
-        dgain = dgain + jnp.sum((grad * x * scale).reshape(BQ // 8, 8, D), axis=0)
-        q1 = grad * gain1
-        mean = jnp.mean(q1 * x, axis=1, keepdims=True)
-        in_ref[at, :] = gm_ref[at, :] + scale * q1 - x * (scale * scale * scale * mean)
-        return dgain
+        return dgain + jnp.sum((dn_ref[at, :] * x * scale).reshape(BQ // 8, 8, D), axis=0)
 
     dgain1 = lax.fori_loop(0, rows // BQ, step, jnp.zeros((8, D), F32))
     dgain1 = jnp.sum(dgain1, axis=0, keepdims=True)
     dgain2 = jnp.sum(dgain_ref[...], axis=0, keepdims=True)
     row = lax.broadcasted_iota(jnp.int32, (LANES, D), 0)
     both = jnp.where(row == 0, dgain1, jnp.where(row == 1, dgain2, 0.0))
-    dw_ref[:, QKV:] = both.T.astype(BF16)
-
-
-def finish(x, n, gm, dq, pieces, w, gains, dgain, cos, sin):
+    dw_ref[:, KV_HEADS * LANES :] = both.T.astype(BF16)
+
+
+def project_back(x, n, dqs, pieces, w, dgain, cos, sin):
     rows = x.shape[0]
+
+    def kernel(x_ref, n_ref, dqa_ref, dqb_ref, *refs):
+        count = len(pieces[0])
+        return project_back_kernel(
+            x_ref, n_ref, dqa_ref, dqb_ref, refs[:count], refs[count : 2 * count],
+            *refs[2 * count :],
+        )
+
     return pl.pallas_call(
-        finish_kernel,
+        kernel,
         out_shape=[
             jax.ShapeDtypeStruct((rows, D), F32),
-            jax.ShapeDtypeStruct((D, QKV_PAD), BF16),
+            jax.ShapeDtypeStruct((D, (KV_HEADS + 1) * LANES), BF16),
         ],
-        scratch_shapes=[pltpu.VMEM((rows, QKV), BF16), pltpu.VMEM((rows, D), F32)],
-        compiler_params=params(60),
-        name="finish",
-    )(x, n, gm, dq, *pieces, w, gains, dgain, cos, sin)
+        scratch_shapes=[pltpu.VMEM((rows, QKV), BF16)],
+        compiler_params=params(48),
+        name="project_back",
+    )(x, n, *dqs, *pieces[0], *pieces[1], w, dgain, cos, sin)
+
+
+def input_grad_kernel(x_ref, gm_ref, dn_ref, gain_ref, in_ref):
+    x = x_ref[...].astype(F32)
+    scale = lax.rsqrt(jnp.mean(x * x, axis=1, keepdims=True) + EPSILON)
+    q1 = dn_ref[...] * gain_ref[0:1, :]
+    mean = jnp.mean(q1 * x, axis=1, keepdims=True)
+    in_ref[...] = gm_ref[...] + scale * q1 - x * (scale * scale * scale * mean)
+
+
+def input_gradient(x, gm, dn, gains):
+    rows = x.shape[0]
+    block = pl.BlockSpec((BQ, D), lambda i: (i, 0))
+    return pl.pallas_call(
+        input_grad_kernel,
+        grid=(rows // BQ,),
+        in_specs=[block] * 3 + [pl.BlockSpec((8, D), lambda i: (0, 0))],
+        out_specs=block,
+        out_shape=jax.ShapeDtypeStruct((rows, D), F32),
+        compiler_params=params(32),
+        cost_estimate=pl.CostEstimate(flops=10**7, bytes_accessed=10**7, transcendentals=0),
+        name="input_gradient",
+    )(x, gm, dn, gains)
 
 
 def body(
@@ -645,25 +786,72 @@
 
     same_core = [list(range(c, size, 2)) for c in range(2)]
 
+    trees = size // span
+    chips = span // 2
+    chip = block // 2
+
+    def stage(*values):
+        return lax.optimization_barrier(values)
+
+    def half_columns(*weights):
+        halves = [
+            jnp.concatenate([w[:, c * w.shape[1] // 2 :][:, : w.shape[1] // 2] for w in weights], axis=1)
+            for c in range(2)
+        ]
+        keep = jnp.where(core == 0, halves[0], halves[1])
+        got = swap(jnp.where(core == 0, halves[1], halves[0]), 1)
+        return jnp.where(
+            core == 0, jnp.concatenate([keep, got], axis=0), jnp.concatenate([got, keep], axis=0)
+        )
+
+    def part(v, index, axis):
+        return lax.dynamic_index_in_dim(v, index, axis, keepdims=False)
+
+    def send_cores(grad):
+        grad = grad.reshape(trees, chips, 2, shard, grad.shape[1])
+        return part(grad, core, 2), swap(part(grad, 1 - core, 2), 1)
+
+    def send_chips(total):
+        return part(total, chip, 1), *(swap(part(total, chip ^ c, 1), 2 * c) for c in range(1, chips))
+
+    def send_trees(total):
+        if trees > 4:
+            across = [list(range(k, size, span)) for k in range(span)]
+            total = lax.psum_scatter(total, "fsdp", axis_index_groups=across)
+            return (total.reshape(total.shape[-2:]),)
+        return part(total, tree, 0), *(
+            swap(part(total, tree ^ t, 0), span * t) for t in range(1, trees)
+        )
+
+    def add(terms):
+        return sum((t.astype(F32) for t in terms[1:]), terms[0].astype(F32))
+
+    def add16(terms):
+        return add(terms).astype(BF16)
+
+    turned = w_output.T
     grouped = [w_query.reshape(shard, KV_HEADS, GROUP * HEAD)]
     grouped += [w.reshape(shard, KV_HEADS, HEAD) for w in (w_key, w_value)]
     grouped = jnp.concatenate(grouped, axis=2).reshape(shard, QKV)
     gain_pair = jnp.stack([norm_gain1, norm_gain2], axis=1)
     gain_pair = jnp.pad(gain_pair, ((0, 0), (0, LANES - 2)))
-    qkv_w = lax.all_gather(
-        jnp.concatenate([grouped, gain_pair], axis=1), "fsdp", axis=0, tiled=True
+    grouped = jnp.concatenate([grouped, gain_pair], axis=1)
+    chip_rows = half_columns(grouped, w_gate, w_up, w_down.T, turned)
+    ff_w = lax.all_gather(
+        chip_rows[:, QKV_PAD // 2 :], "fsdp", tiled=True, axis_index_groups=same_core
     )
-    out_w = lax.all_gather(w_output.T, "fsdp", axis=0, tiled=True)
-    sides = [
-        jnp.concatenate([w[:, c * HALF : (c + 1) * HALF] for w in (w_gate, w_up, w_down.T)], axis=1)
-        for c in range(2)
-    ]
-    keep = jnp.where(core == 0, sides[0], sides[1])
-    got = swap(jnp.where(core == 0, sides[1], sides[0]), 1)
-    ordered = jnp.where(
-        core == 0, jnp.concatenate([keep, got], axis=0), jnp.concatenate([got, keep], axis=0)
-    )
-    ff_w = lax.all_gather(ordered, "fsdp", axis=0, tiled=True, axis_index_groups=same_core)
+    qkv_rows = chip_rows[:, : QKV_PAD // 2]
+    if trees > 4:
+        qkv_rows = lax.all_gather(qkv_rows, "fsdp", tiled=True, axis_index_groups=same_core)[None]
+        qkv_pieces, order = [qkv_rows], jnp.zeros((1,), jnp.int32)
+    else:
+        qkv_rows = jnp.stack([qkv_rows] + [swap(qkv_rows, span * t) for t in range(1, trees)])
+        qkv_pieces = [qkv_rows] + [swap(qkv_rows, 2 * c) for c in range(1, chips)]
+        order = [(tree ^ t) * chips + (chip ^ c) for c in range(chips) for t in range(trees)]
+        order = jnp.stack(order)
+    qkv_place = jnp.stack([core] * len(qkv_pieces) + [1 - core] * len(qkv_pieces))
+    qkv_place = jnp.concatenate([qkv_place, order, order])
+    qkv_pieces = qkv_pieces + [swap(p, 1) for p in qkv_pieces]
 
     tree_seg = segment_ids
     bit = 1
@@ -715,22 +903,33 @@
     active = active & (tile_range[None, :] * BK <= last_row[:, None])
     before = tile_range[:, None] < tile_range[None, :]
     place = jnp.sum((active[:, :, None] & before[None]).astype(jnp.int32), axis=1)
+    barred = (ids[None, :] != ids[:, None]) & (ids[None, :] != parent[:, None])
+    barred = barred & (ids[None, :] != grand[:, None])
+    tile_has = (tile_first[:, None] <= ids[None, :]) & (ids[None, :] <= tile_last[:, None])
+    barred = jnp.any(barred[:, None, :] & tile_has[None, :, :], axis=2)
+    barred = jnp.any(here[:, :, None] & barred[None, :, :], axis=1)
+    whole = active & ~barred & ((tile_range[None, :] + 1) * BK <= last_row[:, None] - BQ + 1)
+    whole_count = jnp.sum(whole.astype(jnp.int32), axis=1)
+    rank = jnp.sum((whole[:, :, None] & before[None]).astype(jnp.int32), axis=1)
+    place = jnp.where(whole, rank, whole_count[:, None] + place - rank)
     chosen = active[:, :, None] & (place[:, :, None] == tile_range[None, None, :])
     listed = jnp.sum(jnp.where(chosen, tile_range[None, :, None], 0), axis=1)
     counts = jnp.sum(active.astype(jnp.int32), axis=1)
-    meta = jnp.concatenate(
-        [block[None], jnp.pad(counts, (0, BQ - steps)), listed.reshape(steps * tiles)]
-    )
+    counts = [jnp.pad(v, (0, BQ // 2 - steps)) for v in (counts, whole_count)]
+    meta = jnp.concatenate([block[None], *counts, listed.reshape(steps * tiles)])
     seg_row = tree_seg[None, :]
 
     og_far = swap(out_grad, 1)
-    normed1, q, kv, gains = project(layer_in, qkv_w, cos, sin)
+    normed1, q, kv, gains, qkv_w, q_top = project(qkv_place, layer_in, cos, sin, qkv_pieces)
     kvs = [kv, swap(kv, 1)]
-    for chip in range(1, span // 2):
-        piece = swap(kv, 2 * chip)
+    for c in range(1, chips):
+        piece = swap(kv, 2 * c)
         kvs += [piece, swap(piece, 1)]
-    att, lse = attention_forward(meta, q, kvs, info, seg_row)
-    mid, normed2 = middle(layer_in, att, out_w, gains)
+    att, lse = attention_forward(meta, q, q_top, kvs, info, seg_row)
+    att, ff_w = stage(att, ff_w)
+    out_w = ff_w[None, :, 3 * HALF :]
+    out_place = jnp.stack([core, 1 - core, 0, 0])
+    mid, normed2, out_w = middle(layer_in, att, gains, [out_w, swap(out_w, 1)], out_place)
     own, far, ff_dw = feed_forward(normed2, swap(normed2, 1), out_grad, og_far, ff_w)
     layer_out, grad_mid, da, out_dw, dgain2 = turn(
         mid, own, swap(far, 1), out_grad, gains, out_w, att
@@ -738,36 +937,65 @@
     ff_dw = lax.psum_scatter(
         ff_dw, "fsdp", scatter_dimension=0, tiled=True, axis_index_groups=same_core
     )
-    out_dw = lax.psum_scatter(out_dw, "fsdp", scatter_dimension=0, tiled=True)
-    dq, near, far = attention_backward(meta, q, da, att, lse, cos, sin, kvs, info, seg_row)
-    got = swap(far, 1)
-    pieces = [near[0], got[0]]
-    for chip in range(1, span // 2):
-        both = (near[chip].astype(F32) + got[chip].astype(F32)).astype(BF16)
-        pieces.append(swap(both, 2 * chip))
-    input_grad, qkv_dw = finish(
-        layer_in, normed1, grad_mid, dq, pieces, qkv_w, gains, dgain2, cos, sin
+
+    def backward(n, meta):
+        return attention_backward(
+            HEAD_PARTS[n], meta, q, da, att, lse, cos, sin, kvs, info, seg_row
+        )
+
+    def meet(near, far):
+        got = swap(far, 1)
+        return [near[0], got[0]], [add16((near[c], got[c])) for c in range(1, chips)]
+
+    dq_a, near, far = backward(0, meta)
+    pieces_a, both = meet(near, far)
+    query_a = query_grad(normed1, dq_a)
+    meta_b, early, *both = stage(meta, jnp.concatenate([out_dw, query_a], axis=1), *both)
+    both = [swap(v, 2 * c + 2) for c, v in enumerate(both)]
+    early = send_cores(early)
+    dq_b, near, far = backward(1, meta_b)
+    near, far, dq_b, *values = stage(near, far, dq_b, *both, *early)
+    pieces_a += values[: len(both)]
+    early = add16(values[len(both) :])
+    pieces_b, both = meet(near, far)
+    query_b = query_grad(normed1, dq_b)
+    early, query_b, *both = stage(early, query_b, *both)
+    pieces_b += [swap(v, 2 * c + 2) for c, v in enumerate(both)]
+    early = send_chips(early)
+    dn, kv_dw = project_back(
+        layer_in, normed1, (dq_a, dq_b), (pieces_a, pieces_b), qkv_w, dgain2, cos, sin
     )
-    qkv_dw = lax.psum_scatter(qkv_dw, "fsdp", scatter_dimension=0, tiled=True).astype(F32)
-
-    groups = qkv_dw[:, :QKV].reshape(shard, KV_HEADS, GROUP_COLS)
-    grad_query = groups[:, :, : GROUP * HEAD].reshape(shard, HEADS * HEAD)
-    grad_key = groups[:, :, GROUP * HEAD : GROUP * HEAD + HEAD].reshape(shard, KV_HEADS * HEAD)
-    grad_value = groups[:, :, GROUP * HEAD + HEAD :].reshape(shard, KV_HEADS * HEAD)
-    mine = jnp.where(core == 0, ff_dw[:shard], ff_dw[shard:])
-    got = swap(jnp.where(core == 0, ff_dw[shard:], ff_dw[:shard]), 1)
-    low = jnp.where(core == 0, mine, got).astype(F32).reshape(shard, 3, HALF)
-    high = jnp.where(core == 0, got, mine).astype(F32).reshape(shard, 3, HALF)
-    ff_grads = jnp.concatenate([low, high], axis=2)
+    late = jnp.concatenate([kv_dw, query_b], axis=1)
+    late, dn, *early = stage(late, dn, *early)
+    early, late = send_trees(add16(early)), send_cores(late)
+    input_grad = input_gradient(layer_in, grad_mid, dn, gains)
+    early, late = add(early), add16(late)
+    late = add(send_trees(add16(send_chips(late))))
+    out_dw, kv_dw = early[:, :D], late[:, : (KV_HEADS + 1) * LANES]
+    query_dw = jnp.concatenate([early[:, D:], late[:, (KV_HEADS + 1) * LANES :]], axis=1)
+
+    groups = kv_dw[:, : KV_HEADS * LANES].reshape(shard, KV_HEADS, LANES)
+    grad_key = groups[:, :, :HEAD].reshape(shard, KV_HEADS * HEAD)
+    grad_value = groups[:, :, HEAD:].reshape(shard, KV_HEADS * HEAD)
+
+    def join(grad):
+        mine, other = grad[:shard], grad[shard:]
+        keep = jnp.where(core == 0, mine, other)
+        got = swap(jnp.where(core == 0, other, mine), 1)
+        low = jnp.where(core == 0, keep, got).astype(F32).reshape(shard, -1, HALF)
+        high = jnp.where(core == 0, got, keep).astype(F32).reshape(shard, -1, HALF)
+        return jnp.concatenate([low, high], axis=2)
+
+    ff_grads = join(ff_dw)
     return (
         layer_out,
         input_grad,
-        qkv_dw[:, QKV],
-        grad_query,
+        kv_dw[:, KV_HEADS * LANES],
+        query_dw,
         grad_key,
         grad_value,
-        out_dw.astype(F32).T,
-        qkv_dw[:, QKV + 1],
+        out_dw.T,
+        kv_dw[:, KV_HEADS * LANES + 1],
         ff_grads[:, 0],
         ff_grads[:, 1],
         ff_grads[:, 2].T,

time: 943 us -> 695 us (0.74)
  waiting for transfers between devices: 544 us -> 245 us
  starting transfers between devices: 129 us -> 161 us
  local copies, waits for them, and re-layouts: 24.6 us -> 38.7 us
    reduce_scatter x2 -> x0, waiting for transfers between devices: 267 us -> none  [the longest x1 139 us: body(): lax.psum_scatter(qkv_dw, 'fsdp', scatter_dimension=0, tiled=True)]
    all_gather x3 -> x1, waiting for transfers between devices: 179 us -> 82 us  [body(): lax.all_gather(chip_rows[:, QKV_PAD // 2:], 'fsdp', tiled=True, axis_inde...]
    ppermute x19 -> x48, waiting for transfers between devices: 97.7 us -> 163 us  [swap(): return lax.ppermute(v, 'fsdp', [(i, i ^ bit) for i in range(size)])]
    ppermute x19 -> x48, starting transfers between devices: 129 us -> 160 us  [swap(): return lax.ppermute(v, 'fsdp', [(i, i ^ bit) for i in range(size)])]
    pallas_call x1, Pallas kernels: 39.1 us -> 21.4 us  [attention_forward(): pl.pallas_call(functools.partial(forward_kernel, tiles=tiles, span=span),...]
    pallas_call x2 -> x6, Pallas kernels: 67.6 us -> 76.7 us  [the longest x2 56.6 us: attention_backward(): pl.pallas_call(functools.partial(backward_kernel, tiles=tiles, span=span,...]
    unnamed x65 -> x103, local copies, waits for them, and re-layouts: 14.6 us -> 20.1 us
  transfers between devices with their start and end apart: 25 -> 50, of which waited for: 18 -> 30; matrix products, arithmetic and copies ran while one was open for 2% -> 4% of each run, Pallas kernels for 15% -> 19%
where the time goes in v2:
time: 695 us; the launch traced here: 685 us
  waiting for transfers between devices  245 us (35%)
  Pallas kernels  205 us (29%)
  starting transfers between devices  161 us (23%)
  local copies, waits for them, and re-layouts  38.7 us (6%)
  other arithmetic  21.1 us (3%)
  between operations  15.5 us (2%)
    ppermute x48, waiting for transfers between devices, swap(): return lax.ppermute(v, 'fsdp', [(i, i ^ bit) for i in range(size)])  163 us
    ppermute x48, starting transfers between devices, swap(): return lax.ppermute(v, 'fsdp', [(i, i ^ bit) for i in range(size)])  160 us
    all_gather x1, waiting for transfers between devices, body(): lax.all_gather(chip_rows[:, QKV_PAD // 2:], 'fsdp', tiled=True, axis_inde...  82 us
    pallas_call x1, Pallas kernels, feed_forward(): pl.pallas_call(feed_forward_kernel, grid=(steps, 3), in_specs=[whole] * 4...  73 us
    pallas_call x2, Pallas kernels, attention_backward(): pl.pallas_call(functools.partial(backward_kernel, tiles=tiles, span=span,...  56.6 us
    pallas_call x1, Pallas kernels, attention_forward(): pl.pallas_call(functools.partial(forward_kernel, tiles=tiles, span=span),...  21.4 us
    unnamed x103, local copies, waits for them, and re-layouts  20.1 us
    pallas_call x1, Pallas kernels, turn(): pl.pallas_call(turn_kernel, out_shape=[jax.ShapeDtypeStruct((rows, D), BF...  16.3 us
  transfers between devices with their start and end apart: 50, of which 30 were waited for; matrix products, arithmetic and copies ran while one was open for 4% of the time, Pallas kernels for 19%

profile of v2, /device:TPU:0, one launch (start us, length us, event | category | flops | bytes accessed | tf_op | source)
XLA Modules:
  0.0 685.3 jit_solution(17393635020104744282)
XLA Ops:
  29.5 12.7 %collective-permute-done.5 = bf16[80,1024]{1,0:T(8,128)(2,1)S(1)} collective-permute-done((bf16[80,1024]{1,0:T(8,128)(2,1)S(1)}, bf16[80,1024]{1,0:T(8,128)(2,1)S(1)}, u32[]{:S(2)}, u32[]{:S(2)}) %collective-permute-start.5) | collective-permute-done | bytes 163872 | tf_op jit(solution)/shard_map/ppermute | solution.py:785
  42.3 5.8 collective-permute-done.6
  52.2 14.1 %collective-permute-done.9.refs_3_ = bf16[4,80,1024]{2,1,0:T(8,128)(2,1)S(1)} collective-permute-done((bf16[4,80,1024]{2,1,0:T(8,128)(2,1)S(1)}, bf16[4,80,1024]{2,1,0:T(8,128)(2,1)S(1)}, u32[]{:S(2)}, u32[]{:S(2)}) %collective-permute-start.9) | collective-permute-done | bytes 655392 | tf_op jit(solution)/shard_map/ppermute | solution.py:785
  66.2 11.1 %collective-permute-done.8.refs_2_ = bf16[4,80,1024]{2,1,0:T(8,128)(2,1)S(1)} collective-permute-done((bf16[4,80,1024]{2,1,0:T(8,128)(2,1)S(1)}, bf16[4,80,1024]{2,1,0:T(8,128)(2,1)S(1)}, u32[]{:S(2)}, u32[]{:S(2)}) %collective-permute-start.8) | collective-permute-done | bytes 655392 | tf_op jit(solution)/shard_map/ppermute | solution.py:785
  81.4 13.1 %project.1 = (bf16[640,1280]{1,0:T(8,128)(2,1)}, bf16[20,640,128]{2,1,0:T(8,128)(2,1)}, bf16[5,656,128]{2,1,0:T(8,128)(2,1)}, f32[8,1280]{1,0:T(8,128)S(1)}, bf1...) custom-call(s32[40]{0:T(128)S(1)} %concatenate.76.place_ref, bf16[640,1280]{1,0:T(8,128)(2,1)} %x_ref.7, ...), custom_call_target="tpu_custom_call" | custom-call | tf_op jit(solution)/shard_map/project/pallas_call | solution.py:136
  99.3 19.6 %collective-permute-done.19.refs_6_ = bf16[5,656,128]{2,1,0:T(8,128)(2,1)S(1)} collective-permute-done((bf16[5,656,128]{2,1,0:T(8,128)(2,1)}, bf16[5,656,128]{2,1,0:T(8,128)(2,1)S(1)}, u32[]{:S(2)}, u32[]{:S(2)}) %collective-permute-start.19) | collective-permute-done | bytes 839712 | tf_op jit(solution)/shard_map/ppermute | solution.py:785
  118.9 16.2 %collective-permute-done.17.refs_4_ = bf16[5,656,128]{2,1,0:T(8,128)(2,1)S(1)} collective-permute-done((bf16[5,656,128]{2,1,0:T(8,128)(2,1)}, bf16[5,656,128]{2,1,0:T(8,128)(2,1)S(1)}, u32[]{:S(2)}, u32[]{:S(2)}) %collective-permute-start.17) | collective-permute-done | bytes 839712 | tf_op jit(solution)/shard_map/ppermute | solution.py:785
  140.9 21.4 %attention_forward.1 = (bf16[640,1280]{1,0:T(8,128)(2,1)}, f32[640,128]{1,0:T(8,128)S(1)}) custom-call(s32[229]{0:T(256)S(1)} %fusion.27.meta_ref, bf16[20,640,128]{2,1,0:T(8,128)(2,1)} %get-tuple-element.64.q_ref, f32[8,128]{1,0:T(8,128)S(1)} %get-tuple-element.65.top_ref, bf16[5,656,128]{2,1,0:T(8,128)(2,1)S(1)} %copy-done.22, ...), custom_call_target="tpu_custom_call" | custom-call | flops 80000000000 | bytes 15000000 | tf_op jit(solution)/shard_map/attention_forward/pallas_call | solution.py:328
  163.8 82.0 %all-gather.2.cloned.1.call-done.wg_ref.wu_ref.wd_ref = bf16[1280,6016]{1,0:T(8,128)(2,1)} async-done(((bf16[80,6016]{1,0:T(8,128)(2,1)}), bf16[1280,6016]{1,0:T(8,128)(2,1)}) %all-gather.2.cloned.1.call-update) | async-done | bytes 15400976 | tf_op jit(solution)/shard_map/all_gather | solution.py:840
  266.0 73.0 %feed_forward.1 = (bf16[2,640,1280]{2,1,0:T(8,128)(2,1)}, bf16[2,640,1280]{2,1,0:T(8,128)(2,1)}, bf16[1280,5376]{1,0:T(8,128)(2,1)}) custom-call(bf16[640,1280]{1,0:T(8,128)(2,1)} %copy-done.21, bf16[640,1280]{1,0:T(8,128)(2,1)} %copy-done.40, bf16[640,1280]{1,0:T(8,128)(2,1)} %og_ref.1, bf16[640,1280]{1,0:T(8,128)(2,1)} %collective-permute-done.23.og2_ref, ...), custom_call_target="tpu_custom_call" | custom-call | flops 51999997952 | bytes 40000000 | tf_op jit(solution)/shard_map/feed_forward/pallas_call | solution.py:592
  339.2 5.9 collective-permute-done.24.got_ref
  346.9 16.3 %turn.1 = (bf16[640,1280]{1,0:T(8,128)(2,1)}, f32[640,1280]{1,0:T(8,128)}, bf16[640,1280]{1,0:T(8,128)(2,1)}, bf16[1280,1280]{1,0:T(8,128)(2,1)}, f32[8,1280]{1,0:T(8,128)}) custom-call(f32[640,1280]{1,0:T(8,128)} %copy-done.3, bf16[2,640,1280]{2,1,0:T(8,128)(2,1)} %get-tuple-element.73.own_ref, bf16[2,640,1280]{2,1,0:T(8,128)(2,1)} %copy-done.26, ...), custom_call_target="tpu_custom_call" | custom-call | tf_op jit(solution)/shard_map/turn/pallas_call | solution.py:650
  363.2 32.6 %attention_backward.2 = (bf16[640,768]{1,0:T(8,128)(2,1)}, bf16[4,3,640,128]{3,2,1,0:T(8,128)(2,1)}, bf16[4,3,640,128]{3,2,1,0:T(8,128)(2,1)}) custom-call(s32[229]{0:T(256)} %copy-done.20, bf16[20,640,128]{2,1,0:T(8,128)(2,1)} %get-tuple-element.64.q_ref, bf16[640,1280]{1,0:T(8,128)(2,1)} %get-tuple-element.79.da_ref, ...), custom_call_target="tpu_custom_call" | custom-call | flops 108000002048 | bytes 30000000 | tf_op jit(solution)/shard_map/attention_backward/pallas_call | solution.py:471
  395.8 13.7 %collective-permute-start.25 = (bf16[4,3,640,128]{3,2,1,0:T(8,128)(2,1)}, bf16[4,3,640,128]{3,2,1,0:T(8,128)(2,1)}, u32[]{:S(2)}, u32[]{:S(2)}) collective-permute-start(bf16[4,3,640,128]{3,2,1,0:T(8,128)(2,1)} %get-tuple-element.84), channel_id=1, source_target_pairs={{0,1},{1,0},{2,3},{3,2},{4,5},{5,4},{6,7},{7,6},{8,9},{9,8},{10,11... | collective-permute-start | bytes 5898248 | tf_op jit(solution)/shard_map/ppermute | solution.py:785
  416.9 28.5 %collective-permute-start.26 = (bf16[3,640,128]{2,1,0:T(8,128)(2,1)S(1)}, bf16[3,640,128]{2,1,0:T(8,128)(2,1)S(1)}, u32[]{:S(2)}, u32[]{:S(2)}) collective-permute-start(bf16[3,640,128]{2,1,0:T(8,128)(2,1)S(1)} %get-tuple-element.89), channel_id=1, source_target_pairs={{0,2},{1,3},{2,0},{3,1},{4,6},{5,7},{6,4},{7,5},{8,10},{9,11},{10,... | collective-permute-start | bytes 1474568 | tf_op jit(solution)/shard_map/ppermute | solution.py:785
  445.5 22.0 %collective-permute-start.27 = (bf16[3,640,128]{2,1,0:T(8,128)(2,1)S(1)}, bf16[3,640,128]{2,1,0:T(8,128)(2,1)S(1)}, u32[]{:S(2)}, u32[]{:S(2)}) collective-permute-start(bf16[3,640,128]{2,1,0:T(8,128)(2,1)S(1)} %get-tuple-element.90), channel_id=1, source_target_pairs={{0,4},{1,5},{2,6},{3,7},{4,0},{5,1},{6,2},{7,3},{8,12},{9,13},{10,... | collective-permute-start | bytes 1474568 | tf_op jit(solution)/shard_map/ppermute | solution.py:785
  469.4 24.0 %attention_backward.3 = (bf16[640,512]{1,0:T(8,128)(2,1)}, bf16[4,2,640,128]{3,2,1,0:T(8,128)(2,1)}, bf16[4,2,640,128]{3,2,1,0:T(8,128)(2,1)}) custom-call(s32[229]{0:T(256)} %copy-done.20, bf16[20,640,128]{2,1,0:T(8,128)(2,1)} %get-tuple-element.64.q_ref, bf16[640,1280]{1,0:T(8,128)(2,1)} %get-tuple-element.79.da_ref, ...), custom_call_target="tpu_custom_call" | custom-call | flops 71999995904 | bytes 30000000 | tf_op jit(solution)/shard_map/attention_backward/pallas_call | solution.py:471
  495.3 8.2 %collective-permute-start.30 = (bf16[4,2,640,128]{3,2,1,0:T(8,128)(2,1)}, bf16[4,2,640,128]{3,2,1,0:T(8,128)(2,1)S(1)}, u32[]{:S(2)}, u32[]{:S(2)}) collective-permute-start(bf16[4,2,640,128]{3,2,1,0:T(8,128)(2,1)} %get-tuple-element.98), channel_id=1, source_target_pairs={{0,1},{1,0},{2,3},{3,2},{4,5},{5,4},{6,7},{7,6},{8,9},{9,8},{10,11... | collective-permute-start | bytes 3932168 | tf_op jit(solution)/shard_map/ppermute | solution.py:785
  511.9 19.4 %collective-permute-start.31 = (bf16[2,640,128]{2,1,0:T(8,128)(2,1)S(1)}, bf16[2,640,128]{2,1,0:T(8,128)(2,1)S(1)}, u32[]{:S(2)}, u32[]{:S(2)}) collective-permute-start(bf16[2,640,128]{2,1,0:T(8,128)(2,1)S(1)} %get-tuple-element.101), channel_id=1, source_target_pairs={{0,2},{1,3},{2,0},{3,1},{4,6},{5,7},{6,4},{7,5},{8,10},{9,11},{10,... | collective-permute-start | bytes 983048 | tf_op jit(solution)/shard_map/ppermute | solution.py:785
  531.3 16.1 %collective-permute-start.32 = (bf16[2,640,128]{2,1,0:T(8,128)(2,1)S(1)}, bf16[2,640,128]{2,1,0:T(8,128)(2,1)S(1)}, u32[]{:S(2)}, u32[]{:S(2)}) collective-permute-start(bf16[2,640,128]{2,1,0:T(8,128)(2,1)S(1)} %get-tuple-element.102), channel_id=1, source_target_pairs={{0,4},{1,5},{2,6},{3,7},{4,0},{5,1},{6,2},{7,3},{8,12},{9,13},{10,... | collective-permute-start | bytes 983048 | tf_op jit(solution)/shard_map/ppermute | solution.py:785
  552.1 31.4 %collective-permute-done.32.refs_8_ = bf16[2,640,128]{2,1,0:T(8,128)(2,1)S(1)} collective-permute-done((bf16[2,640,128]{2,1,0:T(8,128)(2,1)S(1)}, bf16[2,640,128]{2,1,0:T(8,128)(2,1)S(1)}, u32[]{:S(2)}, u32[]{:S(2)}) %collective-permute-start.32) | collective-permute-done | bytes 327712 | tf_op jit(solution)/shard_map/ppermute | solution.py:785
  583.6 13.8 %project_back.1 = (f32[640,1280]{1,0:T(8,128)}, bf16[1280,768]{1,0:T(8,128)(2,1)}) custom-call(bf16[640,1280]{1,0:T(8,128)(2,1)} %x_ref.7, bf16[640,1280]{1,0:T(8,128)(2,1)} %get-tuple-element.78.n_ref, bf16[640,768]{1,0:T(8,128)(2,1)} %get-tuple-element.81.dq_ref.dqa_ref, bf16[640,512]{1,0:T(8,128)(2,1)S(1)} %copy-done.14, ...), custom_call_target="tpu_custom_call" | custom-call | tf_op jit(solution)/shard_map/project_back/pallas_call | solution.py:736
  605.2 20.4 %collective-permute-start.44 = (bf16[40,2048]{1,0:T(8,128)(2,1)S(1)}, bf16[40,2048]{1,0:T(8,128)(2,1)S(1)}, u32[]{:S(2)}, u32[]{:S(2)}) collective-permute-start(bf16[40,2048]{1,0:T(8,128)(2,1)S(1)} %get-tuple-element.163), channel_id=1, source_target_pairs={{0,8},{1,9},{2,10},{3,11},{4,12},{5,13},{6,14},{7,15},{8,0},{9,1},... | collective-permute-start | bytes 491528 | tf_op jit(solution)/shard_map/ppermute | solution.py:785
  646.8 9.5 %collective-permute-done.40 = bf16[4,40,1280]{2,1,0:T(8,128)(2,1)S(1)} collective-permute-done((bf16[4,40,1280]{2,1,0:T(8,128)(2,1)S(1)}, bf16[4,40,1280]{2,1,0:T(8,128)(2,1)S(1)}, u32[]{:S(2)}, u32[]{:S(2)}) %collective-permute-start.40) | collective-permute-done | bytes 409632 | tf_op jit(solution)/shard_map/ppermute | solution.py:785
  (290 shorter events, 139.1 us)
Async XLA Ops:
  7.2 238.6 %all-gather.2.cloned.1.call-start = ((), (), s32[]{:S(2)}) async-start(), calls=%async_computation.1 | async-start | bytes 16363520 | tf_op jit(solution)/shard_map/all_gather | solution.py:840
  14.6 654.8 %reduce-scatter.2.cloned.1.call-start = ((), (), s32[]{:S(2)}) async-start(), calls=%async_computation.2 | async-start | bytes 14622720 | tf_op jit(solution)/shard_map/reduce_scatter | solution.py:937
  29.3 18.7 %collective-permute-start.6 = (bf16[80,1024]{1,0:T(8,128)(2,1)S(1)}, bf16[80,1024]{1,0:T(8,128)(2,1)S(1)}, u32[]{:S(2)}, u32[]{:S(2)}) collective-permute-start(bf16[80,1024]{1,0:T(8,128)(2,1)S(1)} %get-tuple-element.160), channel_id=1, source_target_pairs={{0,24},{1,25},{2,26},{3,27},{4,28},{5,29},{6,30},{7,31},{8,16},{9,... | collective-permute-start | bytes 491528 | tf_op jit(solution)/shard_map/ppermute | solution.py:785
  50.6 26.7 %collective-permute-start.8 = (bf16[4,80,1024]{2,1,0:T(8,128)(2,1)S(1)}, bf16[4,80,1024]{2,1,0:T(8,128)(2,1)S(1)}, u32[]{:S(2)}, u32[]{:S(2)}) collective-permute-start(bf16[4,80,1024]{2,1,0:T(8,128)(2,1)S(1)} %pad_maximum_fusion.2.refs_0_), channel_id=1, source_target_pairs={{0,4},{1,5},{2,6},{3,7},{4,0},{5,1},{6,2},{7,3},{8,12},{9,13},{10,... | collective-permute-start | bytes 1966088 | tf_op jit(solution)/shard_map/ppermute | solution.py:785
  51.1 28.2 %collective-permute-start.7 = (bf16[4,80,1024]{2,1,0:T(8,128)(2,1)S(1)}, bf16[4,80,1024]{2,1,0:T(8,128)(2,1)S(1)}, u32[]{:S(2)}, u32[]{:S(2)}) collective-permute-start(bf16[4,80,1024]{2,1,0:T(8,128)(2,1)S(1)} %pad_maximum_fusion.2.refs_0_), channel_id=1, source_target_pairs={{0,2},{1,3},{2,0},{3,1},{4,6},{5,7},{6,4},{7,5},{8,10},{9,11},{10,... | collective-permute-start | bytes 1966088 | tf_op jit(solution)/shard_map/ppermute | solution.py:785
  52.2 28.6 %collective-permute-start.10 = (bf16[4,80,1024]{2,1,0:T(8,128)(2,1)S(1)}, bf16[4,80,1024]{2,1,0:T(8,128)(2,1)S(1)}, u32[]{:S(2)}, u32[]{:S(2)}) collective-permute-start(bf16[4,80,1024]{2,1,0:T(8,128)(2,1)S(1)} %pad_maximum_fusion.2.refs_0_), channel_id=1, source_target_pairs={{0,1},{1,0},{2,3},{3,2},{4,5},{5,4},{6,7},{7,6},{8,9},{9,8},{10,11... | collective-permute-start | bytes 1966088 | tf_op jit(solution)/shard_map/ppermute | solution.py:785
  94.5 24.4 %collective-permute-start.19 = (bf16[5,656,128]{2,1,0:T(8,128)(2,1)}, bf16[5,656,128]{2,1,0:T(8,128)(2,1)S(1)}, u32[]{:S(2)}, u32[]{:S(2)}) collective-permute-start(bf16[5,656,128]{2,1,0:T(8,128)(2,1)} %get-tuple-element.66.refs_0_), channel_id=1, source_target_pairs={{0,6},{1,7},{2,4},{3,5},{4,2},{5,3},{6,0},{7,1},{8,14},{9,15},{10,... | collective-permute-start | bytes 2519048 | tf_op jit(solution)/shard_map/ppermute | solution.py:785
  95.1 40.0 %collective-permute-start.17 = (bf16[5,656,128]{2,1,0:T(8,128)(2,1)}, bf16[5,656,128]{2,1,0:T(8,128)(2,1)S(1)}, u32[]{:S(2)}, u32[]{:S(2)}) collective-permute-start(bf16[5,656,128]{2,1,0:T(8,128)(2,1)} %get-tuple-element.66.refs_0_), channel_id=1, source_target_pairs={{0,4},{1,5},{2,6},{3,7},{4,0},{5,1},{6,2},{7,3},{8,12},{9,13},{10,... | collective-permute-start | bytes 2519048 | tf_op jit(solution)/shard_map/ppermute | solution.py:785
  98.5 37.7 %collective-permute-start.15 = (bf16[5,656,128]{2,1,0:T(8,128)(2,1)}, bf16[5,656,128]{2,1,0:T(8,128)(2,1)S(1)}, u32[]{:S(2)}, u32[]{:S(2)}) collective-permute-start(bf16[5,656,128]{2,1,0:T(8,128)(2,1)} %get-tuple-element.66.refs_0_), channel_id=1, source_target_pairs={{0,2},{1,3},{2,0},{3,1},{4,6},{5,7},{6,4},{7,5},{8,10},{9,11},{10,... | collective-permute-start | bytes 2519048 | tf_op jit(solution)/shard_map/ppermute | solution.py:785
  99.3 37.5 %collective-permute-start.14 = (bf16[5,656,128]{2,1,0:T(8,128)(2,1)}, bf16[5,656,128]{2,1,0:T(8,128)(2,1)S(1)}, u32[]{:S(2)}, u32[]{:S(2)}) collective-permute-start(bf16[5,656,128]{2,1,0:T(8,128)(2,1)} %get-tuple-element.66.refs_0_), channel_id=1, source_target_pairs={{0,1},{1,0},{2,3},{3,2},{4,5},{5,4},{6,7},{7,6},{8,9},{9,8},{10,11... | collective-permute-start | bytes 2519048 | tf_op jit(solution)/shard_map/ppermute | solution.py:785
  416.9 76.5 %collective-permute-start.26 = (bf16[3,640,128]{2,1,0:T(8,128)(2,1)S(1)}, bf16[3,640,128]{2,1,0:T(8,128)(2,1)S(1)}, u32[]{:S(2)}, u32[]{:S(2)}) collective-permute-start(bf16[3,640,128]{2,1,0:T(8,128)(2,1)S(1)} %get-tuple-element.89), channel_id=1, source_target_pairs={{0,2},{1,3},{2,0},{3,1},{4,6},{5,7},{6,4},{7,5},{8,10},{9,11},{10,... | collective-permute-start | bytes 1474568 | tf_op jit(solution)/shard_map/ppermute | solution.py:785
  445.5 49.5 %collective-permute-start.27 = (bf16[3,640,128]{2,1,0:T(8,128)(2,1)S(1)}, bf16[3,640,128]{2,1,0:T(8,128)(2,1)S(1)}, u32[]{:S(2)}, u32[]{:S(2)}) collective-permute-start(bf16[3,640,128]{2,1,0:T(8,128)(2,1)S(1)} %get-tuple-element.90), channel_id=1, source_target_pairs={{0,4},{1,5},{2,6},{3,7},{4,0},{5,1},{6,2},{7,3},{8,12},{9,13},{10,... | collective-permute-start | bytes 1474568 | tf_op jit(solution)/shard_map/ppermute | solution.py:785
  467.4 27.9 %collective-permute-start.28 = (bf16[3,640,128]{2,1,0:T(8,128)(2,1)S(1)}, bf16[3,640,128]{2,1,0:T(8,128)(2,1)S(1)}, u32[]{:S(2)}, u32[]{:S(2)}) collective-permute-start(bf16[3,640,128]{2,1,0:T(8,128)(2,1)S(1)} %get-tuple-element.91), channel_id=1, source_target_pairs={{0,6},{1,7},{2,4},{3,5},{4,2},{5,3},{6,0},{7,1},{8,14},{9,15},{10,... | collective-permute-start | bytes 1474568 | tf_op jit(solution)/shard_map/ppermute | solution.py:785
  469.4 25.9 %collective-permute-start.29 = (bf16[4,4,40,2048]{3,2,1,0:T(8,128)(2,1)}, bf16[4,4,40,2048]{3,2,1,0:T(8,128)(2,1)}, u32[]{:S(2)}, u32[]{:S(2)}) collective-permute-start(bf16[4,4,40,2048]{3,2,1,0:T(8,128)(2,1)} %get-tuple-element.137), channel_id=1, source_target_pairs={{0,1},{1,0},{2,3},{3,2},{4,5},{5,4},{6,7},{7,6},{8,9},{9,8},{10,11... | collective-permute-start | bytes 7864328 | tf_op jit(solution)/shard_map/ppermute | solution.py:785
  511.9 39.6 %collective-permute-start.31 = (bf16[2,640,128]{2,1,0:T(8,128)(2,1)S(1)}, bf16[2,640,128]{2,1,0:T(8,128)(2,1)S(1)}, u32[]{:S(2)}, u32[]{:S(2)}) collective-permute-start(bf16[2,640,128]{2,1,0:T(8,128)(2,1)S(1)} %get-tuple-element.101), channel_id=1, source_target_pairs={{0,2},{1,3},{2,0},{3,1},{4,6},{5,7},{6,4},{7,5},{8,10},{9,11},{10,... | collective-permute-start | bytes 983048 | tf_op jit(solution)/shard_map/ppermute | solution.py:785
  531.3 52.3 %collective-permute-start.32 = (bf16[2,640,128]{2,1,0:T(8,128)(2,1)S(1)}, bf16[2,640,128]{2,1,0:T(8,128)(2,1)S(1)}, u32[]{:S(2)}, u32[]{:S(2)}) collective-permute-start(bf16[2,640,128]{2,1,0:T(8,128)(2,1)S(1)} %get-tuple-element.102), channel_id=1, source_target_pairs={{0,4},{1,5},{2,6},{3,7},{4,0},{5,1},{6,2},{7,3},{8,12},{9,13},{10,... | collective-permute-start | bytes 983048 | tf_op jit(solution)/shard_map/ppermute | solution.py:785
  547.4 36.1 %collective-permute-start.33 = (bf16[2,640,128]{2,1,0:T(8,128)(2,1)S(1)}, bf16[2,640,128]{2,1,0:T(8,128)(2,1)S(1)}, u32[]{:S(2)}, u32[]{:S(2)}) collective-permute-start(bf16[2,640,128]{2,1,0:T(8,128)(2,1)S(1)} %get-tuple-element.103), channel_id=1, source_target_pairs={{0,6},{1,7},{2,4},{3,5},{4,2},{5,3},{6,0},{7,1},{8,14},{9,15},{10,... | collective-permute-start | bytes 983048 | tf_op jit(solution)/shard_map/ppermute | solution.py:785
  548.5 50.6 %collective-permute-start.36 = (bf16[4,40,2048]{2,1,0:T(8,128)(2,1)S(1)}, bf16[4,40,2048]{2,1,0:T(8,128)(2,1)S(1)}, u32[]{:S(2)}, u32[]{:S(2)}) collective-permute-start(bf16[4,40,2048]{2,1,0:T(8,128)(2,1)S(1)} %get-tuple-element.144), channel_id=1, source_target_pairs={{0,6},{1,7},{2,4},{3,5},{4,2},{5,3},{6,0},{7,1},{8,14},{9,15},{10,... | collective-permute-start | bytes 1966088 | tf_op jit(solution)/shard_map/ppermute | solution.py:785
  551.5 47.7 %collective-permute-start.35 = (bf16[4,40,2048]{2,1,0:T(8,128)(2,1)S(1)}, bf16[4,40,2048]{2,1,0:T(8,128)(2,1)S(1)}, u32[]{:S(2)}, u32[]{:S(2)}) collective-permute-start(bf16[4,40,2048]{2,1,0:T(8,128)(2,1)S(1)} %get-tuple-element.145), channel_id=1, source_target_pairs={{0,4},{1,5},{2,6},{3,7},{4,0},{5,1},{6,2},{7,3},{8,12},{9,13},{10,... | collective-permute-start | bytes 1966088 | tf_op jit(solution)/shard_map/ppermute | solution.py:785
  551.5 47.7 %collective-permute-start.34 = (bf16[4,40,2048]{2,1,0:T(8,128)(2,1)S(1)}, bf16[4,40,2048]{2,1,0:T(8,128)(2,1)S(1)}, u32[]{:S(2)}, u32[]{:S(2)}) collective-permute-start(bf16[4,40,2048]{2,1,0:T(8,128)(2,1)S(1)} %get-tuple-element.146), channel_id=1, source_target_pairs={{0,2},{1,3},{2,0},{3,1},{4,6},{5,7},{6,4},{7,5},{8,10},{9,11},{10,... | collective-permute-start | bytes 1966088 | tf_op jit(solution)/shard_map/ppermute | solution.py:785
  602.9 29.5 %collective-permute-start.37 = (bf16[4,4,40,1280]{3,2,0,1:T(8,128)(2,1)}, bf16[4,4,40,1280]{3,2,0,1:T(8,128)(2,1)}, u32[]{:S(2)}, u32[]{:S(2)}) collective-permute-start(bf16[4,4,40,1280]{3,2,0,1:T(8,128)(2,1)} %bitcast.115), channel_id=1, source_target_pairs={{0,1},{1,0},{2,3},{3,2},{4,5},{5,4},{6,7},{7,6},{8,9},{9,8},{10,11... | collective-permute-start | bytes 4915208 | tf_op jit(solution)/shard_map/ppermute | solution.py:785
  605.2 32.9 %collective-permute-start.44 = (bf16[40,2048]{1,0:T(8,128)(2,1)S(1)}, bf16[40,2048]{1,0:T(8,128)(2,1)S(1)}, u32[]{:S(2)}, u32[]{:S(2)}) collective-permute-start(bf16[40,2048]{1,0:T(8,128)(2,1)S(1)} %get-tuple-element.163), channel_id=1, source_target_pairs={{0,8},{1,9},{2,10},{3,11},{4,12},{5,13},{6,14},{7,15},{8,0},{9,1},... | collective-permute-start | bytes 491528 | tf_op jit(solution)/shard_map/ppermute | solution.py:785
  634.8 21.5 %collective-permute-start.40 = (bf16[4,40,1280]{2,1,0:T(8,128)(2,1)S(1)}, bf16[4,40,1280]{2,1,0:T(8,128)(2,1)S(1)}, u32[]{:S(2)}, u32[]{:S(2)}) collective-permute-start(bf16[4,40,1280]{2,1,0:T(8,128)(2,1)S(1)} %get-tuple-element.152), channel_id=1, source_target_pairs={{0,6},{1,7},{2,4},{3,5},{4,2},{5,3},{6,0},{7,1},{8,14},{9,15},{10,... | collective-permute-start | bytes 1228808 | tf_op jit(solution)/shard_map/ppermute | solution.py:785
  638.1 19.5 %collective-permute-start.39 = (bf16[4,40,1280]{2,1,0:T(8,128)(2,1)S(1)}, bf16[4,40,1280]{2,1,0:T(8,128)(2,1)S(1)}, u32[]{:S(2)}, u32[]{:S(2)}) collective-permute-start(bf16[4,40,1280]{2,1,0:T(8,128)(2,1)S(1)} %get-tuple-element.153), channel_id=1, source_target_pairs={{0,4},{1,5},{2,6},{3,7},{4,0},{5,1},{6,2},{7,3},{8,12},{9,13},{10,... | collective-permute-start | bytes 1228808 | tf_op jit(solution)/shard_map/ppermute | solution.py:785
  (75 other events, 1174.0 us)
Sparse Core Ops, SparseCore 0:
  14.7 231.0 all-gather.1
  339.3 280.7 reduce-scatter.1

commit v3 on v2

--- a/solution.py
+++ b/solution.py
@@ -20,9 +20,11 @@
 GROUP_COLS = GROUP * HEAD + 2 * HEAD
 QKV = KV_HEADS * GROUP_COLS
 QKV_PAD = QKV + LANES
-BQ = 128
+BQ = 160
 BK = 256
 STACK = GROUP * BQ
+FF_BLOCK = 256
+FF_STEPS = (4, 3)
 HEAD_PARTS = ((0, 3), (3, 2))
 
 EPSILON = 1e-05
@@ -37,6 +39,7 @@
 BF16 = jnp.bfloat16
 ROWS_BY_ROWS = (((1,), (1,)), ((), ()))
 COLS_BY_COLS = (((0,), (0,)), ((), ()))
+SMALL = pl.CostEstimate(flops=10**6, bytes_accessed=10**4, transcendentals=0)
 VMEM_SPACE = pl.BlockSpec(memory_space=pltpu.VMEM)
 SMEM_SPACE = pl.BlockSpec(memory_space=pltpu.SMEM)
 ANY_SPACE = pl.BlockSpec(memory_space=pl.ANY)
@@ -151,13 +154,19 @@
     )(place, x, cos, sin, *pieces)
 
 
+def first_row(device, half, rows, span):
+    device = device ^ (span - 1) if half else device
+    return pl.multiple_of(device * rows + half * (rows // 2), BQ)
+
+
 def gather_keys(block, kv_refs, kv, sems, heads):
-    rows = kv_refs[0].shape[1] - 16
+    rows, span = kv_refs[0].shape[1] - 16, len(kv_refs)
     copies = []
     for e, ref in enumerate(kv_refs):
-        at = pl.multiple_of((block ^ e) * rows, LANES)
-        to = kv.at[:, pl.ds(at, rows), :]
-        copies.append(pltpu.make_async_copy(ref.at[heads, pl.ds(0, rows), :], to, sems.at[e]))
+        for half in range(2):
+            source = ref.at[heads, pl.ds(half * (rows // 2), rows // 2), :]
+            to = kv.at[:, pl.ds(first_row(block ^ e, half, rows, span), rows // 2), :]
+            copies.append(pltpu.make_async_copy(source, to, sems.at[2 * e + half]))
     return copies
 
 
@@ -217,7 +226,7 @@
     copies = gather_keys(meta_ref[0], kv_refs, kv, sems, pl.ds(0, KV_HEADS))
     for e, ref in enumerate(kv_refs):
         source = ref.at[0, pl.ds(rows, 16), :]
-        copies.append(pltpu.make_async_copy(source, k_tops.at[e], sems.at[span + e]))
+        copies.append(pltpu.make_async_copy(source, k_tops.at[e], sems.at[2 * span + e]))
     for copy in copies:
         copy.start()
     for copy in copies:
@@ -339,12 +348,10 @@
             pltpu.VMEM((KV_HEADS, STACK, LANES), F32),
             pltpu.VMEM((KV_HEADS, STACK, LANES), F32),
             pltpu.VMEM((span, 16, LANES), BF16),
-            pltpu.SemaphoreType.DMA((2 * span,)),
+            pltpu.SemaphoreType.DMA((3 * span,)),
         ],
         compiler_params=params(52),
-        cost_estimate=pl.CostEstimate(
-            flops=80 * 10**9, bytes_accessed=15 * 10**6, transcendentals=3 * 10**7
-        ),
+        cost_estimate=SMALL,
         name="attention_forward",
     )(meta, q, top, *kvs, info, seg)
 
@@ -449,16 +456,17 @@
     factor = jnp.where(lane < HEAD, SCALE, 1.0)
     for e in range(span):
         target = near_ref if e % 2 == 0 else far_ref
-        first = (block ^ e) * rows
-
-        def leave(n, _):
-            at = pl.ds(pl.multiple_of(n * BQ, BQ), BQ)
-            source = pl.ds(pl.multiple_of(first + n * BQ, BQ), BQ)
-            for g in range(groups):
-                target[e // 2, g, at, :] = (dkv[g, source, :] * factor).astype(BF16)
-            return 0
-
-        lax.fori_loop(0, rows // BQ, leave, 0)
+        for half in range(2):
+            first = first_row(block ^ e, half, rows, span)
+
+            def leave(n, _):
+                at = pl.ds(pl.multiple_of(half * (rows // 2) + n * BQ, BQ), BQ)
+                source = pl.ds(pl.multiple_of(first + n * BQ, BQ), BQ)
+                for g in range(groups):
+                    target[e // 2, g, at, :] = (dkv[g, source, :] * factor).astype(BF16)
+                return 0
+
+            lax.fori_loop(0, rows // 2 // BQ, leave, 0)
 
 
 def attention_backward(heads, meta, q, da, att, lse, cos, sin, kvs, info, seg):
@@ -467,7 +475,6 @@
     keys = span * rows
     tiles = keys // BK
     groups = heads[1]
-    work = 36 * 10**9 * groups
     return pl.pallas_call(
         functools.partial(backward_kernel, tiles=tiles, span=span, heads=heads),
         out_shape=[
@@ -484,12 +491,10 @@
             pltpu.VMEM((groups, STACK, LANES), F32),
             pltpu.VMEM((groups, 2 * STACK, LANES), BF16),
             pltpu.VMEM((groups, 2 * STACK, LANES), BF16),
-            pltpu.SemaphoreType.DMA((span,)),
+            pltpu.SemaphoreType.DMA((2 * span,)),
         ],
         compiler_params=params(56),
-        cost_estimate=pl.CostEstimate(
-            flops=work, bytes_accessed=30 * 10**6, transcendentals=3 * 10**7
-        ),
+        cost_estimate=SMALL,
         name="attention_backward",
     )(meta, q, da, att, lse, cos, sin, *kvs, info, seg)
 
@@ -531,10 +536,10 @@
 
 
 def feed_forward_kernel(
-    n1_ref, n2_ref, og1_ref, og2_ref, wg_ref, wu_ref, wd_ref,
-    own_ref, far_ref, dw_ref,
-    n, og, nt, ogt, oacc, nacc, hid, dgate, dup,
+    n1_ref, n2_ref, og1_ref, og2_ref, wg_ref, wu_ref, wd_ref, *refs, later
 ):
+    priors, refs = refs[: 2 * later], refs[2 * later :]
+    own_ref, far_ref, dw_ref, n, og, nt, ogt, oacc, nacc, hid, dgate, dup = refs
     f = pl.program_id(0)
     part = pl.program_id(1)
     rows = n1_ref.shape[0]
@@ -547,8 +552,14 @@
         og[rows:] = og2_ref[...]
         nt[...] = n[...].T
         ogt[...] = og[...].T
-        oacc[...] = jnp.zeros_like(oacc)
-        nacc[...] = jnp.zeros_like(nacc)
+        if later:
+            for k, (prior, target) in enumerate(zip(priors, (own_ref, far_ref))):
+                pltpu.sync_copy(prior, target)
+                oacc[k * rows : (k + 1) * rows] = target[0].astype(F32)
+                nacc[k * rows : (k + 1) * rows] = target[1].astype(F32)
+        else:
+            oacc[...] = jnp.zeros_like(oacc)
+            nacc[...] = jnp.zeros_like(nacc)
 
     @pl.when(part == 0)
     def _():
@@ -582,22 +593,21 @@
         far_ref[1] = nacc[rows:].astype(BF16)
 
 
-def feed_forward(n_own, n_far, og_own, og_far, w):
+def feed_forward(steps, n_own, n_far, og_own, og_far, w, priors=()):
     rows = n_own.shape[0]
-    block = 256
-    steps = HALF // block
+    block = FF_BLOCK
     whole = pl.BlockSpec((rows, D), lambda f, k: (0, 0), pipeline_mode=pl.Buffered(1))
     sides = pl.BlockSpec((2, rows, D), lambda f, k: (0, 0, 0))
     slab = [pl.BlockSpec((D, block), lambda f, k, m=m: (0, m * steps + f)) for m in range(3)]
     return pl.pallas_call(
-        feed_forward_kernel,
+        functools.partial(feed_forward_kernel, later=bool(priors)),
         grid=(steps, 3),
-        in_specs=[whole] * 4 + slab,
+        in_specs=[whole] * 4 + slab + [ANY_SPACE] * len(priors),
         out_specs=[sides, sides, pl.BlockSpec((D, block), lambda f, k: (0, k * steps + f))],
         out_shape=[
             jax.ShapeDtypeStruct((2, rows, D), BF16),
             jax.ShapeDtypeStruct((2, rows, D), BF16),
-            jax.ShapeDtypeStruct((D, 3 * HALF), BF16),
+            jax.ShapeDtypeStruct((D, 3 * steps * block), BF16),
         ],
         scratch_shapes=[
             pltpu.VMEM((2 * rows, D), BF16),
@@ -611,11 +621,9 @@
             pltpu.VMEM((2 * rows, block), BF16),
         ],
         compiler_params=params(62),
-        cost_estimate=pl.CostEstimate(
-            flops=52 * 10**9, bytes_accessed=40 * 10**6, transcendentals=3 * 10**6
-        ),
+        cost_estimate=SMALL,
         name="feed_forward",
-    )(n_own, n_far, og_own, og_far, w, w, w)
+    )(n_own, n_far, og_own, og_far, w, w, w, *priors)
 
 
 def turn_kernel(
@@ -662,22 +670,6 @@
     )(mid, own, got, og, gains, w, att)
 
 
-def query_grad_kernel(n_ref, dq_ref, dw_ref):
-    dw_ref[...] = dot_cc(n_ref[...], dq_ref[...]).astype(BF16)
-
-
-def query_grad(n, dq):
-    return pl.pallas_call(
-        query_grad_kernel,
-        out_shape=jax.ShapeDtypeStruct((D, dq.shape[1]), BF16),
-        compiler_params=params(32),
-        cost_estimate=pl.CostEstimate(
-            flops=4 * 10**9, bytes_accessed=10**7, transcendentals=0
-        ),
-        name="query_grad",
-    )(n, dq)
-
-
 def project_back_kernel(
     x_ref, n_ref, dqa_ref, dqb_ref, ka_refs, kb_refs, w_ref, dgain_ref,
     cos_ref, sin_ref, dn_ref, dw_ref, dz,
@@ -703,10 +695,7 @@
         return 0
 
     lax.fori_loop(0, rows // BQ, turn_back, 0)
-    kv_cols = [dz[:, g * GROUP_COLS + GROUP * HEAD : (g + 1) * GROUP_COLS] for g in range(KV_HEADS)]
-    dw_ref[:, : KV_HEADS * LANES] = dot_cc(
-        n_ref[...], jnp.concatenate(kv_cols, axis=1)
-    ).astype(BF16)
+    dw_ref[:, :QKV] = dot_cc(n_ref[...], dz[...]).astype(BF16)
     dn_ref[...] = dot_tr(dz[...], w_ref[:, :QKV])
 
     def step(i, dgain):
@@ -720,7 +709,7 @@
     dgain2 = jnp.sum(dgain_ref[...], axis=0, keepdims=True)
     row = lax.broadcasted_iota(jnp.int32, (LANES, D), 0)
     both = jnp.where(row == 0, dgain1, jnp.where(row == 1, dgain2, 0.0))
-    dw_ref[:, KV_HEADS * LANES :] = both.T.astype(BF16)
+    dw_ref[:, QKV:] = both.T.astype(BF16)
 
 
 def project_back(x, n, dqs, pieces, w, dgain, cos, sin):
@@ -737,7 +726,7 @@
         kernel,
         out_shape=[
             jax.ShapeDtypeStruct((rows, D), F32),
-            jax.ShapeDtypeStruct((D, (KV_HEADS + 1) * LANES), BF16),
+            jax.ShapeDtypeStruct((D, QKV_PAD), BF16),
         ],
         scratch_shapes=[pltpu.VMEM((rows, QKV), BF16)],
         compiler_params=params(48),
@@ -763,7 +752,7 @@
         out_specs=block,
         out_shape=jax.ShapeDtypeStruct((rows, D), F32),
         compiler_params=params(32),
-        cost_estimate=pl.CostEstimate(flops=10**7, bytes_accessed=10**7, transcendentals=0),
+        cost_estimate=SMALL,
         name="input_gradient",
     )(x, gm, dn, gains)
 
@@ -793,11 +782,7 @@
     def stage(*values):
         return lax.optimization_barrier(values)
 
-    def half_columns(*weights):
-        halves = [
-            jnp.concatenate([w[:, c * w.shape[1] // 2 :][:, : w.shape[1] // 2] for w in weights], axis=1)
-            for c in range(2)
-        ]
+    def half_columns(*halves):
         keep = jnp.where(core == 0, halves[0], halves[1])
         got = swap(jnp.where(core == 0, halves[1], halves[0]), 1)
         return jnp.where(
@@ -823,11 +808,25 @@
             swap(part(total, tree ^ t, 0), span * t) for t in range(1, trees)
         )
 
+    def halve(v, bit, axis, distance):
+        return part(v, bit, axis), swap(part(v, 1 - bit, axis), distance)
+
+    def trees_first(v):
+        if trees != 4:
+            return (v,)
+        return halve(v.reshape(2, 2, *v.shape[1:]), tree // 2, 0, 2 * span)
+
+    def trees_second(v):
+        return halve(v, tree % 2, 0, span) if trees == 4 else send_trees(v)
+
     def add(terms):
         return sum((t.astype(F32) for t in terms[1:]), terms[0].astype(F32))
 
     def add16(terms):
         return add(terms).astype(BF16)
+
+    def even_out(v):
+        return jnp.concatenate([v[: rows // 2], swap(v[rows // 2 :], span - 1).astype(v.dtype)])
 
     turned = w_output.T
     grouped = [w_query.reshape(shard, KV_HEADS, GROUP * HEAD)]
@@ -836,10 +835,29 @@
     gain_pair = jnp.stack([norm_gain1, norm_gain2], axis=1)
     gain_pair = jnp.pad(gain_pair, ((0, 0), (0, LANES - 2)))
     grouped = jnp.concatenate([grouped, gain_pair], axis=1)
-    chip_rows = half_columns(grouped, w_gate, w_up, w_down.T, turned)
-    ff_w = lax.all_gather(
-        chip_rows[:, QKV_PAD // 2 :], "fsdp", tiled=True, axis_index_groups=same_core
-    )
+
+    def columns(c):
+        parts = [grouped[:, c * QKV_PAD // 2 : (c + 1) * QKV_PAD // 2]]
+        first = c * HALF
+        for k, count in enumerate(FF_STEPS):
+            last = first + count * FF_BLOCK
+            parts += [w[:, first:last] for w in (w_gate, w_up, down)]
+            if k == 0:
+                parts += [turned[:, c * D // 2 : (c + 1) * D // 2]]
+            first = last
+        return jnp.concatenate(parts, axis=1)
+
+    down = w_down.T
+    chip_rows = half_columns(columns(0), columns(1))
+    first, ff_w = QKV_PAD // 2, []
+    for k, count in enumerate(FF_STEPS):
+        last = first + 3 * count * FF_BLOCK + (D // 2 if k == 0 else 0)
+        ff_w += [
+            lax.all_gather(
+                chip_rows[:, first:last], "fsdp", tiled=True, axis_index_groups=same_core
+            )
+        ]
+        first = last
     qkv_rows = chip_rows[:, : QKV_PAD // 2]
     if trees > 4:
         qkv_rows = lax.all_gather(qkv_rows, "fsdp", tiled=True, axis_index_groups=same_core)[None]
@@ -862,10 +880,16 @@
             [jnp.where(first, tree_seg, other), jnp.where(first, other, tree_seg)], axis=0
         )
         bit *= 2
+    layer_in, tree_seg = stage(layer_in, tree_seg)
+    tokens_in = even_out(layer_in)
     seg_count = segment_parents.shape[0] * span // size
     seg_base = tree * seg_count
     tree_seg = tree_seg - seg_base
-    own_seg = segment_ids - seg_base
+    starts = [first_row(block, half, rows, span) for half in range(2)]
+    own_row = jnp.concatenate([n + jnp.arange(rows // 2, dtype=jnp.int32) for n in starts])
+    own_seg = jnp.concatenate(
+        [lax.dynamic_slice_in_dim(tree_seg, n, rows // 2) for n in starts]
+    )
     ids = jnp.arange(seg_count, dtype=jnp.int32)
     parent = lax.dynamic_slice_in_dim(segment_parents, seg_base, seg_count) - seg_base
 
@@ -877,7 +901,6 @@
     starts = jnp.sum(jnp.where(ids[None, :] < ids[:, None], lengths[None, :], 0), axis=1)
     depth = jnp.where(parent != ids, look(parent, lengths), 0)
     depth = depth + jnp.where(grand != parent, look(grand, lengths), 0)
-    own_row = block * rows + jnp.arange(rows, dtype=jnp.int32)
     positions = (look(own_seg, depth - starts) + own_row).astype(F32)
     lane = jnp.arange(LANES, dtype=jnp.int32)
     inverse = jnp.exp((lane % 32).astype(F32) * (-2.0 * math.log(ROPE_BASE) / HEAD))
@@ -899,7 +922,7 @@
     here = (step_seg[:, :1] <= ids[None, :]) & (ids[None, :] <= step_seg[:, -1:])
     active = jnp.any(here[:, :, None] & hit[None, :, :], axis=1)
     tile_range = jnp.arange(tiles, dtype=jnp.int32)
-    last_row = block * rows + (jnp.arange(steps, dtype=jnp.int32) + 1) * BQ - 1
+    last_row = own_row.reshape(steps, BQ)[:, -1]
     active = active & (tile_range[None, :] * BK <= last_row[:, None])
     before = tile_range[:, None] < tile_range[None, :]
     place = jnp.sum((active[:, :, None] & before[None]).astype(jnp.int32), axis=1)
@@ -919,23 +942,32 @@
     meta = jnp.concatenate([block[None], *counts, listed.reshape(steps * tiles)])
     seg_row = tree_seg[None, :]
 
-    og_far = swap(out_grad, 1)
-    normed1, q, kv, gains, qkv_w, q_top = project(qkv_place, layer_in, cos, sin, qkv_pieces)
+    normed1, q, kv, gains, qkv_w, q_top = project(qkv_place, tokens_in, cos, sin, qkv_pieces)
     kvs = [kv, swap(kv, 1)]
     for c in range(1, chips):
         piece = swap(kv, 2 * c)
         kvs += [piece, swap(piece, 1)]
+    out_grad, *kvs = stage(out_grad, *kvs)
+    grads_in = even_out(out_grad)
     att, lse = attention_forward(meta, q, q_top, kvs, info, seg_row)
-    att, ff_w = stage(att, ff_w)
-    out_w = ff_w[None, :, 3 * HALF :]
+    att, grads_in = stage(att, grads_in)
+    og_far = swap(grads_in, 1)
+    att, ff_w[0] = stage(att, ff_w[0])
+    out_w = ff_w[0][None, :, 3 * FF_STEPS[0] * FF_BLOCK :]
     out_place = jnp.stack([core, 1 - core, 0, 0])
-    mid, normed2, out_w = middle(layer_in, att, gains, [out_w, swap(out_w, 1)], out_place)
-    own, far, ff_dw = feed_forward(normed2, swap(normed2, 1), out_grad, og_far, ff_w)
-    layer_out, grad_mid, da, out_dw, dgain2 = turn(
-        mid, own, swap(far, 1), out_grad, gains, out_w, att
-    )
+    mid, normed2, out_w = middle(tokens_in, att, gains, [out_w, swap(out_w, 1)], out_place)
+    normed2_far = swap(normed2, 1)
+    tokens = (normed2, normed2_far, grads_in, og_far)
+    *sums, ff_dw = feed_forward(FF_STEPS[0], *tokens, ff_w[0])
     ff_dw = lax.psum_scatter(
         ff_dw, "fsdp", scatter_dimension=0, tiled=True, axis_index_groups=same_core
+    )
+    ff_w[1], *sums = stage(ff_w[1], *sums)
+    *sums, next_dw = feed_forward(FF_STEPS[1], *tokens, ff_w[1], sums)
+    next_dw = send_chips(next_dw.reshape(trees, chips, 2 * shard, next_dw.shape[1]))
+    own, far = sums
+    layer_out, grad_mid, da, out_dw, dgain2 = turn(
+        mid, own, swap(far, 1), grads_in, gains, out_w, att
     )
 
     def backward(n, meta):
@@ -947,58 +979,74 @@
         got = swap(far, 1)
         return [near[0], got[0]], [add16((near[c], got[c])) for c in range(1, chips)]
 
+    chip_x, chip_y = chip % 2, chip // 2
+    out_dw = send_cores(out_dw)
+    layer_out = even_out(layer_out)
     dq_a, near, far = backward(0, meta)
+    near, far, dq_a, layer_out, *values = stage(near, far, dq_a, layer_out, *out_dw, *next_dw)
+    out_dw, next_dw = add16(values[:2]), add16(values[2:])
     pieces_a, both = meet(near, far)
-    query_a = query_grad(normed1, dq_a)
-    meta_b, early, *both = stage(meta, jnp.concatenate([out_dw, query_a], axis=1), *both)
+    meta, out_dw, next_dw, *both = stage(meta, out_dw, next_dw, *both)
     both = [swap(v, 2 * c + 2) for c, v in enumerate(both)]
-    early = send_cores(early)
-    dq_b, near, far = backward(1, meta_b)
-    near, far, dq_b, *values = stage(near, far, dq_b, *both, *early)
+    out_dw = halve(out_dw.reshape(trees, 2, 2, shard, D), chip_x, 2, 2)
+    next_dw = trees_first(next_dw)
+    dq_b, near, far = backward(1, meta)
+    near, far, dq_b, *values = stage(near, far, dq_b, *both, *out_dw, *next_dw)
     pieces_a += values[: len(both)]
-    early = add16(values[len(both) :])
+    values = values[len(both) :]
+    out_dw, next_dw = add16(values[:2]), add16(values[2:])
     pieces_b, both = meet(near, far)
-    query_b = query_grad(normed1, dq_b)
-    early, query_b, *both = stage(early, query_b, *both)
+    out_dw, next_dw, *both = stage(out_dw, next_dw, *both)
     pieces_b += [swap(v, 2 * c + 2) for c, v in enumerate(both)]
-    early = send_chips(early)
-    dn, kv_dw = project_back(
-        layer_in, normed1, (dq_a, dq_b), (pieces_a, pieces_b), qkv_w, dgain2, cos, sin
+    out_dw = halve(out_dw, chip_y, 1, 4)
+    next_dw = trees_second(next_dw)
+    dn, qkv_dw = project_back(
+        tokens_in, normed1, (dq_a, dq_b), (pieces_a, pieces_b), qkv_w, dgain2, cos, sin
     )
-    late = jnp.concatenate([kv_dw, query_b], axis=1)
-    late, dn, *early = stage(late, dn, *early)
-    early, late = send_trees(add16(early)), send_cores(late)
-    input_grad = input_gradient(layer_in, grad_mid, dn, gains)
-    early, late = add(early), add16(late)
-    late = add(send_trees(add16(send_chips(late))))
-    out_dw, kv_dw = early[:, :D], late[:, : (KV_HEADS + 1) * LANES]
-    query_dw = jnp.concatenate([early[:, D:], late[:, (KV_HEADS + 1) * LANES :]], axis=1)
-
-    groups = kv_dw[:, : KV_HEADS * LANES].reshape(shard, KV_HEADS, LANES)
-    grad_key = groups[:, :, :HEAD].reshape(shard, KV_HEADS * HEAD)
-    grad_value = groups[:, :, HEAD:].reshape(shard, KV_HEADS * HEAD)
-
-    def join(grad):
-        mine, other = grad[:shard], grad[shard:]
-        keep = jnp.where(core == 0, mine, other)
-        got = swap(jnp.where(core == 0, other, mine), 1)
-        low = jnp.where(core == 0, keep, got).astype(F32).reshape(shard, -1, HALF)
-        high = jnp.where(core == 0, got, keep).astype(F32).reshape(shard, -1, HALF)
-        return jnp.concatenate([low, high], axis=2)
-
-    ff_grads = join(ff_dw)
+    qkv_dw = send_cores(qkv_dw)
+    dn, *values = stage(dn, *out_dw, *next_dw, *qkv_dw)
+    out_dw, values = add16(values[:2]), values[2:]
+    next_dw, qkv_dw = add16(values[: len(next_dw)]), add16(values[len(next_dw) :])
+    qkv_dw = send_chips(qkv_dw)
+    ff_dw = jnp.concatenate([ff_dw, next_dw], axis=1).reshape(2, shard, -1)
+    ff_dw = halve(ff_dw, core, 0, 1)
+    out_dw = trees_first(out_dw)
+    input_grad = input_gradient(tokens_in, grad_mid, dn, gains)
+    input_grad, *values = stage(input_grad, *ff_dw, *out_dw, *qkv_dw)
+    (keep, got), values = values[:2], values[2:]
+    out_dw, qkv_dw = add16(values[: len(out_dw)]), add16(values[len(out_dw) :])
+    out_dw, qkv_dw = trees_second(out_dw), send_trees(qkv_dw)
+    travelled = swap(input_grad[rows // 2 :].astype(BF16), span - 1)
+    input_grad = jnp.concatenate([input_grad[: rows // 2], travelled.astype(F32)])
+    out_dw, qkv_dw = add(out_dw), add(qkv_dw)
+
+    groups = qkv_dw[:, :QKV].reshape(shard, KV_HEADS, GROUP_COLS)
+    grad_query = groups[:, :, : GROUP * HEAD].reshape(shard, HEADS * HEAD)
+    grad_key = groups[:, :, GROUP * HEAD : GROUP * HEAD + HEAD].reshape(shard, KV_HEADS * HEAD)
+    grad_value = groups[:, :, GROUP * HEAD + HEAD :].reshape(shard, KV_HEADS * HEAD)
+
+    grads = [[], [], []]
+    for c in range(2):
+        half = jnp.where(core == c, keep, got).astype(F32)
+        first = 0
+        for steps in FF_STEPS:
+            for grad in grads:
+                last = first + steps * FF_BLOCK
+                grad.append(half[:, first:last])
+                first = last
+    ff_grads = [jnp.concatenate(grad, axis=1) for grad in grads]
     return (
         layer_out,
         input_grad,
-        kv_dw[:, KV_HEADS * LANES],
-        query_dw,
+        qkv_dw[:, QKV],
+        grad_query,
         grad_key,
         grad_value,
         out_dw.T,
-        kv_dw[:, KV_HEADS * LANES + 1],
-        ff_grads[:, 0],
-        ff_grads[:, 1],
-        ff_grads[:, 2].T,
+        qkv_dw[:, QKV + 1],
+        ff_grads[0],
+        ff_grads[1],
+        ff_grads[2].T,
     )
 
 

time: 695 us -> 681 us (0.980)
  starting transfers between devices: 161 us -> 68.1 us
  Pallas kernels: 205 us -> 289 us
  waiting for transfers between devices: 245 us -> 217 us
  other arithmetic: 21.1 us -> 34.9 us
  local copies, waits for them, and re-layouts: 38.7 us -> 46.3 us
    ppermute x48 -> x55, starting transfers between devices: 160 us -> 68 us  [swap(): return lax.ppermute(v, 'fsdp', [(i, i ^ bit) for i in range(size)])]
    all_gather x1 -> x2, waiting for transfers between devices: 82 us -> 0.01 us  [body(): lax.all_gather(chip_rows[:, first:last], 'fsdp', tiled=True, axis_index_g...]
    ppermute x48 -> x55, waiting for transfers between devices: 163 us -> 217 us  [swap(): return lax.ppermute(v, 'fsdp', [(i, i ^ bit) for i in range(size)])]
    pallas_call x2, Pallas kernels: 56.6 us -> 107 us  [attention_backward(): pl.pallas_call(functools.partial(backward_kernel, tiles=tiles, span=span,...]
    pallas_call x1, Pallas kernels: 21.4 us -> 42.9 us  [attention_forward(): pl.pallas_call(functools.partial(forward_kernel, tiles=tiles, span=span),...]
    squeeze x5 -> x12, local copies, waits for them, and re-layouts: 3.29 us -> 16.1 us  [part(): return lax.dynamic_index_in_dim(v, index, axis, keepdims=False)]
    pallas_call x3 -> x2, Pallas kernels: 76 us -> 86.9 us  [feed_forward(): pl.pallas_call(functools.partial(feed_forward_kernel, later=bool(priors))...]
    unnamed x103 -> x102, local copies, waits for them, and re-layouts: 20.1 us -> 14.6 us
  transfers between devices with their start and end apart: 50 -> 58, of which waited for: 30 -> 23; matrix products, arithmetic and copies ran while one was open for 4% -> 9% of each run, Pallas kernels for 19% -> 37%
where the time goes in v3:
time: 681 us; the launch traced here: 671 us
  Pallas kernels  289 us (42%)
  waiting for transfers between devices  217 us (32%)
  starting transfers between devices  68.1 us (10%)
  local copies, waits for them, and re-layouts  46.3 us (7%)
  other arithmetic  34.9 us (5%)
  between operations  15 us (2%)
    ppermute x55, waiting for transfers between devices, swap(): return lax.ppermute(v, 'fsdp', [(i, i ^ bit) for i in range(size)])  217 us
    pallas_call x2, Pallas kernels, attention_backward(): pl.pallas_call(functools.partial(backward_kernel, tiles=tiles, span=span,...  107 us
    pallas_call x2, Pallas kernels, feed_forward(): pl.pallas_call(functools.partial(feed_forward_kernel, later=bool(priors))...  86.9 us
    ppermute x55, starting transfers between devices, swap(): return lax.ppermute(v, 'fsdp', [(i, i ^ bit) for i in range(size)])  68 us
    pallas_call x1, Pallas kernels, attention_forward(): pl.pallas_call(functools.partial(forward_kernel, tiles=tiles, span=span),...  42.9 us
    pallas_call x1, Pallas kernels, project_back(): pl.pallas_call(kernel, out_shape=[jax.ShapeDtypeStruct((rows, D), F32), j...  17 us
    pallas_call x1, Pallas kernels, turn(): pl.pallas_call(turn_kernel, out_shape=[jax.ShapeDtypeStruct((rows, D), BF...  16.5 us
    squeeze x12, local copies, waits for them, and re-layouts, part(): return lax.dynamic_index_in_dim(v, index, axis, keepdims=False)  16.1 us
  transfers between devices with their start and end apart: 58, of which 23 were waited for; matrix products, arithmetic and copies ran while one was open for 9% of the time, Pallas kernels for 37%

profile of v3, /device:TPU:0, one launch (start us, length us, event | category | flops | bytes accessed | tf_op | source)
XLA Modules:
  0.0 670.6 jit_solution(13246690745473300143)
XLA Ops:
  29.7 9.6 %collective-permute-done.5 = bf16[80,1024]{1,0:T(8,128)(2,1)S(1)} collective-permute-done((bf16[80,1024]{1,0:T(8,128)(2,1)S(1)}, bf16[80,1024]{1,0:T(8,128)(2,1)S(1)}, u32[]{:S(2)}, u32[]{:S(2)}) %collective-permute-start.5) | collective-permute-done | bytes 163872 | tf_op jit(solution)/shard_map/ppermute | solution.py:774
  39.3 10.0 %collective-permute-done.6 = bf16[80,1024]{1,0:T(8,128)(2,1)S(1)} collective-permute-done((bf16[80,1024]{1,0:T(8,128)(2,1)S(1)}, bf16[80,1024]{1,0:T(8,128)(2,1)S(1)}, u32[]{:S(2)}, u32[]{:S(2)}) %collective-permute-start.6) | collective-permute-done | bytes 163872 | tf_op jit(solution)/shard_map/ppermute | solution.py:774
  54.1 15.1 %collective-permute-done.8.refs_1_ = bf16[4,80,1024]{2,1,0:T(8,128)(2,1)S(1)} collective-permute-done((bf16[4,80,1024]{2,1,0:T(8,128)(2,1)S(1)}, bf16[4,80,1024]{2,1,0:T(8,128)(2,1)S(1)}, u32[]{:S(2)}, u32[]{:S(2)}) %collective-permute-start.8) | collective-permute-done | bytes 655392 | tf_op jit(solution)/shard_map/ppermute | solution.py:774
  71.8 23.8 %collective-permute-done.10.refs_3_ = bf16[4,80,1024]{2,1,0:T(8,128)(2,1)S(1)} collective-permute-done((bf16[4,80,1024]{2,1,0:T(8,128)(2,1)S(1)}, bf16[4,80,1024]{2,1,0:T(8,128)(2,1)S(1)}, u32[]{:S(2)}, u32[]{:S(2)}) %collective-permute-start.10) | collective-permute-done | bytes 655392 | tf_op jit(solution)/shard_map/ppermute | solution.py:774
  98.9 13.0 %project.1 = (bf16[640,1280]{1,0:T(8,128)(2,1)}, bf16[20,640,128]{2,1,0:T(8,128)(2,1)}, bf16[5,656,128]{2,1,0:T(8,128)(2,1)}, f32[8,1280]{1,0:T(8,128)S(1)}, bf1...) custom-call(s32[40]{0:T(128)S(1)} %concatenate.86.place_ref, bf16[640,1280]{1,0:T(8,128)(2,1)} %pad_maximum_fusion.1.x_ref, ...), custom_call_target="tpu_custom_call" | custom-call | tf_op jit(solution)/shard_map/project/pallas_call | solution.py:139
  115.9 35.7 %collective-permute-done.16.refs_2_ = bf16[5,656,128]{2,1,0:T(8,128)(2,1)S(1)} collective-permute-done((bf16[5,656,128]{2,1,0:T(8,128)(2,1)}, bf16[5,656,128]{2,1,0:T(8,128)(2,1)S(1)}, u32[]{:S(2)}, u32[]{:S(2)}) %collective-permute-start.16) | collective-permute-done | bytes 839712 | tf_op jit(solution)/shard_map/ppermute | solution.py:774
  155.4 29.8 %collective-permute-done.20.refs_6_ = bf16[5,656,128]{2,1,0:T(8,128)(2,1)S(1)} collective-permute-done((bf16[5,656,128]{2,1,0:T(8,128)(2,1)}, bf16[5,656,128]{2,1,0:T(8,128)(2,1)S(1)}, u32[]{:S(2)}, u32[]{:S(2)}) %collective-permute-start.20) | collective-permute-done | bytes 839712 | tf_op jit(solution)/shard_map/ppermute | solution.py:774
  194.2 42.9 %attention_forward.1 = (bf16[640,1280]{1,0:T(8,128)(2,1)}, f32[640,128]{1,0:T(8,128)S(1)}) custom-call(s32[241]{0:T(256)S(1)} %fusion.26.meta_ref, bf16[20,640,128]{2,1,0:T(8,128)(2,1)} %get-tuple-element.108.q_ref, f32[8,128]{1,0:T(8,128)S(1)} %get-tuple-element.109.top_ref, bf16[5,656,128]{2,1,0:T(8,128)(2,1)S(1)} %copy-done.8, ...), custom_call_target="tpu_custom_call" | custom-call | flops 1000000 | bytes 10000 | tf_op jit(solution)/shard_map/attention_forward/pallas_call | solution.py:337
  260.0 46.4 %feed_forward.2 = (bf16[2,640,1280]{2,1,0:T(8,128)(2,1)}, bf16[2,640,1280]{2,1,0:T(8,128)(2,1)}, bf16[1280,3072]{1,0:T(8,128)(2,1)}) custom-call(bf16[640,1280]{1,0:T(8,128)(2,1)} %copy-done.9, bf16[640,1280]{1,0:T(8,128)(2,1)} %copy-done.25, bf16[640,1280]{1,0:T(8,128)(2,1)} %pad_maximum_fusion.2.og1_ref.og_ref, ...), custom_call_target="tpu_custom_call" | custom-call | flops 1000000 | bytes 10000 | tf_op jit(solution)/shard_map/feed_forward/pallas_call | solution.py:602
  306.4 40.5 %feed_forward.3 = (bf16[2,640,1280]{2,1,0:T(8,128)(2,1)}, bf16[2,640,1280]{2,1,0:T(8,128)(2,1)}, bf16[1280,2304]{1,0:T(8,128)(2,1)}) custom-call(bf16[640,1280]{1,0:T(8,128)(2,1)} %copy-done.9, bf16[640,1280]{1,0:T(8,128)(2,1)} %copy-done.25, bf16[640,1280]{1,0:T(8,128)(2,1)} %pad_maximum_fusion.2.og1_ref.og_ref, ...), custom_call_target="tpu_custom_call" | custom-call | flops 1000000 | bytes 10000 | tf_op jit(solution)/shard_map/feed_forward/pallas_call | solution.py:602
  352.2 12.2 %collective-permute-start.29 = (bf16[4,80,2304]{2,1,0:T(8,128)(2,1)}, bf16[4,80,2304]{2,1,0:T(8,128)(2,1)}, u32[]{:S(2)}, u32[]{:S(2)}) collective-permute-start(bf16[4,80,2304]{2,1,0:T(8,128)(2,1)} %get-tuple-element.225), channel_id=1, source_target_pairs={{0,2},{1,3},{2,0},{3,1},{4,6},{5,7},{6,4},{7,5},{8,10},{9,11},{10,... | collective-permute-start | bytes 4423688 | tf_op jit(solution)/shard_map/ppermute | solution.py:774
  365.9 16.5 %turn.1 = (bf16[640,1280]{1,0:T(8,128)(2,1)}, f32[640,1280]{1,0:T(8,128)}, bf16[640,1280]{1,0:T(8,128)(2,1)}, bf16[1280,1280]{1,0:T(8,128)(2,1)}, f32[8,1280]{1,0:T(8,128)}) custom-call(f32[640,1280]{1,0:T(8,128)} %copy-done.11, bf16[2,640,1280]{2,1,0:T(8,128)(2,1)} %get-tuple-element.133.own_ref, bf16[2,640,1280]{2,1,0:T(8,128)(2,1)} %collective-permute-done.26.got_ref, ...), custom_call_target="tpu_custom_call" | custom-call | tf_op jit(solution)/shard_map/turn/pallas_call | solution.py:658
  387.4 62.4 %attention_backward.2 = (bf16[640,768]{1,0:T(8,128)(2,1)}, bf16[4,3,640,128]{3,2,1,0:T(8,128)(2,1)}, bf16[4,3,640,128]{3,2,1,0:T(8,128)(2,1)}) custom-call(s32[241]{0:T(256)} %copy-done.21, bf16[20,640,128]{2,1,0:T(8,128)(2,1)} %get-tuple-element.108.q_ref, bf16[640,1280]{1,0:T(8,128)(2,1)} %get-tuple-element.136.da_ref, ...), custom_call_target="tpu_custom_call" | custom-call | flops 1000000 | bytes 10000 | tf_op jit(solution)/shard_map/attention_backward/pallas_call | solution.py:478
  449.7 12.5 %collective-permute-done.27 = bf16[320,1280]{1,0:T(8,128)(2,1)S(1)} collective-permute-done((bf16[320,1280]{1,0:T(8,128)(2,1)}, bf16[320,1280]{1,0:T(8,128)(2,1)S(1)}, u32[]{:S(2)}, u32[]{:S(2)}) %collective-permute-start.27) | collective-permute-done | bytes 819232 | tf_op jit(solution)/shard_map/ppermute | solution.py:774
  471.7 7.4 %collective-permute-start.36 = (bf16[4,2,40,1280]{3,2,1,0:T(8,128)(2,1)S(1)}, bf16[4,2,40,1280]{3,2,1,0:T(8,128)(2,1)S(1)}, u32[]{:S(2)}, u32[]{:S(2)}) collective-permute-start(bf16[4,2,40,1280]{3,2,1,0:T(8,128)(2,1)S(1)} %get-tuple-element.241), channel_id=1, source_target_pairs={{0,2},{1,3},{2,0},{3,1},{4,6},{5,7},{6,4},{7,5},{8,10},{9,11},{10,... | collective-permute-start | bytes 2457608 | tf_op jit(solution)/shard_map/ppermute | solution.py:774
  483.5 44.9 %attention_backward.3 = (bf16[640,512]{1,0:T(8,128)(2,1)}, bf16[4,2,640,128]{3,2,1,0:T(8,128)(2,1)}, bf16[4,2,640,128]{3,2,1,0:T(8,128)(2,1)}) custom-call(s32[241]{0:T(256)} %copy-done.21, bf16[20,640,128]{2,1,0:T(8,128)(2,1)} %get-tuple-element.108.q_ref, bf16[640,1280]{1,0:T(8,128)(2,1)} %get-tuple-element.136.da_ref, ...), custom_call_target="tpu_custom_call" | custom-call | flops 1000000 | bytes 10000 | tf_op jit(solution)/shard_map/attention_backward/pallas_call | solution.py:478
  536.5 8.8 %collective-permute-start.39 = (bf16[2,640,128]{2,1,0:T(8,128)(2,1)S(1)}, bf16[2,640,128]{2,1,0:T(8,128)(2,1)S(1)}, u32[]{:S(2)}, u32[]{:S(2)}) collective-permute-start(bf16[2,640,128]{2,1,0:T(8,128)(2,1)S(1)} %get-tuple-element.175), channel_id=1, source_target_pairs={{0,2},{1,3},{2,0},{3,1},{4,6},{5,7},{6,4},{7,5},{8,10},{9,11},{10,... | collective-permute-start | bytes 983048 | tf_op jit(solution)/shard_map/ppermute | solution.py:774
  546.9 6.9 %collective-permute-done.39.refs_7_ = bf16[2,640,128]{2,1,0:T(8,128)(2,1)S(1)} collective-permute-done((bf16[2,640,128]{2,1,0:T(8,128)(2,1)S(1)}, bf16[2,640,128]{2,1,0:T(8,128)(2,1)S(1)}, u32[]{:S(2)}, u32[]{:S(2)}) %collective-permute-start.39) | collective-permute-done | bytes 327712 | tf_op jit(solution)/shard_map/ppermute | solution.py:774
  553.8 10.9 %collective-permute-done.40.refs_8_ = bf16[2,640,128]{2,1,0:T(8,128)(2,1)S(1)} collective-permute-done((bf16[2,640,128]{2,1,0:T(8,128)(2,1)S(1)}, bf16[2,640,128]{2,1,0:T(8,128)(2,1)S(1)}, u32[]{:S(2)}, u32[]{:S(2)}) %collective-permute-start.40) | collective-permute-done | bytes 327712 | tf_op jit(solution)/shard_map/ppermute | solution.py:774
  564.7 17.0 %project_back.1 = (f32[640,1280]{1,0:T(8,128)}, bf16[1280,2048]{1,0:T(8,128)(2,1)}) custom-call(bf16[640,1280]{1,0:T(8,128)(2,1)} %pad_maximum_fusion.1.x_ref, bf16[640,1280]{1,0:T(8,128)(2,1)} %get-tuple-element.146.n_ref, bf16[640,768]{1,0:T(8,128)(2,1)} %get-tuple-element.147.dqa_ref, bf16[640,512]{1,0:T(8,128)(2,1)S(1)} %copy-done.17, ...), custom_call_target="tpu_custom_call" | custom-call | tf_op jit(solution)/shard_map/project_back/pallas_call | solution.py:725
  587.7 11.0 %collective-permute-done.43 = bf16[80,2304]{1,0:T(8,128)(2,1)S(1)} collective-permute-done((bf16[80,2304]{1,0:T(8,128)(2,1)S(1)}, bf16[80,2304]{1,0:T(8,128)(2,1)S(1)}, u32[]{:S(2)}, u32[]{:S(2)}) %collective-permute-start.43) | collective-permute-done | bytes 368672 | tf_op jit(solution)/shard_map/ppermute | solution.py:774
  614.5 7.4 %collective-permute-done.46 = bf16[2,40,1280]{2,1,0:T(8,128)(2,1)S(1)} collective-permute-done((bf16[2,40,1280]{2,1,0:T(8,128)(2,1)}, bf16[2,40,1280]{2,1,0:T(8,128)(2,1)S(1)}, u32[]{:S(2)}, u32[]{:S(2)}) %collective-permute-start.46) | collective-permute-done | bytes 204832 | tf_op jit(solution)/shard_map/ppermute | solution.py:774
  621.9 11.6 %collective-permute-done.48 = bf16[4,40,2048]{2,1,0:T(8,128)(2,1)} collective-permute-done((bf16[4,40,2048]{2,1,0:T(8,128)(2,1)}, bf16[4,40,2048]{2,1,0:T(8,128)(2,1)}, u32[]{:S(2)}, u32[]{:S(2)}) %collective-permute-start.48) | collective-permute-done | bytes 655392 | tf_op jit(solution)/shard_map/ppermute | solution.py:774
  647.0 11.3 %collective-permute-done.52 = bf16[40,2048]{1,0:T(8,128)(2,1)S(1)} collective-permute-done((bf16[40,2048]{1,0:T(8,128)(2,1)S(1)}, bf16[40,2048]{1,0:T(8,128)(2,1)S(1)}, u32[]{:S(2)}, u32[]{:S(2)}) %collective-permute-start.52) | collective-permute-done | bytes 163872 | tf_op jit(solution)/shard_map/ppermute | solution.py:774
  (329 shorter events, 148.1 us)
Async XLA Ops:
  7.2 231.3 %all-gather.3.cloned.1.call-start = ((), (), s32[]{:S(2)}) async-start(), calls=%async_computation.1 | async-start | bytes 10096640 | tf_op jit(solution)/shard_map/all_gather | solution.py:856
  14.5 291.9 %all-gather.5.cloned.1.call-start = ((), (), s32[]{:S(2)}) async-start(), calls=%async_computation.2 | async-start | bytes 6266880 | tf_op jit(solution)/shard_map/all_gather | solution.py:856
  19.9 586.6 %reduce-scatter.2.cloned.1.call-start = ((), (), s32[]{:S(2)}) async-start(), calls=%async_computation.3 | async-start | bytes 8355840 | tf_op jit(solution)/shard_map/reduce_scatter | solution.py:962
  29.4 68.0 %collective-permute-start.3 = (bf16[320,1280]{1,0:T(8,128)(2,1)S(1)}, bf16[320,1280]{1,0:T(8,128)(2,1)S(1)}, u32[]{:S(2)}, u32[]{:S(2)}) collective-permute-start(bf16[320,1280]{1,0:T(8,128)(2,1)S(1)} %get-tuple-element.248), channel_id=1, source_target_pairs={{0,7},{1,6},{2,5},{3,4},{4,3},{5,2},{6,1},{7,0},{8,15},{9,14},{10,... | collective-permute-start | bytes 2457608 | tf_op jit(solution)/shard_map/ppermute | solution.py:774
  52.4 43.2 %collective-permute-start.10 = (bf16[4,80,1024]{2,1,0:T(8,128)(2,1)S(1)}, bf16[4,80,1024]{2,1,0:T(8,128)(2,1)S(1)}, u32[]{:S(2)}, u32[]{:S(2)}) collective-permute-start(bf16[4,80,1024]{2,1,0:T(8,128)(2,1)S(1)} %pad_maximum_fusion.5.refs_0_), channel_id=1, source_target_pairs={{0,6},{1,7},{2,4},{3,5},{4,2},{5,3},{6,0},{7,1},{8,14},{9,15},{10,... | collective-permute-start | bytes 1966088 | tf_op jit(solution)/shard_map/ppermute | solution.py:774
  54.1 44.8 %collective-permute-start.11 = (bf16[4,80,1024]{2,1,0:T(8,128)(2,1)S(1)}, bf16[4,80,1024]{2,1,0:T(8,128)(2,1)S(1)}, u32[]{:S(2)}, u32[]{:S(2)}) collective-permute-start(bf16[4,80,1024]{2,1,0:T(8,128)(2,1)S(1)} %pad_maximum_fusion.5.refs_0_), channel_id=1, source_target_pairs={{0,1},{1,0},{2,3},{3,2},{4,5},{5,4},{6,7},{7,6},{8,9},{9,8},{10,11... | collective-permute-start | bytes 1966088 | tf_op jit(solution)/shard_map/ppermute | solution.py:774
  112.0 39.6 %collective-permute-start.16 = (bf16[5,656,128]{2,1,0:T(8,128)(2,1)}, bf16[5,656,128]{2,1,0:T(8,128)(2,1)S(1)}, u32[]{:S(2)}, u32[]{:S(2)}) collective-permute-start(bf16[5,656,128]{2,1,0:T(8,128)(2,1)} %get-tuple-element.111.refs_0_), channel_id=1, source_target_pairs={{0,2},{1,3},{2,0},{3,1},{4,6},{5,7},{6,4},{7,5},{8,10},{9,11},{10,... | collective-permute-start | bytes 2519048 | tf_op jit(solution)/shard_map/ppermute | solution.py:774
  113.4 42.1 %collective-permute-start.18 = (bf16[5,656,128]{2,1,0:T(8,128)(2,1)}, bf16[5,656,128]{2,1,0:T(8,128)(2,1)S(1)}, u32[]{:S(2)}, u32[]{:S(2)}) collective-permute-start(bf16[5,656,128]{2,1,0:T(8,128)(2,1)} %get-tuple-element.111.refs_0_), channel_id=1, source_target_pairs={{0,4},{1,5},{2,6},{3,7},{4,0},{5,1},{6,2},{7,3},{8,12},{9,13},{10,... | collective-permute-start | bytes 2519048 | tf_op jit(solution)/shard_map/ppermute | solution.py:774
  113.7 71.5 %collective-permute-start.20 = (bf16[5,656,128]{2,1,0:T(8,128)(2,1)}, bf16[5,656,128]{2,1,0:T(8,128)(2,1)S(1)}, u32[]{:S(2)}, u32[]{:S(2)}) collective-permute-start(bf16[5,656,128]{2,1,0:T(8,128)(2,1)} %get-tuple-element.111.refs_0_), channel_id=1, source_target_pairs={{0,6},{1,7},{2,4},{3,5},{4,2},{5,3},{6,0},{7,1},{8,14},{9,15},{10,... | collective-permute-start | bytes 2519048 | tf_op jit(solution)/shard_map/ppermute | solution.py:774
  115.8 70.3 %collective-permute-start.15 = (bf16[5,656,128]{2,1,0:T(8,128)(2,1)}, bf16[5,656,128]{2,1,0:T(8,128)(2,1)}, u32[]{:S(2)}, u32[]{:S(2)}) collective-permute-start(bf16[5,656,128]{2,1,0:T(8,128)(2,1)} %get-tuple-element.111.refs_0_), channel_id=1, source_target_pairs={{0,1},{1,0},{2,3},{3,2},{4,5},{5,4},{6,7},{7,6},{8,9},{9,8},{10,11... | collective-permute-start | bytes 2519048 | tf_op jit(solution)/shard_map/ppermute | solution.py:774
  151.6 34.5 %collective-permute-start.17 = (bf16[5,656,128]{2,1,0:T(8,128)(2,1)S(1)}, bf16[5,656,128]{2,1,0:T(8,128)(2,1)}, u32[]{:S(2)}, u32[]{:S(2)}) collective-permute-start(bf16[5,656,128]{2,1,0:T(8,128)(2,1)S(1)} %collective-permute-done.16.refs_2_), channel_id=1, source_target_pairs={{0,1},{1,0},{2,3},{3,2},{4,5},{5,4},{6,7},{7,6},{8,9},{9,8},{10,11... | collective-permute-start | bytes 2519048 | tf_op jit(solution)/shard_map/ppermute | solution.py:774
  155.4 30.7 %collective-permute-start.19 = (bf16[5,656,128]{2,1,0:T(8,128)(2,1)S(1)}, bf16[5,656,128]{2,1,0:T(8,128)(2,1)}, u32[]{:S(2)}, u32[]{:S(2)}) collective-permute-start(bf16[5,656,128]{2,1,0:T(8,128)(2,1)S(1)} %collective-permute-done.18.refs_4_), channel_id=1, source_target_pairs={{0,1},{1,0},{2,3},{3,2},{4,5},{5,4},{6,7},{7,6},{8,9},{9,8},{10,11... | collective-permute-start | bytes 2519048 | tf_op jit(solution)/shard_map/ppermute | solution.py:774
  190.4 46.8 %collective-permute-start.22 = (bf16[320,1280]{1,0:T(8,128)(2,1)}, bf16[320,1280]{1,0:T(8,128)(2,1)S(1)}, u32[]{:S(2)}, u32[]{:S(2)}) collective-permute-start(bf16[320,1280]{1,0:T(8,128)(2,1)} %get-tuple-element.246), channel_id=1, source_target_pairs={{0,7},{1,6},{2,5},{3,4},{4,3},{5,2},{6,1},{7,0},{8,15},{9,14},{10,... | collective-permute-start | bytes 2457608 | tf_op jit(solution)/shard_map/ppermute | solution.py:774
  352.2 111.3 %collective-permute-start.29 = (bf16[4,80,2304]{2,1,0:T(8,128)(2,1)}, bf16[4,80,2304]{2,1,0:T(8,128)(2,1)}, u32[]{:S(2)}, u32[]{:S(2)}) collective-permute-start(bf16[4,80,2304]{2,1,0:T(8,128)(2,1)} %get-tuple-element.225), channel_id=1, source_target_pairs={{0,2},{1,3},{2,0},{3,1},{4,6},{5,7},{6,4},{7,5},{8,10},{9,11},{10,... | collective-permute-start | bytes 4423688 | tf_op jit(solution)/shard_map/ppermute | solution.py:774
  364.4 99.1 %collective-permute-start.30 = (bf16[4,80,2304]{2,1,0:T(8,128)(2,1)}, bf16[4,80,2304]{2,1,0:T(8,128)(2,1)}, u32[]{:S(2)}, u32[]{:S(2)}) collective-permute-start(bf16[4,80,2304]{2,1,0:T(8,128)(2,1)} %get-tuple-element.224), channel_id=1, source_target_pairs={{0,4},{1,5},{2,6},{3,7},{4,0},{5,1},{6,2},{7,3},{8,12},{9,13},{10,... | collective-permute-start | bytes 4423688 | tf_op jit(solution)/shard_map/ppermute | solution.py:774
  364.4 99.1 %collective-permute-start.31 = (bf16[4,80,2304]{2,1,0:T(8,128)(2,1)}, bf16[4,80,2304]{2,1,0:T(8,128)(2,1)}, u32[]{:S(2)}, u32[]{:S(2)}) collective-permute-start(bf16[4,80,2304]{2,1,0:T(8,128)(2,1)} %get-tuple-element.223), channel_id=1, source_target_pairs={{0,6},{1,7},{2,4},{3,5},{4,2},{5,3},{6,0},{7,1},{8,14},{9,15},{10,... | collective-permute-start | bytes 4423688 | tf_op jit(solution)/shard_map/ppermute | solution.py:774
  384.7 78.8 %collective-permute-start.28 = (bf16[4,4,40,1280]{3,2,1,0:T(8,128)(2,1)S(1)}, bf16[4,4,40,1280]{3,2,1,0:T(8,128)(2,1)}, u32[]{:S(2)}, u32[]{:S(2)}) collective-permute-start(bf16[4,4,40,1280]{3,2,1,0:T(8,128)(2,1)S(1)} %get-tuple-element.232), channel_id=1, source_target_pairs={{0,1},{1,0},{2,3},{3,2},{4,5},{5,4},{6,7},{7,6},{8,9},{9,8},{10,11... | collective-permute-start | bytes 4915208 | tf_op jit(solution)/shard_map/ppermute | solution.py:774
  385.9 76.4 %collective-permute-start.27 = (bf16[320,1280]{1,0:T(8,128)(2,1)}, bf16[320,1280]{1,0:T(8,128)(2,1)S(1)}, u32[]{:S(2)}, u32[]{:S(2)}) collective-permute-start(bf16[320,1280]{1,0:T(8,128)(2,1)} %get-tuple-element.244), channel_id=1, source_target_pairs={{0,7},{1,6},{2,5},{3,4},{4,3},{5,2},{6,1},{7,0},{8,15},{9,14},{10,... | collective-permute-start | bytes 2457608 | tf_op jit(solution)/shard_map/ppermute | solution.py:774
  471.7 59.9 %collective-permute-start.36 = (bf16[4,2,40,1280]{3,2,1,0:T(8,128)(2,1)S(1)}, bf16[4,2,40,1280]{3,2,1,0:T(8,128)(2,1)S(1)}, u32[]{:S(2)}, u32[]{:S(2)}) collective-permute-start(bf16[4,2,40,1280]{3,2,1,0:T(8,128)(2,1)S(1)} %get-tuple-element.241), channel_id=1, source_target_pairs={{0,2},{1,3},{2,0},{3,1},{4,6},{5,7},{6,4},{7,5},{8,10},{9,11},{10,... | collective-permute-start | bytes 2457608 | tf_op jit(solution)/shard_map/ppermute | solution.py:774
  480.0 51.6 %collective-permute-start.37 = (bf16[2,80,2304]{2,1,0:T(8,128)(2,1)}, bf16[2,80,2304]{2,1,0:T(8,128)(2,1)S(1)}, u32[]{:S(2)}, u32[]{:S(2)}) collective-permute-start(bf16[2,80,2304]{2,1,0:T(8,128)(2,1)} %get-tuple-element.249), channel_id=1, source_target_pairs={{0,16},{1,17},{2,18},{3,19},{4,20},{5,21},{6,22},{7,23},{8,24},{9,... | collective-permute-start | bytes 2211848 | tf_op jit(solution)/shard_map/ppermute | solution.py:774
  480.0 48.5 %collective-permute-start.33 = (bf16[3,640,128]{2,1,0:T(8,128)(2,1)}, bf16[3,640,128]{2,1,0:T(8,128)(2,1)S(1)}, u32[]{:S(2)}, u32[]{:S(2)}) collective-permute-start(bf16[3,640,128]{2,1,0:T(8,128)(2,1)} %get-tuple-element.160), channel_id=1, source_target_pairs={{0,2},{1,3},{2,0},{3,1},{4,6},{5,7},{6,4},{7,5},{8,10},{9,11},{10,... | collective-permute-start | bytes 1474568 | tf_op jit(solution)/shard_map/ppermute | solution.py:774
  480.0 48.5 %collective-permute-start.34 = (bf16[3,640,128]{2,1,0:T(8,128)(2,1)}, bf16[3,640,128]{2,1,0:T(8,128)(2,1)S(1)}, u32[]{:S(2)}, u32[]{:S(2)}) collective-permute-start(bf16[3,640,128]{2,1,0:T(8,128)(2,1)} %get-tuple-element.161), channel_id=1, source_target_pairs={{0,4},{1,5},{2,6},{3,7},{4,0},{5,1},{6,2},{7,3},{8,12},{9,13},{10,... | collective-permute-start | bytes 1474568 | tf_op jit(solution)/shard_map/ppermute | solution.py:774
  481.4 50.1 %collective-permute-start.35 = (bf16[3,640,128]{2,1,0:T(8,128)(2,1)}, bf16[3,640,128]{2,1,0:T(8,128)(2,1)S(1)}, u32[]{:S(2)}, u32[]{:S(2)}) collective-permute-start(bf16[3,640,128]{2,1,0:T(8,128)(2,1)} %get-tuple-element.162), channel_id=1, source_target_pairs={{0,6},{1,7},{2,4},{3,5},{4,2},{5,3},{6,0},{7,1},{8,14},{9,15},{10,... | collective-permute-start | bytes 1474568 | tf_op jit(solution)/shard_map/ppermute | solution.py:774
  603.1 30.5 %collective-permute-start.48 = (bf16[4,40,2048]{2,1,0:T(8,128)(2,1)}, bf16[4,40,2048]{2,1,0:T(8,128)(2,1)}, u32[]{:S(2)}, u32[]{:S(2)}) collective-permute-start(bf16[4,40,2048]{2,1,0:T(8,128)(2,1)} %get-tuple-element.235), channel_id=1, source_target_pairs={{0,4},{1,5},{2,6},{3,7},{4,0},{5,1},{6,2},{7,3},{8,12},{9,13},{10,... | collective-permute-start | bytes 1966088 | tf_op jit(solution)/shard_map/ppermute | solution.py:774
  (82 other events, 1495.4 us)
Sparse Core Ops, SparseCore 0:
  14.6 189.1 all-gather.2
  207.2 91.1 all-gather.4
  347.5 227.1 reduce-scatter.1

commit v4 on v3

--- a/solution.py
+++ b/solution.py
@@ -24,7 +24,7 @@
 BK = 256
 STACK = GROUP * BQ
 FF_BLOCK = 256
-FF_STEPS = (4, 3)
+FF_STEPS = (3, 4)
 HEAD_PARTS = ((0, 3), (3, 2))
 
 EPSILON = 1e-05
@@ -84,9 +84,22 @@
     return copies
 
 
-def project_kernel(place_ref, x_ref, cos_ref, sin_ref, *refs):
-    piece_refs, (n_ref, q_ref, kv_ref, gain_ref, w_ref, top_ref, sems) = refs[:-7], refs[-7:]
-    for copy in assembly(place_ref, piece_refs, w_ref, sems):
+def square_sums(rows):
+    shape = (LANES, LANES)
+    same = (lax.broadcasted_iota(jnp.int32, shape, 0) < HEAD) == (lane_iota(shape) < HEAD)
+    same = jnp.where(same, 1.0, 0.0).astype(BF16)
+
+    def squares(z):
+        sums = dot((z * z).astype(BF16), same)
+        return jnp.max(sums.reshape(rows // 8, 8, LANES), axis=0)
+
+    return squares
+
+
+def project_keys_kernel(place_ref, x_ref, cos_ref, sin_ref, *refs):
+    piece_refs, (n_ref, kv_ref, gain_ref, w_ref, sems) = refs[:-5], refs[-5:]
+    copies = assembly(place_ref, piece_refs, w_ref, sems)
+    for copy in copies:
         copy.wait()
     gains = w_ref[:, QKV:].astype(F32).T
     gain_ref[...] = gains[:8, :]
@@ -104,54 +117,70 @@
     lane = lane_iota((rows, LANES))
     low = (lane % HEAD) < HEAD // 2
     left = lane < HEAD
-    cos = cos_ref[...]
-    sin = sin_ref[...]
-    same = (lax.broadcasted_iota(jnp.int32, (LANES, LANES), 0) < HEAD) == left[:LANES]
-    same = jnp.where(same, 1.0, 0.0).astype(BF16)
-
-    def squares(z):
-        sums = dot((z * z).astype(BF16), same)
-        return jnp.max(sums.reshape(rows // 8, 8, LANES), axis=0)
-
-    q_top = jnp.zeros((8, LANES), F32)
-    k_top = jnp.zeros((8, LANES), F32)
+    squares = square_sums(rows)
+    tops = jnp.zeros((8, LANES), F32)
+    columns = [w_ref[:, (g + 1) * GROUP_COLS - LANES : (g + 1) * GROUP_COLS] for g in range(KV_HEADS)]
+    z = dot(n_ref[...], jnp.concatenate(columns, axis=1))
     for g in range(KV_HEADS):
-        z = dot(n_ref[...], w_ref[:, g * GROUP_COLS : (g + 1) * GROUP_COLS])
+        zk = z[:, g * LANES : (g + 1) * LANES]
+        rot = zk * cos_ref[...] + half_turn(zk, low) * sin_ref[...]
+        tops = jnp.maximum(tops, squares(rot))
+        kv_ref[g, :rows] = jnp.where(left, rot, zk).astype(BF16)
+    top = jnp.max(jnp.where(left[:8], tops, 0.0)) * 1.02
+    kv_ref[:, rows:] = jnp.full((KV_HEADS, 16, LANES), top, F32).astype(BF16)
+
+
+def project_keys(place, x, cos, sin, pieces):
+    rows = x.shape[0]
+    count = sum(p.shape[0] for p in pieces)
+    return pl.pallas_call(
+        project_keys_kernel,
+        out_shape=[
+            jax.ShapeDtypeStruct((rows, D), BF16),
+            jax.ShapeDtypeStruct((KV_HEADS, rows + 16, LANES), BF16),
+            jax.ShapeDtypeStruct((8, D), F32),
+            jax.ShapeDtypeStruct((D, QKV_PAD), BF16),
+        ],
+        in_specs=[SMEM_SPACE] + [VMEM_SPACE] * 3 + [ANY_SPACE] * len(pieces),
+        out_specs=[VMEM_SPACE] * 4,
+        scratch_shapes=[pltpu.SemaphoreType.DMA((count,))],
+        compiler_params=params(48),
+        name="project_keys",
+    )(place, x, cos, sin, *pieces)
+
+
+def project_queries_kernel(n_ref, w_ref, cos_ref, sin_ref, q_ref, top_ref):
+    rows = n_ref.shape[0]
+    lane = lane_iota((rows, LANES))
+    low = (lane % HEAD) < HEAD // 2
+    left = lane < HEAD
+    squares = square_sums(rows)
+    tops = jnp.zeros((8, LANES), F32)
+    for g in range(KV_HEADS):
+        z = dot(n_ref[...], w_ref[:, g * GROUP_COLS : (g + 1) * GROUP_COLS - LANES])
         for pair in range(GROUP // 2):
             zp = z[:, pair * LANES : (pair + 1) * LANES]
-            rot = (zp * cos + half_turn(zp, low) * sin).astype(BF16).astype(F32)
-            q_top = jnp.maximum(q_top, squares(rot))
+            rot = zp * cos_ref[...] + half_turn(zp, low) * sin_ref[...]
+            rot = rot.astype(BF16).astype(F32)
+            tops = jnp.maximum(tops, squares(rot))
             head = g * GROUP + 2 * pair
             q_ref[head] = jnp.where(left, rot, 0.0).astype(BF16)
             q_ref[head + 1] = jnp.where(left, pltpu.roll(rot, HEAD, 1), 0.0).astype(BF16)
-        zk = z[:, GROUP * HEAD :]
-        rot = zk * cos + half_turn(zk, low) * sin
-        k_top = jnp.maximum(k_top, squares(rot))
-        kv_ref[g, :rows] = jnp.where(left, rot, zk).astype(BF16)
-    top_ref[...] = q_top
-    k_top = jnp.max(jnp.where(left[:8], k_top, 0.0)) * 1.02
-    kv_ref[:, rows:] = jnp.full((KV_HEADS, 16, LANES), k_top, F32).astype(BF16)
-
-
-def project(place, x, cos, sin, pieces):
-    rows = x.shape[0]
-    count = sum(p.shape[0] for p in pieces)
+    top_ref[...] = tops
+
+
+def project_queries(n, w, cos, sin):
+    rows = n.shape[0]
     return pl.pallas_call(
-        project_kernel,
+        project_queries_kernel,
         out_shape=[
-            jax.ShapeDtypeStruct((rows, D), BF16),
             jax.ShapeDtypeStruct((HEADS, rows, LANES), BF16),
-            jax.ShapeDtypeStruct((KV_HEADS, rows + 16, LANES), BF16),
-            jax.ShapeDtypeStruct((8, D), F32),
-            jax.ShapeDtypeStruct((D, QKV_PAD), BF16),
             jax.ShapeDtypeStruct((8, LANES), F32),
         ],
-        in_specs=[SMEM_SPACE] + [VMEM_SPACE] * 3 + [ANY_SPACE] * len(pieces),
-        out_specs=[VMEM_SPACE] * 6,
-        scratch_shapes=[pltpu.SemaphoreType.DMA((count,))],
         compiler_params=params(48),
-        name="project",
-    )(place, x, cos, sin, *pieces)
+        cost_estimate=SMALL,
+        name="project_queries",
+    )(n, w, cos, sin)
 
 
 def first_row(device, half, rows, span):
@@ -942,12 +971,15 @@
     meta = jnp.concatenate([block[None], *counts, listed.reshape(steps * tiles)])
     seg_row = tree_seg[None, :]
 
-    normed1, q, kv, gains, qkv_w, q_top = project(qkv_place, tokens_in, cos, sin, qkv_pieces)
-    kvs = [kv, swap(kv, 1)]
-    for c in range(1, chips):
-        piece = swap(kv, 2 * c)
+    normed1, kv, gains, qkv_w = project_keys(qkv_place, tokens_in, cos, sin, qkv_pieces)
+    kv_near = swap(kv, 1)
+    kv_far = [swap(kv, 2 * c) for c in range(1, chips)]
+    q, q_top = project_queries(normed1, qkv_w, cos, sin)
+    q, kv_near, *kv_far = stage(q, kv_near, *kv_far)
+    kvs = [kv, kv_near]
+    for piece in kv_far:
         kvs += [piece, swap(piece, 1)]
-    out_grad, *kvs = stage(out_grad, *kvs)
+    out_grad, q, *kvs = stage(out_grad, q, *kvs)
     grads_in = even_out(out_grad)
     att, lse = attention_forward(meta, q, q_top, kvs, info, seg_row)
     att, grads_in = stage(att, grads_in)
@@ -958,13 +990,13 @@
     mid, normed2, out_w = middle(tokens_in, att, gains, [out_w, swap(out_w, 1)], out_place)
     normed2_far = swap(normed2, 1)
     tokens = (normed2, normed2_far, grads_in, og_far)
-    *sums, ff_dw = feed_forward(FF_STEPS[0], *tokens, ff_w[0])
+    *sums, next_dw = feed_forward(FF_STEPS[0], *tokens, ff_w[0])
+    next_dw = send_chips(next_dw.reshape(trees, chips, 2 * shard, next_dw.shape[1]))
+    ff_w[1], *sums = stage(ff_w[1], *sums)
+    *sums, ff_dw = feed_forward(FF_STEPS[1], *tokens, ff_w[1], sums)
     ff_dw = lax.psum_scatter(
         ff_dw, "fsdp", scatter_dimension=0, tiled=True, axis_index_groups=same_core
     )
-    ff_w[1], *sums = stage(ff_w[1], *sums)
-    *sums, next_dw = feed_forward(FF_STEPS[1], *tokens, ff_w[1], sums)
-    next_dw = send_chips(next_dw.reshape(trees, chips, 2 * shard, next_dw.shape[1]))
     own, far = sums
     layer_out, grad_mid, da, out_dw, dgain2 = turn(
         mid, own, swap(far, 1), grads_in, gains, out_w, att
@@ -1008,7 +1040,7 @@
     out_dw, values = add16(values[:2]), values[2:]
     next_dw, qkv_dw = add16(values[: len(next_dw)]), add16(values[len(next_dw) :])
     qkv_dw = send_chips(qkv_dw)
-    ff_dw = jnp.concatenate([ff_dw, next_dw], axis=1).reshape(2, shard, -1)
+    ff_dw = jnp.concatenate([next_dw, ff_dw], axis=1).reshape(2, shard, -1)
     ff_dw = halve(ff_dw, core, 0, 1)
     out_dw = trees_first(out_dw)
     input_grad = input_gradient(tokens_in, grad_mid, dn, gains)

time: 681 us -> 669 us (0.982)
  waiting for transfers between devices: 217 us -> 204 us
    ppermute x55, waiting for transfers between devices: 217 us -> 197 us  [swap(): return lax.ppermute(v, 'fsdp', [(i, i ^ bit) for i in range(size)])]
    all_gather x2, waiting for transfers between devices: 0.01 us -> 7.25 us  [body(): lax.all_gather(chip_rows[:, first:last], 'fsdp', tiled=True, axis_index_g...]
    pallas_call x1 -> x2, Pallas kernels: 13 us -> 16.6 us  [the longest x1 8.57 us: project_keys(): pl.pallas_call(project_keys_kernel, out_shape=[jax.ShapeDtypeStruct((rows...]
    unnamed x102 -> x120, local copies, waits for them, and re-layouts: 14.6 us -> 16.2 us
  transfers between devices with their start and end apart: 58 -> 58, of which waited for: 23 -> 23; matrix products, arithmetic and copies ran while one was open for 9% -> 10% of each run, Pallas kernels for 37% -> 36%
where the time goes in v4:
time: 669 us; the launch traced here: 659 us
  Pallas kernels  286 us (43%)
  waiting for transfers between devices  204 us (30%)
  starting transfers between devices  67.4 us (10%)
  local copies, waits for them, and re-layouts  49.4 us (7%)
  other arithmetic  36.9 us (6%)
  between operations  15 us (2%)
    ppermute x55, waiting for transfers between devices, swap(): return lax.ppermute(v, 'fsdp', [(i, i ^ bit) for i in range(size)])  197 us
    pallas_call x2, Pallas kernels, attention_backward(): pl.pallas_call(functools.partial(backward_kernel, tiles=tiles, span=span,...  103 us
    pallas_call x2, Pallas kernels, feed_forward(): pl.pallas_call(functools.partial(feed_forward_kernel, later=bool(priors))...  86.4 us
    ppermute x55, starting transfers between devices, swap(): return lax.ppermute(v, 'fsdp', [(i, i ^ bit) for i in range(size)])  67.2 us
    pallas_call x1, Pallas kernels, attention_forward(): pl.pallas_call(functools.partial(forward_kernel, tiles=tiles, span=span),...  41 us
    pallas_call x1, Pallas kernels, project_back(): pl.pallas_call(kernel, out_shape=[jax.ShapeDtypeStruct((rows, D), F32), j...  17 us
    pallas_call x1, Pallas kernels, turn(): pl.pallas_call(turn_kernel, out_shape=[jax.ShapeDtypeStruct((rows, D), BF...  16.4 us
    squeeze x12, local copies, waits for them, and re-layouts, part(): return lax.dynamic_index_in_dim(v, index, axis, keepdims=False)  16.2 us
  transfers between devices with their start and end apart: 58, of which 23 were waited for; matrix products, arithmetic and copies ran while one was open for 10% of the time, Pallas kernels for 36%

profile of v4, /device:TPU:0, one launch (start us, length us, event | category | flops | bytes accessed | tf_op | source)
XLA Modules:
  0.0 658.7 jit_solution(6196289985361803385)
XLA Ops:
  32.7 10.9 %collective-permute-done.5 = bf16[80,1024]{1,0:T(8,128)(2,1)S(1)} collective-permute-done((bf16[80,1024]{1,0:T(8,128)(2,1)S(1)}, bf16[80,1024]{1,0:T(8,128)(2,1)S(1)}, u32[]{:S(2)}, u32[]{:S(2)}) %collective-permute-start.5) | collective-permute-done | bytes 163872 | tf_op jit(solution)/shard_map/ppermute | solution.py:803
  43.6 8.1 %collective-permute-done.6 = bf16[80,1024]{1,0:T(8,128)(2,1)S(1)} collective-permute-done((bf16[80,1024]{1,0:T(8,128)(2,1)S(1)}, bf16[80,1024]{1,0:T(8,128)(2,1)S(1)}, u32[]{:S(2)}, u32[]{:S(2)}) %collective-permute-start.6) | collective-permute-done | bytes 163872 | tf_op jit(solution)/shard_map/ppermute | solution.py:803
  56.5 24.2 %collective-permute-done.8.refs_1_ = bf16[4,80,1024]{2,1,0:T(8,128)(2,1)S(1)} collective-permute-done((bf16[4,80,1024]{2,1,0:T(8,128)(2,1)S(1)}, bf16[4,80,1024]{2,1,0:T(8,128)(2,1)S(1)}, u32[]{:S(2)}, u32[]{:S(2)}) %collective-permute-start.8) | collective-permute-done | bytes 655392 | tf_op jit(solution)/shard_map/ppermute | solution.py:803
  81.1 14.4 %collective-permute-done.10.refs_3_ = bf16[4,80,1024]{2,1,0:T(8,128)(2,1)S(1)} collective-permute-done((bf16[4,80,1024]{2,1,0:T(8,128)(2,1)S(1)}, bf16[4,80,1024]{2,1,0:T(8,128)(2,1)S(1)}, u32[]{:S(2)}, u32[]{:S(2)}) %collective-permute-start.10) | collective-permute-done | bytes 655392 | tf_op jit(solution)/shard_map/ppermute | solution.py:803
  98.9 8.6 %project_keys.1 = (bf16[640,1280]{1,0:T(8,128)(2,1)}, bf16[5,656,128]{2,1,0:T(8,128)(2,1)}, f32[8,1280]{1,0:T(8,128)S(1)}, bf16[1280,2048]{1,0:T(8,128)(2,1)}) custom-call(s32[40]{0:T(128)S(1)} %concatenate.86.place_ref, bf16[640,1280]{1,0:T(8,128)(2,1)} %pad_maximum_fusion.1.x_ref, f32[640,128]{1,0:T(8,128)S(1)} %get-tuple-element.319.cos_ref.refs_12_, ...), custom_call_target="tpu_custom_call" | custom-call | tf_op jit(solution)/shard_map/project_keys/pallas_call | solution.py:136
  114.6 8.0 %project_queries.1 = (bf16[20,640,128]{2,1,0:T(8,128)(2,1)S(1)}, f32[8,128]{1,0:T(8,128)S(1)}) custom-call(bf16[640,1280]{1,0:T(8,128)(2,1)S(1)} %copy-done.10, bf16[1280,2048]{1,0:T(8,128)(2,1)} %get-tuple-element.115.w_ref.refs_10_, f32[640,128]{1,0:T(8,128)S(1)} %get-tuple-element.319.cos_ref.refs_12_, f32[640,128]{1,0:T(8,128)S(1)} %get-tuple-element.318.sin_ref.refs_13_), custom_call_target="tpu_custom_call" | custom-call | flops 1000000 | bytes 10000 | tf_op jit(solution)/shard_map/project_queries/pallas_call | solution.py:174
  124.4 23.2 %collective-permute-done.16.refs_2_ = bf16[5,656,128]{2,1,0:T(8,128)(2,1)S(1)} collective-permute-done((bf16[5,656,128]{2,1,0:T(8,128)(2,1)}, bf16[5,656,128]{2,1,0:T(8,128)(2,1)S(1)}, u32[]{:S(2)}, u32[]{:S(2)}) %collective-permute-start.16) | collective-permute-done | bytes 839712 | tf_op jit(solution)/shard_map/ppermute | solution.py:803
  147.5 18.7 %collective-permute-done.18.refs_6_ = bf16[5,656,128]{2,1,0:T(8,128)(2,1)} collective-permute-done((bf16[5,656,128]{2,1,0:T(8,128)(2,1)}, bf16[5,656,128]{2,1,0:T(8,128)(2,1)}, u32[]{:S(2)}, u32[]{:S(2)}) %collective-permute-start.18) | collective-permute-done | bytes 839712 | tf_op jit(solution)/shard_map/ppermute | solution.py:803
  176.6 41.0 %attention_forward.1 = (bf16[640,1280]{1,0:T(8,128)(2,1)}, f32[640,128]{1,0:T(8,128)S(1)}) custom-call(s32[241]{0:T(256)S(1)} %fusion.26.meta_ref, bf16[20,640,128]{2,1,0:T(8,128)(2,1)} %copy-done.2, f32[8,128]{1,0:T(8,128)S(1)} %get-tuple-element.124.top_ref, bf16[5,656,128]{2,1,0:T(8,128)(2,1)S(1)} %copy-done.9, bf16[5,656,128]{2,1,0:T(8,128)(2,1)} %copy-done.24, ...), custom_call_target="tpu_custom_call" | custom-call | flops 1000000 | bytes 10000 | tf_op jit(solution)/shard_map/attention_forward/pallas_call | solution.py:366
  220.7 8.1 %collective-permute-start.23 = (bf16[1,1280,640]{2,1,0:T(8,128)(2,1)S(1)}, bf16[1,1280,640]{2,1,0:T(8,128)(2,1)S(1)}, u32[]{:S(2)}, u32[]{:S(2)}) collective-permute-start(bf16[1,1280,640]{2,1,0:T(8,128)(2,1)S(1)} %slice_bitcast_fusion.refs_0_), channel_id=1, source_target_pairs={{0,1},{1,0},{2,3},{3,2},{4,5},{5,4},{6,7},{7,6},{8,9},{9,8},{10,11... | collective-permute-start | bytes 4915208 | tf_op jit(solution)/shard_map/ppermute | solution.py:803
  246.5 37.1 %feed_forward.2 = (bf16[2,640,1280]{2,1,0:T(8,128)(2,1)}, bf16[2,640,1280]{2,1,0:T(8,128)(2,1)}, bf16[1280,2304]{1,0:T(8,128)(2,1)}) custom-call(bf16[640,1280]{1,0:T(8,128)(2,1)} %copy-done.11, bf16[640,1280]{1,0:T(8,128)(2,1)} %copy-done.27, bf16[640,1280]{1,0:T(8,128)(2,1)} %pad_maximum_fusion.2.og1_ref.og_ref, ...), custom_call_target="tpu_custom_call" | custom-call | flops 1000000 | bytes 10000 | tf_op jit(solution)/shard_map/feed_forward/pallas_call | solution.py:631
  283.6 7.3 %all-gather.5.cloned.1.call-done.wg_ref.wu_ref.wd_ref = bf16[1280,3072]{1,0:T(8,128)(2,1)} async-done(((bf16[80,3072]{1,0:T(8,128)(2,1)}), bf16[1280,3072]{1,0:T(8,128)(2,1)}) %all-gather.5.cloned.1.call-update) | async-done | bytes 7864336 | tf_op jit(solution)/shard_map/all_gather | solution.py:885
  290.8 49.4 %feed_forward.3 = (bf16[2,640,1280]{2,1,0:T(8,128)(2,1)}, bf16[2,640,1280]{2,1,0:T(8,128)(2,1)}, bf16[1280,3072]{1,0:T(8,128)(2,1)}) custom-call(bf16[640,1280]{1,0:T(8,128)(2,1)} %copy-done.11, bf16[640,1280]{1,0:T(8,128)(2,1)} %copy-done.27, bf16[640,1280]{1,0:T(8,128)(2,1)} %pad_maximum_fusion.2.og1_ref.og_ref, ...), custom_call_target="tpu_custom_call" | custom-call | flops 1000000 | bytes 10000 | tf_op jit(solution)/shard_map/feed_forward/pallas_call | solution.py:631
  348.7 16.4 %turn.1 = (bf16[640,1280]{1,0:T(8,128)(2,1)}, f32[640,1280]{1,0:T(8,128)}, bf16[640,1280]{1,0:T(8,128)(2,1)}, bf16[1280,1280]{1,0:T(8,128)(2,1)}, f32[8,1280]{1,0:T(8,128)}) custom-call(f32[640,1280]{1,0:T(8,128)} %copy-done.13, bf16[2,640,1280]{2,1,0:T(8,128)(2,1)} %get-tuple-element.147.own_ref, bf16[2,640,1280]{2,1,0:T(8,128)(2,1)} %collective-permute-done.26.got_ref, ...), custom_call_target="tpu_custom_call" | custom-call | tf_op jit(solution)/shard_map/turn/pallas_call | solution.py:687
  370.2 59.6 %attention_backward.2 = (bf16[640,768]{1,0:T(8,128)(2,1)}, bf16[4,3,640,128]{3,2,1,0:T(8,128)(2,1)}, bf16[4,3,640,128]{3,2,1,0:T(8,128)(2,1)}) custom-call(s32[241]{0:T(256)} %copy-done.23, bf16[20,640,128]{2,1,0:T(8,128)(2,1)} %copy-done.2, bf16[640,1280]{1,0:T(8,128)(2,1)} %get-tuple-element.150.da_ref, bf16[640,1280]{1,0:T(8,128)(2,1)} %get-tuple-element.136.att_ref, ...), custom_call_target="tpu_custom_call" | custom-call | flops 1000000 | bytes 10000 | tf_op jit(solution)/shard_map/attention_backward/pallas_call | solution.py:507
  429.8 23.2 %collective-permute-done.27 = bf16[320,1280]{1,0:T(8,128)(2,1)S(1)} collective-permute-done((bf16[320,1280]{1,0:T(8,128)(2,1)}, bf16[320,1280]{1,0:T(8,128)(2,1)S(1)}, u32[]{:S(2)}, u32[]{:S(2)}) %collective-permute-start.27) | collective-permute-done | bytes 819232 | tf_op jit(solution)/shard_map/ppermute | solution.py:803
  468.8 43.2 %attention_backward.3 = (bf16[640,512]{1,0:T(8,128)(2,1)}, bf16[4,2,640,128]{3,2,1,0:T(8,128)(2,1)}, bf16[4,2,640,128]{3,2,1,0:T(8,128)(2,1)}) custom-call(s32[241]{0:T(256)} %copy-done.23, bf16[20,640,128]{2,1,0:T(8,128)(2,1)} %copy-done.2, bf16[640,1280]{1,0:T(8,128)(2,1)} %get-tuple-element.150.da_ref, bf16[640,1280]{1,0:T(8,128)(2,1)} %get-tuple-element.136.att_ref, ...), custom_call_target="tpu_custom_call" | custom-call | flops 1000000 | bytes 10000 | tf_op jit(solution)/shard_map/attention_backward/pallas_call | solution.py:507
  522.6 11.1 %collective-permute-start.39 = (bf16[2,640,128]{2,1,0:T(8,128)(2,1)S(1)}, bf16[2,640,128]{2,1,0:T(8,128)(2,1)S(1)}, u32[]{:S(2)}, u32[]{:S(2)}) collective-permute-start(bf16[2,640,128]{2,1,0:T(8,128)(2,1)S(1)} %get-tuple-element.188), channel_id=1, source_target_pairs={{0,2},{1,3},{2,0},{3,1},{4,6},{5,7},{6,4},{7,5},{8,10},{9,11},{10,... | collective-permute-start | bytes 983048 | tf_op jit(solution)/shard_map/ppermute | solution.py:803
  535.3 9.7 %collective-permute-done.39.refs_7_ = bf16[2,640,128]{2,1,0:T(8,128)(2,1)S(1)} collective-permute-done((bf16[2,640,128]{2,1,0:T(8,128)(2,1)S(1)}, bf16[2,640,128]{2,1,0:T(8,128)(2,1)S(1)}, u32[]{:S(2)}, u32[]{:S(2)}) %collective-permute-start.39) | collective-permute-done | bytes 327712 | tf_op jit(solution)/shard_map/ppermute | solution.py:803
  552.0 17.0 %project_back.1 = (f32[640,1280]{1,0:T(8,128)}, bf16[1280,2048]{1,0:T(8,128)(2,1)}) custom-call(bf16[640,1280]{1,0:T(8,128)(2,1)} %pad_maximum_fusion.1.x_ref, bf16[640,1280]{1,0:T(8,128)(2,1)} %get-tuple-element.114.n_ref, bf16[640,768]{1,0:T(8,128)(2,1)} %get-tuple-element.160.dqa_ref, bf16[640,512]{1,0:T(8,128)(2,1)S(1)} %copy-done.19, ...), custom_call_target="tpu_custom_call" | custom-call | tf_op jit(solution)/shard_map/project_back/pallas_call | solution.py:754
  575.2 10.7 %collective-permute-done.43 = bf16[80,2304]{1,0:T(8,128)(2,1)S(1)} collective-permute-done((bf16[80,2304]{1,0:T(8,128)(2,1)S(1)}, bf16[80,2304]{1,0:T(8,128)(2,1)S(1)}, u32[]{:S(2)}, u32[]{:S(2)}) %collective-permute-start.43) | collective-permute-done | bytes 368672 | tf_op jit(solution)/shard_map/ppermute | solution.py:803
  601.8 7.4 %collective-permute-done.46 = bf16[2,40,1280]{2,1,0:T(8,128)(2,1)S(1)} collective-permute-done((bf16[2,40,1280]{2,1,0:T(8,128)(2,1)}, bf16[2,40,1280]{2,1,0:T(8,128)(2,1)S(1)}, u32[]{:S(2)}, u32[]{:S(2)}) %collective-permute-start.46) | collective-permute-done | bytes 204832 | tf_op jit(solution)/shard_map/ppermute | solution.py:803
  609.2 12.8 %collective-permute-done.48 = bf16[4,40,2048]{2,1,0:T(8,128)(2,1)} collective-permute-done((bf16[4,40,2048]{2,1,0:T(8,128)(2,1)}, bf16[4,40,2048]{2,1,0:T(8,128)(2,1)}, u32[]{:S(2)}, u32[]{:S(2)}) %collective-permute-start.48) | collective-permute-done | bytes 655392 | tf_op jit(solution)/shard_map/ppermute | solution.py:803
  635.5 11.3 %collective-permute-done.52 = bf16[40,2048]{1,0:T(8,128)(2,1)S(1)} collective-permute-done((bf16[40,2048]{1,0:T(8,128)(2,1)S(1)}, bf16[40,2048]{1,0:T(8,128)(2,1)S(1)}, u32[]{:S(2)}, u32[]{:S(2)}) %collective-permute-start.52) | collective-permute-done | bytes 163872 | tf_op jit(solution)/shard_map/ppermute | solution.py:803
  (348 shorter events, 162.4 us)
Async XLA Ops:
  7.2 211.7 %all-gather.3.cloned.1.call-start = ((), (), s32[]{:S(2)}) async-start(), calls=%async_computation.1 | async-start | bytes 8007680 | tf_op jit(solution)/shard_map/all_gather | solution.py:885
  14.4 276.4 %all-gather.5.cloned.1.call-start = ((), (), s32[]{:S(2)}) async-start(), calls=%async_computation.2 | async-start | bytes 8355840 | tf_op jit(solution)/shard_map/all_gather | solution.py:885
  15.3 578.5 %reduce-scatter.2.cloned.1.call-start = ((), (), s32[]{:S(2)}) async-start(), calls=%async_computation.3 | async-start | bytes 8355840 | tf_op jit(solution)/shard_map/reduce_scatter | solution.py:997
  32.4 65.1 %collective-permute-start.3 = (bf16[320,1280]{1,0:T(8,128)(2,1)S(1)}, bf16[320,1280]{1,0:T(8,128)(2,1)S(1)}, u32[]{:S(2)}, u32[]{:S(2)}) collective-permute-start(bf16[320,1280]{1,0:T(8,128)(2,1)S(1)} %get-tuple-element.260), channel_id=1, source_target_pairs={{0,7},{1,6},{2,5},{3,4},{4,3},{5,2},{6,1},{7,0},{8,15},{9,14},{10,... | collective-permute-start | bytes 2457608 | tf_op jit(solution)/shard_map/ppermute | solution.py:803
  51.8 28.9 %collective-permute-start.8 = (bf16[4,80,1024]{2,1,0:T(8,128)(2,1)S(1)}, bf16[4,80,1024]{2,1,0:T(8,128)(2,1)S(1)}, u32[]{:S(2)}, u32[]{:S(2)}) collective-permute-start(bf16[4,80,1024]{2,1,0:T(8,128)(2,1)S(1)} %pad_maximum_fusion.5.refs_0_), channel_id=1, source_target_pairs={{0,2},{1,3},{2,0},{3,1},{4,6},{5,7},{6,4},{7,5},{8,10},{9,11},{10,... | collective-permute-start | bytes 1966088 | tf_op jit(solution)/shard_map/ppermute | solution.py:803
  53.5 27.2 %collective-permute-start.9 = (bf16[4,80,1024]{2,1,0:T(8,128)(2,1)S(1)}, bf16[4,80,1024]{2,1,0:T(8,128)(2,1)S(1)}, u32[]{:S(2)}, u32[]{:S(2)}) collective-permute-start(bf16[4,80,1024]{2,1,0:T(8,128)(2,1)S(1)} %pad_maximum_fusion.5.refs_0_), channel_id=1, source_target_pairs={{0,4},{1,5},{2,6},{3,7},{4,0},{5,1},{6,2},{7,3},{8,12},{9,13},{10,... | collective-permute-start | bytes 1966088 | tf_op jit(solution)/shard_map/ppermute | solution.py:803
  54.8 40.7 %collective-permute-start.10 = (bf16[4,80,1024]{2,1,0:T(8,128)(2,1)S(1)}, bf16[4,80,1024]{2,1,0:T(8,128)(2,1)S(1)}, u32[]{:S(2)}, u32[]{:S(2)}) collective-permute-start(bf16[4,80,1024]{2,1,0:T(8,128)(2,1)S(1)} %pad_maximum_fusion.5.refs_0_), channel_id=1, source_target_pairs={{0,6},{1,7},{2,4},{3,5},{4,2},{5,3},{6,0},{7,1},{8,14},{9,15},{10,... | collective-permute-start | bytes 1966088 | tf_op jit(solution)/shard_map/ppermute | solution.py:803
  56.5 42.4 %collective-permute-start.11 = (bf16[4,80,1024]{2,1,0:T(8,128)(2,1)S(1)}, bf16[4,80,1024]{2,1,0:T(8,128)(2,1)S(1)}, u32[]{:S(2)}, u32[]{:S(2)}) collective-permute-start(bf16[4,80,1024]{2,1,0:T(8,128)(2,1)S(1)} %pad_maximum_fusion.5.refs_0_), channel_id=1, source_target_pairs={{0,1},{1,0},{2,3},{3,2},{4,5},{5,4},{6,7},{7,6},{8,9},{9,8},{10,11... | collective-permute-start | bytes 1966088 | tf_op jit(solution)/shard_map/ppermute | solution.py:803
  108.2 39.4 %collective-permute-start.16 = (bf16[5,656,128]{2,1,0:T(8,128)(2,1)}, bf16[5,656,128]{2,1,0:T(8,128)(2,1)S(1)}, u32[]{:S(2)}, u32[]{:S(2)}) collective-permute-start(bf16[5,656,128]{2,1,0:T(8,128)(2,1)} %get-tuple-element.125.refs_0_), channel_id=1, source_target_pairs={{0,2},{1,3},{2,0},{3,1},{4,6},{5,7},{6,4},{7,5},{8,10},{9,11},{10,... | collective-permute-start | bytes 2519048 | tf_op jit(solution)/shard_map/ppermute | solution.py:803
  109.6 38.0 %collective-permute-start.17 = (bf16[5,656,128]{2,1,0:T(8,128)(2,1)}, bf16[5,656,128]{2,1,0:T(8,128)(2,1)}, u32[]{:S(2)}, u32[]{:S(2)}) collective-permute-start(bf16[5,656,128]{2,1,0:T(8,128)(2,1)} %get-tuple-element.125.refs_0_), channel_id=1, source_target_pairs={{0,4},{1,5},{2,6},{3,7},{4,0},{5,1},{6,2},{7,3},{8,12},{9,13},{10,... | collective-permute-start | bytes 2519048 | tf_op jit(solution)/shard_map/ppermute | solution.py:803
  110.1 56.1 %collective-permute-start.18 = (bf16[5,656,128]{2,1,0:T(8,128)(2,1)}, bf16[5,656,128]{2,1,0:T(8,128)(2,1)}, u32[]{:S(2)}, u32[]{:S(2)}) collective-permute-start(bf16[5,656,128]{2,1,0:T(8,128)(2,1)} %get-tuple-element.125.refs_0_), channel_id=1, source_target_pairs={{0,6},{1,7},{2,4},{3,5},{4,2},{5,3},{6,0},{7,1},{8,14},{9,15},{10,... | collective-permute-start | bytes 2519048 | tf_op jit(solution)/shard_map/ppermute | solution.py:803
  174.0 43.6 %collective-permute-start.22 = (bf16[320,1280]{1,0:T(8,128)(2,1)}, bf16[320,1280]{1,0:T(8,128)(2,1)S(1)}, u32[]{:S(2)}, u32[]{:S(2)}) collective-permute-start(bf16[320,1280]{1,0:T(8,128)(2,1)} %get-tuple-element.258), channel_id=1, source_target_pairs={{0,7},{1,6},{2,5},{3,4},{4,3},{5,2},{6,1},{7,0},{8,15},{9,14},{10,... | collective-permute-start | bytes 2457608 | tf_op jit(solution)/shard_map/ppermute | solution.py:803
  345.1 109.1 %collective-permute-start.29 = (bf16[4,80,2304]{2,1,0:T(8,128)(2,1)}, bf16[4,80,2304]{2,1,0:T(8,128)(2,1)}, u32[]{:S(2)}, u32[]{:S(2)}) collective-permute-start(bf16[4,80,2304]{2,1,0:T(8,128)(2,1)} %get-tuple-element.237), channel_id=1, source_target_pairs={{0,2},{1,3},{2,0},{3,1},{4,6},{5,7},{6,4},{7,5},{8,10},{9,11},{10,... | collective-permute-start | bytes 4423688 | tf_op jit(solution)/shard_map/ppermute | solution.py:803
  347.2 107.0 %collective-permute-start.30 = (bf16[4,80,2304]{2,1,0:T(8,128)(2,1)}, bf16[4,80,2304]{2,1,0:T(8,128)(2,1)}, u32[]{:S(2)}, u32[]{:S(2)}) collective-permute-start(bf16[4,80,2304]{2,1,0:T(8,128)(2,1)} %get-tuple-element.236), channel_id=1, source_target_pairs={{0,4},{1,5},{2,6},{3,7},{4,0},{5,1},{6,2},{7,3},{8,12},{9,13},{10,... | collective-permute-start | bytes 4423688 | tf_op jit(solution)/shard_map/ppermute | solution.py:803
  347.2 107.0 %collective-permute-start.31 = (bf16[4,80,2304]{2,1,0:T(8,128)(2,1)}, bf16[4,80,2304]{2,1,0:T(8,128)(2,1)}, u32[]{:S(2)}, u32[]{:S(2)}) collective-permute-start(bf16[4,80,2304]{2,1,0:T(8,128)(2,1)} %get-tuple-element.235), channel_id=1, source_target_pairs={{0,6},{1,7},{2,4},{3,5},{4,2},{5,3},{6,0},{7,1},{8,14},{9,15},{10,... | collective-permute-start | bytes 4423688 | tf_op jit(solution)/shard_map/ppermute | solution.py:803
  367.5 86.7 %collective-permute-start.28 = (bf16[4,4,40,1280]{3,2,1,0:T(8,128)(2,1)S(1)}, bf16[4,4,40,1280]{3,2,1,0:T(8,128)(2,1)}, u32[]{:S(2)}, u32[]{:S(2)}) collective-permute-start(bf16[4,4,40,1280]{3,2,1,0:T(8,128)(2,1)S(1)} %get-tuple-element.244), channel_id=1, source_target_pairs={{0,1},{1,0},{2,3},{3,2},{4,5},{5,4},{6,7},{7,6},{8,9},{9,8},{10,11... | collective-permute-start | bytes 4915208 | tf_op jit(solution)/shard_map/ppermute | solution.py:803
  368.7 84.3 %collective-permute-start.27 = (bf16[320,1280]{1,0:T(8,128)(2,1)}, bf16[320,1280]{1,0:T(8,128)(2,1)S(1)}, u32[]{:S(2)}, u32[]{:S(2)}) collective-permute-start(bf16[320,1280]{1,0:T(8,128)(2,1)} %get-tuple-element.256), channel_id=1, source_target_pairs={{0,7},{1,6},{2,5},{3,4},{4,3},{5,2},{6,1},{7,0},{8,15},{9,14},{10,... | collective-permute-start | bytes 2457608 | tf_op jit(solution)/shard_map/ppermute | solution.py:803
  462.2 50.5 %collective-permute-start.36 = (bf16[4,2,40,1280]{3,2,1,0:T(8,128)(2,1)S(1)}, bf16[4,2,40,1280]{3,2,1,0:T(8,128)(2,1)S(1)}, u32[]{:S(2)}, u32[]{:S(2)}) collective-permute-start(bf16[4,2,40,1280]{3,2,1,0:T(8,128)(2,1)S(1)} %get-tuple-element.253), channel_id=1, source_target_pairs={{0,2},{1,3},{2,0},{3,1},{4,6},{5,7},{6,4},{7,5},{8,10},{9,11},{10,... | collective-permute-start | bytes 2457608 | tf_op jit(solution)/shard_map/ppermute | solution.py:803
  463.8 49.0 %collective-permute-start.37 = (bf16[2,80,2304]{2,1,0:T(8,128)(2,1)}, bf16[2,80,2304]{2,1,0:T(8,128)(2,1)S(1)}, u32[]{:S(2)}, u32[]{:S(2)}) collective-permute-start(bf16[2,80,2304]{2,1,0:T(8,128)(2,1)} %get-tuple-element.261), channel_id=1, source_target_pairs={{0,16},{1,17},{2,18},{3,19},{4,20},{5,21},{6,22},{7,23},{8,24},{9,... | collective-permute-start | bytes 2211848 | tf_op jit(solution)/shard_map/ppermute | solution.py:803
  465.0 46.9 %collective-permute-start.33 = (bf16[3,640,128]{2,1,0:T(8,128)(2,1)}, bf16[3,640,128]{2,1,0:T(8,128)(2,1)S(1)}, u32[]{:S(2)}, u32[]{:S(2)}) collective-permute-start(bf16[3,640,128]{2,1,0:T(8,128)(2,1)} %get-tuple-element.173), channel_id=1, source_target_pairs={{0,2},{1,3},{2,0},{3,1},{4,6},{5,7},{6,4},{7,5},{8,10},{9,11},{10,... | collective-permute-start | bytes 1474568 | tf_op jit(solution)/shard_map/ppermute | solution.py:803
  465.8 46.2 %collective-permute-start.34 = (bf16[3,640,128]{2,1,0:T(8,128)(2,1)}, bf16[3,640,128]{2,1,0:T(8,128)(2,1)S(1)}, u32[]{:S(2)}, u32[]{:S(2)}) collective-permute-start(bf16[3,640,128]{2,1,0:T(8,128)(2,1)} %get-tuple-element.174), channel_id=1, source_target_pairs={{0,4},{1,5},{2,6},{3,7},{4,0},{5,1},{6,2},{7,3},{8,12},{9,13},{10,... | collective-permute-start | bytes 1474568 | tf_op jit(solution)/shard_map/ppermute | solution.py:803
  468.8 44.0 %collective-permute-start.35 = (bf16[3,640,128]{2,1,0:T(8,128)(2,1)}, bf16[3,640,128]{2,1,0:T(8,128)(2,1)S(1)}, u32[]{:S(2)}, u32[]{:S(2)}) collective-permute-start(bf16[3,640,128]{2,1,0:T(8,128)(2,1)} %get-tuple-element.175), channel_id=1, source_target_pairs={{0,6},{1,7},{2,4},{3,5},{4,2},{5,3},{6,0},{7,1},{8,14},{9,15},{10,... | collective-permute-start | bytes 1474568 | tf_op jit(solution)/shard_map/ppermute | solution.py:803
  591.6 30.4 %collective-permute-start.48 = (bf16[4,40,2048]{2,1,0:T(8,128)(2,1)}, bf16[4,40,2048]{2,1,0:T(8,128)(2,1)}, u32[]{:S(2)}, u32[]{:S(2)}) collective-permute-start(bf16[4,40,2048]{2,1,0:T(8,128)(2,1)} %get-tuple-element.247), channel_id=1, source_target_pairs={{0,4},{1,5},{2,6},{3,7},{4,0},{5,1},{6,2},{7,3},{8,12},{9,13},{10,... | collective-permute-start | bytes 1966088 | tf_op jit(solution)/shard_map/ppermute | solution.py:803
  592.4 29.7 %collective-permute-start.49 = (bf16[4,40,2048]{2,1,0:T(8,128)(2,1)}, bf16[4,40,2048]{2,1,0:T(8,128)(2,1)}, u32[]{:S(2)}, u32[]{:S(2)}) collective-permute-start(bf16[4,40,2048]{2,1,0:T(8,128)(2,1)} %get-tuple-element.246), channel_id=1, source_target_pairs={{0,6},{1,7},{2,4},{3,5},{4,2},{5,3},{6,0},{7,1},{8,14},{9,15},{10,... | collective-permute-start | bytes 1966088 | tf_op jit(solution)/shard_map/ppermute | solution.py:803
  (91 other events, 1677.3 us)
Sparse Core Ops, SparseCore 0:
  14.6 149.4 all-gather.2
  167.4 123.3 all-gather.4
  340.3 216.2 reduce-scatter.1

commit v5 on v4

--- a/solution.py
+++ b/solution.py
@@ -568,35 +568,33 @@
     n1_ref, n2_ref, og1_ref, og2_ref, wg_ref, wu_ref, wd_ref, *refs, later
 ):
     priors, refs = refs[: 2 * later], refs[2 * later :]
-    own_ref, far_ref, dw_ref, n, og, nt, ogt, oacc, nacc, hid, dgate, dup = refs
+    own_ref, far_ref, dw_ref, nt, ogt, oacc, nacc, hid, dgate, dup, sems = refs
     f = pl.program_id(0)
     part = pl.program_id(1)
     rows = n1_ref.shape[0]
+    copies = [
+        pltpu.make_async_copy(prior, target, sems.at[k])
+        for k, (prior, target) in enumerate(zip(priors, (own_ref, far_ref)))
+    ]
 
     @pl.when((f == 0) & (part == 0))
     def _():
-        n[:rows] = n1_ref[...]
-        n[rows:] = n2_ref[...]
-        og[:rows] = og1_ref[...]
-        og[rows:] = og2_ref[...]
-        nt[...] = n[...].T
-        ogt[...] = og[...].T
-        if later:
-            for k, (prior, target) in enumerate(zip(priors, (own_ref, far_ref))):
-                pltpu.sync_copy(prior, target)
-                oacc[k * rows : (k + 1) * rows] = target[0].astype(F32)
-                nacc[k * rows : (k + 1) * rows] = target[1].astype(F32)
-        else:
-            oacc[...] = jnp.zeros_like(oacc)
-            nacc[...] = jnp.zeros_like(nacc)
+        for copy in copies:
+            copy.start()
+        nt[:, :rows] = n1_ref[...].T
+        nt[:, rows:] = n2_ref[...].T
+        ogt[:, :rows] = og1_ref[...].T
+        ogt[:, rows:] = og2_ref[...].T
+        oacc[...] = jnp.zeros_like(oacc)
+        nacc[...] = jnp.zeros_like(nacc)
 
     @pl.when(part == 0)
     def _():
-        for k in range(2):
+        for k, (n_ref, og_ref) in enumerate(((n1_ref, og1_ref), (n2_ref, og2_ref))):
             at = slice(k * rows, (k + 1) * rows)
-            gate = dot(n[at], wg_ref[...])
-            up = dot(n[at], wu_ref[...])
-            grad = dot(og[at], wd_ref[...])
+            gate = dot(n_ref[...], wg_ref[...])
+            up = dot(n_ref[...], wu_ref[...])
+            grad = dot(og_ref[...], wd_ref[...])
             sig = jax.nn.sigmoid(gate)
             silu = gate * sig
             hid[at] = (silu * up).astype(BF16)
@@ -616,10 +614,14 @@
 
     @pl.when((f == pl.num_programs(0) - 1) & (part == 2))
     def _():
-        own_ref[0] = oacc[:rows].astype(BF16)
-        own_ref[1] = nacc[:rows].astype(BF16)
-        far_ref[0] = oacc[rows:].astype(BF16)
-        far_ref[1] = nacc[rows:].astype(BF16)
+        for copy in copies:
+            copy.wait()
+        for k, target in enumerate((own_ref, far_ref)):
+            for side, acc in enumerate((oacc, nacc)):
+                total = acc[k * rows : (k + 1) * rows]
+                if later:
+                    total = total + target[side].astype(F32)
+                target[side] = total.astype(BF16)
 
 
 def feed_forward(steps, n_own, n_far, og_own, og_far, w, priors=()):
@@ -639,8 +641,6 @@
             jax.ShapeDtypeStruct((D, 3 * steps * block), BF16),
         ],
         scratch_shapes=[
-            pltpu.VMEM((2 * rows, D), BF16),
-            pltpu.VMEM((2 * rows, D), BF16),
             pltpu.VMEM((D, 2 * rows), BF16),
             pltpu.VMEM((D, 2 * rows), BF16),
             pltpu.VMEM((2 * rows, D), F32),
@@ -648,6 +648,7 @@
             pltpu.VMEM((2 * rows, block), BF16),
             pltpu.VMEM((2 * rows, block), BF16),
             pltpu.VMEM((2 * rows, block), BF16),
+            pltpu.SemaphoreType.DMA((2,)),
         ],
         compiler_params=params(62),
         cost_estimate=SMALL,
@@ -1032,6 +1033,7 @@
     pieces_b += [swap(v, 2 * c + 2) for c, v in enumerate(both)]
     out_dw = halve(out_dw, chip_y, 1, 4)
     next_dw = trees_second(next_dw)
+    pieces_b[-1], *next_dw = stage(pieces_b[-1], *next_dw)
     dn, qkv_dw = project_back(
         tokens_in, normed1, (dq_a, dq_b), (pieces_a, pieces_b), qkv_w, dgain2, cos, sin
     )

time: 669 us -> 666 us (level)
  Pallas kernels: 286 us -> 295 us
  starting transfers between devices: 67.4 us -> 58.5 us
  waiting for transfers between devices: 204 us -> 196 us
    ppermute x55, waiting for transfers between devices: 197 us -> 187 us  [swap(): return lax.ppermute(v, 'fsdp', [(i, i ^ bit) for i in range(size)])]
    pallas_call x2, Pallas kernels: 103 us -> 112 us  [attention_backward(): pl.pallas_call(functools.partial(backward_kernel, tiles=tiles, span=span,...]
    ppermute x55, starting transfers between devices: 67.2 us -> 58.3 us  [swap(): return lax.ppermute(v, 'fsdp', [(i, i ^ bit) for i in range(size)])]
    unnamed x120 -> x124, local copies, waits for them, and re-layouts: 16.2 us -> 15.7 us
  transfers between devices with their start and end apart: 58 -> 58, of which waited for: 23 -> 26; matrix products, arithmetic and copies ran while one was open for 10% -> 10% of each run, Pallas kernels for 36% -> 38%
where the time goes in v5:
time: 666 us; the launch traced here: 655 us
  Pallas kernels  295 us (44%)
  waiting for transfers between devices  196 us (29%)
  starting transfers between devices  58.5 us (9%)
  local copies, waits for them, and re-layouts  51.8 us (8%)
  other arithmetic  38.3 us (6%)
  between operations  15.1 us (2%)
    ppermute x55, waiting for transfers between devices, swap(): return lax.ppermute(v, 'fsdp', [(i, i ^ bit) for i in range(size)])  187 us
    pallas_call x2, Pallas kernels, attention_backward(): pl.pallas_call(functools.partial(backward_kernel, tiles=tiles, span=span,...  112 us
    pallas_call x2, Pallas kernels, feed_forward(): pl.pallas_call(functools.partial(feed_forward_kernel, later=bool(priors))...  83 us
    ppermute x55, starting transfers between devices, swap(): return lax.ppermute(v, 'fsdp', [(i, i ^ bit) for i in range(size)])  58.3 us
    pallas_call x1, Pallas kernels, attention_forward(): pl.pallas_call(functools.partial(forward_kernel, tiles=tiles, span=span),...  44.9 us
    squeeze x12, local copies, waits for them, and re-layouts, part(): return lax.dynamic_index_in_dim(v, index, axis, keepdims=False)  18 us
    pallas_call x1, Pallas kernels, project_back(): pl.pallas_call(kernel, out_shape=[jax.ShapeDtypeStruct((rows, D), F32), j...  17 us
    pallas_call x1, Pallas kernels, turn(): pl.pallas_call(turn_kernel, out_shape=[jax.ShapeDtypeStruct((rows, D), BF...  16.4 us
  transfers between devices with their start and end apart: 58, of which 26 were waited for; matrix products, arithmetic and copies ran while one was open for 10% of the time, Pallas kernels for 38%

profile of v5, /device:TPU:0, one launch (start us, length us, event | category | flops | bytes accessed | tf_op | source)
XLA Modules:
  0.0 654.7 jit_solution(14651988685852570190)
XLA Ops:
  32.6 11.0 %collective-permute-done.5 = bf16[80,1024]{1,0:T(8,128)(2,1)S(1)} collective-permute-done((bf16[80,1024]{1,0:T(8,128)(2,1)S(1)}, bf16[80,1024]{1,0:T(8,128)(2,1)S(1)}, u32[]{:S(2)}, u32[]{:S(2)}) %collective-permute-start.5) | collective-permute-done | bytes 163872 | tf_op jit(solution)/shard_map/ppermute | solution.py:804
  43.7 6.1 collective-permute-done.6
  56.1 24.1 %collective-permute-done.8.refs_1_ = bf16[4,80,1024]{2,1,0:T(8,128)(2,1)S(1)} collective-permute-done((bf16[4,80,1024]{2,1,0:T(8,128)(2,1)S(1)}, bf16[4,80,1024]{2,1,0:T(8,128)(2,1)S(1)}, u32[]{:S(2)}, u32[]{:S(2)}) %collective-permute-start.8) | collective-permute-done | bytes 655392 | tf_op jit(solution)/shard_map/ppermute | solution.py:804
  80.7 14.8 %collective-permute-done.10.refs_3_ = bf16[4,80,1024]{2,1,0:T(8,128)(2,1)S(1)} collective-permute-done((bf16[4,80,1024]{2,1,0:T(8,128)(2,1)S(1)}, bf16[4,80,1024]{2,1,0:T(8,128)(2,1)S(1)}, u32[]{:S(2)}, u32[]{:S(2)}) %collective-permute-start.10) | collective-permute-done | bytes 655392 | tf_op jit(solution)/shard_map/ppermute | solution.py:804
  98.9 8.6 %project_keys.1 = (bf16[640,1280]{1,0:T(8,128)(2,1)}, bf16[5,656,128]{2,1,0:T(8,128)(2,1)}, f32[8,1280]{1,0:T(8,128)S(1)}, bf16[1280,2048]{1,0:T(8,128)(2,1)}) custom-call(s32[40]{0:T(128)S(1)} %concatenate.86.place_ref, bf16[640,1280]{1,0:T(8,128)(2,1)} %pad_maximum_fusion.1.x_ref, f32[640,128]{1,0:T(8,128)S(1)} %get-tuple-element.325.cos_ref.refs_12_, ...), custom_call_target="tpu_custom_call" | custom-call | tf_op jit(solution)/shard_map/project_keys/pallas_call | solution.py:136
  114.5 8.0 %project_queries.1 = (bf16[20,640,128]{2,1,0:T(8,128)(2,1)S(1)}, f32[8,128]{1,0:T(8,128)S(1)}) custom-call(bf16[640,1280]{1,0:T(8,128)(2,1)S(1)} %copy-done.10, bf16[1280,2048]{1,0:T(8,128)(2,1)} %get-tuple-element.118.w_ref.refs_10_, f32[640,128]{1,0:T(8,128)S(1)} %get-tuple-element.325.cos_ref.refs_12_, f32[640,128]{1,0:T(8,128)S(1)} %get-tuple-element.324.sin_ref.refs_13_), custom_call_target="tpu_custom_call" | custom-call | flops 1000000 | bytes 10000 | tf_op jit(solution)/shard_map/project_queries/pallas_call | solution.py:174
  124.3 23.3 %collective-permute-done.16.refs_2_ = bf16[5,656,128]{2,1,0:T(8,128)(2,1)S(1)} collective-permute-done((bf16[5,656,128]{2,1,0:T(8,128)(2,1)}, bf16[5,656,128]{2,1,0:T(8,128)(2,1)S(1)}, u32[]{:S(2)}, u32[]{:S(2)}) %collective-permute-start.16) | collective-permute-done | bytes 839712 | tf_op jit(solution)/shard_map/ppermute | solution.py:804
  147.6 18.7 %collective-permute-done.18.refs_6_ = bf16[5,656,128]{2,1,0:T(8,128)(2,1)} collective-permute-done((bf16[5,656,128]{2,1,0:T(8,128)(2,1)}, bf16[5,656,128]{2,1,0:T(8,128)(2,1)}, u32[]{:S(2)}, u32[]{:S(2)}) %collective-permute-start.18) | collective-permute-done | bytes 839712 | tf_op jit(solution)/shard_map/ppermute | solution.py:804
  176.6 44.9 %attention_forward.1 = (bf16[640,1280]{1,0:T(8,128)(2,1)}, f32[640,128]{1,0:T(8,128)S(1)}) custom-call(s32[241]{0:T(256)S(1)} %fusion.26.meta_ref, bf16[20,640,128]{2,1,0:T(8,128)(2,1)} %copy-done.2, f32[8,128]{1,0:T(8,128)S(1)} %get-tuple-element.127.top_ref, bf16[5,656,128]{2,1,0:T(8,128)(2,1)S(1)} %copy-done.9, bf16[5,656,128]{2,1,0:T(8,128)(2,1)} %copy-done.24, ...), custom_call_target="tpu_custom_call" | custom-call | flops 1000000 | bytes 10000 | tf_op jit(solution)/shard_map/attention_forward/pallas_call | solution.py:366
  244.6 37.1 %feed_forward.2 = (bf16[2,640,1280]{2,1,0:T(8,128)(2,1)}, bf16[2,640,1280]{2,1,0:T(8,128)(2,1)}, bf16[1280,2304]{1,0:T(8,128)(2,1)}) custom-call(bf16[640,1280]{1,0:T(8,128)(2,1)} %copy-done.11, bf16[640,1280]{1,0:T(8,128)(2,1)} %copy-done.27, bf16[640,1280]{1,0:T(8,128)(2,1)} %pad_maximum_fusion.2.og1_ref.og_ref, ...), custom_call_target="tpu_custom_call" | custom-call | flops 1000000 | bytes 10000 | tf_op jit(solution)/shard_map/feed_forward/pallas_call | solution.py:633
  281.6 9.1 %all-gather.5.cloned.1.call-done.wg_ref.wu_ref.wd_ref = bf16[1280,3072]{1,0:T(8,128)(2,1)} async-done(((bf16[80,3072]{1,0:T(8,128)(2,1)}), bf16[1280,3072]{1,0:T(8,128)(2,1)}) %all-gather.5.cloned.1.call-update) | async-done | bytes 7864336 | tf_op jit(solution)/shard_map/all_gather | solution.py:886
  290.7 45.9 %feed_forward.3 = (bf16[2,640,1280]{2,1,0:T(8,128)(2,1)}, bf16[2,640,1280]{2,1,0:T(8,128)(2,1)}, bf16[1280,3072]{1,0:T(8,128)(2,1)}) custom-call(bf16[640,1280]{1,0:T(8,128)(2,1)} %copy-done.11, bf16[640,1280]{1,0:T(8,128)(2,1)} %copy-done.27, bf16[640,1280]{1,0:T(8,128)(2,1)} %pad_maximum_fusion.2.og1_ref.og_ref, ...), custom_call_target="tpu_custom_call" | custom-call | flops 1000000 | bytes 10000 | tf_op jit(solution)/shard_map/feed_forward/pallas_call | solution.py:633
  336.8 4.9 dynamic-slice_bitcast_fusion.4
  345.2 16.4 %turn.1 = (bf16[640,1280]{1,0:T(8,128)(2,1)}, f32[640,1280]{1,0:T(8,128)}, bf16[640,1280]{1,0:T(8,128)(2,1)}, bf16[1280,1280]{1,0:T(8,128)(2,1)}, f32[8,1280]{1,0:T(8,128)}) custom-call(f32[640,1280]{1,0:T(8,128)} %copy-done.13, bf16[2,640,1280]{2,1,0:T(8,128)(2,1)} %get-tuple-element.150.own_ref, bf16[2,640,1280]{2,1,0:T(8,128)(2,1)} %collective-permute-done.26.got_ref, ...), custom_call_target="tpu_custom_call" | custom-call | tf_op jit(solution)/shard_map/turn/pallas_call | solution.py:688
  366.6 65.2 %attention_backward.2 = (bf16[640,768]{1,0:T(8,128)(2,1)}, bf16[4,3,640,128]{3,2,1,0:T(8,128)(2,1)}, bf16[4,3,640,128]{3,2,1,0:T(8,128)(2,1)}) custom-call(s32[241]{0:T(256)} %copy-done.23, bf16[20,640,128]{2,1,0:T(8,128)(2,1)} %copy-done.2, bf16[640,1280]{1,0:T(8,128)(2,1)} %get-tuple-element.153.da_ref, bf16[640,1280]{1,0:T(8,128)(2,1)} %get-tuple-element.139.att_ref, ...), custom_call_target="tpu_custom_call" | custom-call | flops 1000000 | bytes 10000 | tf_op jit(solution)/shard_map/attention_backward/pallas_call | solution.py:507
  431.8 15.6 %collective-permute-done.27 = bf16[320,1280]{1,0:T(8,128)(2,1)S(1)} collective-permute-done((bf16[320,1280]{1,0:T(8,128)(2,1)}, bf16[320,1280]{1,0:T(8,128)(2,1)S(1)}, u32[]{:S(2)}, u32[]{:S(2)}) %collective-permute-start.27) | collective-permute-done | bytes 819232 | tf_op jit(solution)/shard_map/ppermute | solution.py:804
  468.6 46.9 %attention_backward.3 = (bf16[640,512]{1,0:T(8,128)(2,1)}, bf16[4,2,640,128]{3,2,1,0:T(8,128)(2,1)}, bf16[4,2,640,128]{3,2,1,0:T(8,128)(2,1)}) custom-call(s32[241]{0:T(256)} %copy-done.23, bf16[20,640,128]{2,1,0:T(8,128)(2,1)} %copy-done.2, bf16[640,1280]{1,0:T(8,128)(2,1)} %get-tuple-element.153.da_ref, bf16[640,1280]{1,0:T(8,128)(2,1)} %get-tuple-element.139.att_ref, ...), custom_call_target="tpu_custom_call" | custom-call | flops 1000000 | bytes 10000 | tf_op jit(solution)/shard_map/attention_backward/pallas_call | solution.py:507
  523.8 6.2 collective-permute-start.41
  538.6 5.9 collective-permute-done.42
  548.1 17.0 %project_back.1 = (f32[640,1280]{1,0:T(8,128)}, bf16[1280,2048]{1,0:T(8,128)(2,1)}) custom-call(bf16[640,1280]{1,0:T(8,128)(2,1)} %pad_maximum_fusion.1.x_ref, bf16[640,1280]{1,0:T(8,128)(2,1)} %get-tuple-element.117.n_ref, bf16[640,768]{1,0:T(8,128)(2,1)} %get-tuple-element.163.dqa_ref, bf16[640,512]{1,0:T(8,128)(2,1)S(1)} %copy-done.19, ...), custom_call_target="tpu_custom_call" | custom-call | tf_op jit(solution)/shard_map/project_back/pallas_call | solution.py:755
  571.3 10.5 %collective-permute-done.43 = bf16[4,40,1280]{2,1,0:T(8,128)(2,1)S(1)} collective-permute-done((bf16[4,40,1280]{2,1,0:T(8,128)(2,1)S(1)}, bf16[4,40,1280]{2,1,0:T(8,128)(2,1)S(1)}, u32[]{:S(2)}, u32[]{:S(2)}) %collective-permute-start.43) | collective-permute-done | bytes 409632 | tf_op jit(solution)/shard_map/ppermute | solution.py:804
  598.6 6.8 %collective-permute-done.46 = bf16[2,40,1280]{2,1,0:T(8,128)(2,1)S(1)} collective-permute-done((bf16[2,40,1280]{2,1,0:T(8,128)(2,1)}, bf16[2,40,1280]{2,1,0:T(8,128)(2,1)S(1)}, u32[]{:S(2)}, u32[]{:S(2)}) %collective-permute-start.46) | collective-permute-done | bytes 204832 | tf_op jit(solution)/shard_map/ppermute | solution.py:804
  605.4 12.2 %collective-permute-done.49 = bf16[4,40,2048]{2,1,0:T(8,128)(2,1)} collective-permute-done((bf16[4,40,2048]{2,1,0:T(8,128)(2,1)}, bf16[4,40,2048]{2,1,0:T(8,128)(2,1)}, u32[]{:S(2)}, u32[]{:S(2)}) %collective-permute-start.49) | collective-permute-done | bytes 655392 | tf_op jit(solution)/shard_map/ppermute | solution.py:804
  632.2 9.3 %collective-permute-done.52 = bf16[40,2048]{1,0:T(8,128)(2,1)S(1)} collective-permute-done((bf16[40,2048]{1,0:T(8,128)(2,1)S(1)}, bf16[40,2048]{1,0:T(8,128)(2,1)S(1)}, u32[]{:S(2)}, u32[]{:S(2)}) %collective-permute-start.52) | collective-permute-done | bytes 163872 | tf_op jit(solution)/shard_map/ppermute | solution.py:804
  (352 shorter events, 171.2 us)
Async XLA Ops:
  7.2 215.6 %all-gather.3.cloned.1.call-start = ((), (), s32[]{:S(2)}) async-start(), calls=%async_computation.1 | async-start | bytes 8007680 | tf_op jit(solution)/shard_map/all_gather | solution.py:886
  14.4 276.3 %all-gather.5.cloned.1.call-start = ((), (), s32[]{:S(2)}) async-start(), calls=%async_computation.2 | async-start | bytes 8355840 | tf_op jit(solution)/shard_map/all_gather | solution.py:886
  15.3 574.4 %reduce-scatter.2.cloned.1.call-start = ((), (), s32[]{:S(2)}) async-start(), calls=%async_computation.3 | async-start | bytes 8355840 | tf_op jit(solution)/shard_map/reduce_scatter | solution.py:998
  32.4 65.1 %collective-permute-start.3 = (bf16[320,1280]{1,0:T(8,128)(2,1)S(1)}, bf16[320,1280]{1,0:T(8,128)(2,1)S(1)}, u32[]{:S(2)}, u32[]{:S(2)}) collective-permute-start(bf16[320,1280]{1,0:T(8,128)(2,1)S(1)} %get-tuple-element.266), channel_id=1, source_target_pairs={{0,7},{1,6},{2,5},{3,4},{4,3},{5,2},{6,1},{7,0},{8,15},{9,14},{10,... | collective-permute-start | bytes 2457608 | tf_op jit(solution)/shard_map/ppermute | solution.py:804
  51.4 28.8 %collective-permute-start.8 = (bf16[4,80,1024]{2,1,0:T(8,128)(2,1)S(1)}, bf16[4,80,1024]{2,1,0:T(8,128)(2,1)S(1)}, u32[]{:S(2)}, u32[]{:S(2)}) collective-permute-start(bf16[4,80,1024]{2,1,0:T(8,128)(2,1)S(1)} %pad_maximum_fusion.5.refs_0_), channel_id=1, source_target_pairs={{0,2},{1,3},{2,0},{3,1},{4,6},{5,7},{6,4},{7,5},{8,10},{9,11},{10,... | collective-permute-start | bytes 1966088 | tf_op jit(solution)/shard_map/ppermute | solution.py:804
  53.3 27.0 %collective-permute-start.9 = (bf16[4,80,1024]{2,1,0:T(8,128)(2,1)S(1)}, bf16[4,80,1024]{2,1,0:T(8,128)(2,1)S(1)}, u32[]{:S(2)}, u32[]{:S(2)}) collective-permute-start(bf16[4,80,1024]{2,1,0:T(8,128)(2,1)S(1)} %pad_maximum_fusion.5.refs_0_), channel_id=1, source_target_pairs={{0,4},{1,5},{2,6},{3,7},{4,0},{5,1},{6,2},{7,3},{8,12},{9,13},{10,... | collective-permute-start | bytes 1966088 | tf_op jit(solution)/shard_map/ppermute | solution.py:804
  54.9 40.7 %collective-permute-start.10 = (bf16[4,80,1024]{2,1,0:T(8,128)(2,1)S(1)}, bf16[4,80,1024]{2,1,0:T(8,128)(2,1)S(1)}, u32[]{:S(2)}, u32[]{:S(2)}) collective-permute-start(bf16[4,80,1024]{2,1,0:T(8,128)(2,1)S(1)} %pad_maximum_fusion.5.refs_0_), channel_id=1, source_target_pairs={{0,6},{1,7},{2,4},{3,5},{4,2},{5,3},{6,0},{7,1},{8,14},{9,15},{10,... | collective-permute-start | bytes 1966088 | tf_op jit(solution)/shard_map/ppermute | solution.py:804
  56.1 42.8 %collective-permute-start.11 = (bf16[4,80,1024]{2,1,0:T(8,128)(2,1)S(1)}, bf16[4,80,1024]{2,1,0:T(8,128)(2,1)S(1)}, u32[]{:S(2)}, u32[]{:S(2)}) collective-permute-start(bf16[4,80,1024]{2,1,0:T(8,128)(2,1)S(1)} %pad_maximum_fusion.5.refs_0_), channel_id=1, source_target_pairs={{0,1},{1,0},{2,3},{3,2},{4,5},{5,4},{6,7},{7,6},{8,9},{9,8},{10,11... | collective-permute-start | bytes 1966088 | tf_op jit(solution)/shard_map/ppermute | solution.py:804
  108.1 39.4 %collective-permute-start.16 = (bf16[5,656,128]{2,1,0:T(8,128)(2,1)}, bf16[5,656,128]{2,1,0:T(8,128)(2,1)S(1)}, u32[]{:S(2)}, u32[]{:S(2)}) collective-permute-start(bf16[5,656,128]{2,1,0:T(8,128)(2,1)} %get-tuple-element.128.refs_0_), channel_id=1, source_target_pairs={{0,2},{1,3},{2,0},{3,1},{4,6},{5,7},{6,4},{7,5},{8,10},{9,11},{10,... | collective-permute-start | bytes 2519048 | tf_op jit(solution)/shard_map/ppermute | solution.py:804
  109.6 38.0 %collective-permute-start.17 = (bf16[5,656,128]{2,1,0:T(8,128)(2,1)}, bf16[5,656,128]{2,1,0:T(8,128)(2,1)}, u32[]{:S(2)}, u32[]{:S(2)}) collective-permute-start(bf16[5,656,128]{2,1,0:T(8,128)(2,1)} %get-tuple-element.128.refs_0_), channel_id=1, source_target_pairs={{0,4},{1,5},{2,6},{3,7},{4,0},{5,1},{6,2},{7,3},{8,12},{9,13},{10,... | collective-permute-start | bytes 2519048 | tf_op jit(solution)/shard_map/ppermute | solution.py:804
  110.1 56.1 %collective-permute-start.18 = (bf16[5,656,128]{2,1,0:T(8,128)(2,1)}, bf16[5,656,128]{2,1,0:T(8,128)(2,1)}, u32[]{:S(2)}, u32[]{:S(2)}) collective-permute-start(bf16[5,656,128]{2,1,0:T(8,128)(2,1)} %get-tuple-element.128.refs_0_), channel_id=1, source_target_pairs={{0,6},{1,7},{2,4},{3,5},{4,2},{5,3},{6,0},{7,1},{8,14},{9,15},{10,... | collective-permute-start | bytes 2519048 | tf_op jit(solution)/shard_map/ppermute | solution.py:804
  174.0 47.5 %collective-permute-start.22 = (bf16[320,1280]{1,0:T(8,128)(2,1)}, bf16[320,1280]{1,0:T(8,128)(2,1)S(1)}, u32[]{:S(2)}, u32[]{:S(2)}) collective-permute-start(bf16[320,1280]{1,0:T(8,128)(2,1)} %get-tuple-element.264), channel_id=1, source_target_pairs={{0,7},{1,6},{2,5},{3,4},{4,3},{5,2},{6,1},{7,0},{8,15},{9,14},{10,... | collective-permute-start | bytes 2457608 | tf_op jit(solution)/shard_map/ppermute | solution.py:804
  341.7 107.0 %collective-permute-start.29 = (bf16[4,80,2304]{2,1,0:T(8,128)(2,1)}, bf16[4,80,2304]{2,1,0:T(8,128)(2,1)}, u32[]{:S(2)}, u32[]{:S(2)}) collective-permute-start(bf16[4,80,2304]{2,1,0:T(8,128)(2,1)} %get-tuple-element.243), channel_id=1, source_target_pairs={{0,2},{1,3},{2,0},{3,1},{4,6},{5,7},{6,4},{7,5},{8,10},{9,11},{10,... | collective-permute-start | bytes 4423688 | tf_op jit(solution)/shard_map/ppermute | solution.py:804
  343.2 105.5 %collective-permute-start.30 = (bf16[4,80,2304]{2,1,0:T(8,128)(2,1)}, bf16[4,80,2304]{2,1,0:T(8,128)(2,1)}, u32[]{:S(2)}, u32[]{:S(2)}) collective-permute-start(bf16[4,80,2304]{2,1,0:T(8,128)(2,1)} %get-tuple-element.242), channel_id=1, source_target_pairs={{0,4},{1,5},{2,6},{3,7},{4,0},{5,1},{6,2},{7,3},{8,12},{9,13},{10,... | collective-permute-start | bytes 4423688 | tf_op jit(solution)/shard_map/ppermute | solution.py:804
  343.7 104.9 %collective-permute-start.31 = (bf16[4,80,2304]{2,1,0:T(8,128)(2,1)}, bf16[4,80,2304]{2,1,0:T(8,128)(2,1)}, u32[]{:S(2)}, u32[]{:S(2)}) collective-permute-start(bf16[4,80,2304]{2,1,0:T(8,128)(2,1)} %get-tuple-element.241), channel_id=1, source_target_pairs={{0,6},{1,7},{2,4},{3,5},{4,2},{5,3},{6,0},{7,1},{8,14},{9,15},{10,... | collective-permute-start | bytes 4423688 | tf_op jit(solution)/shard_map/ppermute | solution.py:804
  363.9 84.8 %collective-permute-start.28 = (bf16[4,4,40,1280]{3,2,1,0:T(8,128)(2,1)S(1)}, bf16[4,4,40,1280]{3,2,1,0:T(8,128)(2,1)}, u32[]{:S(2)}, u32[]{:S(2)}) collective-permute-start(bf16[4,4,40,1280]{3,2,1,0:T(8,128)(2,1)S(1)} %get-tuple-element.250), channel_id=1, source_target_pairs={{0,1},{1,0},{2,3},{3,2},{4,5},{5,4},{6,7},{7,6},{8,9},{9,8},{10,11... | collective-permute-start | bytes 4915208 | tf_op jit(solution)/shard_map/ppermute | solution.py:804
  365.2 82.2 %collective-permute-start.27 = (bf16[320,1280]{1,0:T(8,128)(2,1)}, bf16[320,1280]{1,0:T(8,128)(2,1)S(1)}, u32[]{:S(2)}, u32[]{:S(2)}) collective-permute-start(bf16[320,1280]{1,0:T(8,128)(2,1)} %get-tuple-element.262), channel_id=1, source_target_pairs={{0,7},{1,6},{2,5},{3,4},{4,3},{5,2},{6,1},{7,0},{8,15},{9,14},{10,... | collective-permute-start | bytes 2457608 | tf_op jit(solution)/shard_map/ppermute | solution.py:804
  457.7 60.1 %collective-permute-start.36 = (bf16[4,2,40,1280]{3,2,1,0:T(8,128)(2,1)}, bf16[4,2,40,1280]{3,2,1,0:T(8,128)(2,1)S(1)}, u32[]{:S(2)}, u32[]{:S(2)}) collective-permute-start(bf16[4,2,40,1280]{3,2,1,0:T(8,128)(2,1)} %get-tuple-element.259), channel_id=1, source_target_pairs={{0,2},{1,3},{2,0},{3,1},{4,6},{5,7},{6,4},{7,5},{8,10},{9,11},{10,... | collective-permute-start | bytes 2457608 | tf_op jit(solution)/shard_map/ppermute | solution.py:804
  461.2 56.6 %collective-permute-start.37 = (bf16[2,80,2304]{2,1,0:T(8,128)(2,1)}, bf16[2,80,2304]{2,1,0:T(8,128)(2,1)}, u32[]{:S(2)}, u32[]{:S(2)}) collective-permute-start(bf16[2,80,2304]{2,1,0:T(8,128)(2,1)} %get-tuple-element.267), channel_id=1, source_target_pairs={{0,16},{1,17},{2,18},{3,19},{4,20},{5,21},{6,22},{7,23},{8,24},{9,... | collective-permute-start | bytes 2211848 | tf_op jit(solution)/shard_map/ppermute | solution.py:804
  464.0 51.4 %collective-permute-start.33 = (bf16[3,640,128]{2,1,0:T(8,128)(2,1)}, bf16[3,640,128]{2,1,0:T(8,128)(2,1)S(1)}, u32[]{:S(2)}, u32[]{:S(2)}) collective-permute-start(bf16[3,640,128]{2,1,0:T(8,128)(2,1)} %get-tuple-element.176), channel_id=1, source_target_pairs={{0,2},{1,3},{2,0},{3,1},{4,6},{5,7},{6,4},{7,5},{8,10},{9,11},{10,... | collective-permute-start | bytes 1474568 | tf_op jit(solution)/shard_map/ppermute | solution.py:804
  464.2 51.3 %collective-permute-start.34 = (bf16[3,640,128]{2,1,0:T(8,128)(2,1)}, bf16[3,640,128]{2,1,0:T(8,128)(2,1)S(1)}, u32[]{:S(2)}, u32[]{:S(2)}) collective-permute-start(bf16[3,640,128]{2,1,0:T(8,128)(2,1)} %get-tuple-element.177), channel_id=1, source_target_pairs={{0,4},{1,5},{2,6},{3,7},{4,0},{5,1},{6,2},{7,3},{8,12},{9,13},{10,... | collective-permute-start | bytes 1474568 | tf_op jit(solution)/shard_map/ppermute | solution.py:804
  465.5 49.9 %collective-permute-start.35 = (bf16[3,640,128]{2,1,0:T(8,128)(2,1)}, bf16[3,640,128]{2,1,0:T(8,128)(2,1)S(1)}, u32[]{:S(2)}, u32[]{:S(2)}) collective-permute-start(bf16[3,640,128]{2,1,0:T(8,128)(2,1)} %get-tuple-element.178), channel_id=1, source_target_pairs={{0,6},{1,7},{2,4},{3,5},{4,2},{5,3},{6,0},{7,1},{8,14},{9,15},{10,... | collective-permute-start | bytes 1474568 | tf_op jit(solution)/shard_map/ppermute | solution.py:804
  587.4 30.1 %collective-permute-start.49 = (bf16[4,40,2048]{2,1,0:T(8,128)(2,1)}, bf16[4,40,2048]{2,1,0:T(8,128)(2,1)}, u32[]{:S(2)}, u32[]{:S(2)}) collective-permute-start(bf16[4,40,2048]{2,1,0:T(8,128)(2,1)} %get-tuple-element.252), channel_id=1, source_target_pairs={{0,6},{1,7},{2,4},{3,5},{4,2},{5,3},{6,0},{7,1},{8,14},{9,15},{10,... | collective-permute-start | bytes 1966088 | tf_op jit(solution)/shard_map/ppermute | solution.py:804
  591.7 25.9 %collective-permute-start.45 = (bf16[40,5376]{1,0:T(8,128)(2,1)}, bf16[40,5376]{1,0:T(8,128)(2,1)}, u32[]{:S(2)}, u32[]{:S(2)}) collective-permute-start(bf16[40,5376]{1,0:T(8,128)(2,1)} %get-tuple-element.287), channel_id=1, source_target_pairs={{0,1},{1,0},{2,3},{3,2},{4,5},{5,4},{6,7},{7,6},{8,9},{9,8},{10,11... | collective-permute-start | bytes 1290248 | tf_op jit(solution)/shard_map/ppermute | solution.py:804
  (93 other events, 1662.2 us)
Sparse Core Ops, SparseCore 0:
  14.6 149.3 all-gather.2
  167.4 123.3 all-gather.4
  336.9 208.1 reduce-scatter.1
